TPU v7x, 32 devices: a whole 2x2x4 slice. The times are simulated.
32 devices in a mesh: gx: 8 (over z, y), gy: 4 (over x, core).
Axes of the slice: x: 2, y: 2, z: 4, core: 2. Of those that a mesh axis runs over, the one named last changes fastest.
Arguments:
- phase: float32 [128, 128, 256], P('gx', 'gy'), may hold values from -1 to 1
- solute: float32 [128, 128, 256], P('gx', 'gy'), may hold values from -1 to 1
- macro_temp: float32 [32, 32, 64], P('gx', None, 'gy'), may hold values from -1 to 1
Outputs:
- phase_out: float32 [128, 128, 256], P('gx', 'gy')
- solute_out: float32 [128, 128, 256], P('gx', 'gy')
- latent_heat: float32 [32, 32, 64], P('gx', None, 'gy')
All inputs are finite; a program needn't handle non-finite values.
Results may differ from a plain program's by a relative error of at most 0.0001.
Values sent between devices are 32-bit elements; how exact they have to be, the bound alone decides.
No kernel may reach another device: no remote copies, remote signals or barrier semaphores. Data moves between devices by JAX's collectives and lax.ppermute only.
A program may use at most 64 MiB of HBM per device.

v0:
```python
import jax
import jax.numpy as jnp
from jax import lax
from jax.sharding import PartitionSpec as P

SUBSTEPS = 2


time_step = 0.1
anisotropy = 0.3
coupling = 2.0
rejection = 0.5


def padded(cells, sides, width):
    for axis, dim in sides:
        count = lax.axis_size(axis)
        head = lax.slice_in_dim(cells, 0, width, axis=dim)
        tail = lax.slice_in_dim(cells, cells.shape[dim] - width, cells.shape[dim], axis=dim)
        cells = jnp.concatenate(
            [
                lax.ppermute(tail, axis, [(i, (i + 1) % count) for i in range(count)]),
                cells,
                lax.ppermute(head, axis, [((i + 1) % count, i) for i in range(count)]),
            ],
            axis=dim,
        )
    return cells


def divergence(pad_field, with_aniso):
    grid = jnp.pad(pad_field, ((0, 0), (0, 0), (2, 2)), mode="edge")
    grad_x = 0.5 * (grid[2:, 1:-1, 1:-1] - grid[:-2, 1:-1, 1:-1])
    grad_y = 0.5 * (grid[1:-1, 2:, 1:-1] - grid[1:-1, :-2, 1:-1])
    grad_z = 0.5 * (grid[1:-1, 1:-1, 2:] - grid[1:-1, 1:-1, :-2])
    if with_aniso:
        sq_x = grad_x * grad_x
        sq_y = grad_y * grad_y
        planar = sq_x + sq_y + 1.0
        factor = 1.0 + anisotropy * (sq_x * sq_x - 6.0 * sq_x * sq_y + sq_y * sq_y) / (
            planar * planar
        )
        stiff = factor * factor
        grad_x = stiff * grad_x
        grad_y = stiff * grad_y
        grad_z = stiff * grad_z
    total = 0.5 * (grad_x[2:, 1:-1, 1:-1] - grad_x[:-2, 1:-1, 1:-1])
    total = total + 0.5 * (grad_y[1:-1, 2:, 1:-1] - grad_y[1:-1, :-2, 1:-1])
    total = total + 0.5 * (grad_z[1:-1, 1:-1, 2:] - grad_z[1:-1, 1:-1, :-2])
    return total


def substep(phase_pad, solute_pad, theta):
    old = phase_pad[2:-2, 2:-2, :]
    conc = solute_pad[2:-2, 2:-2, :]
    square = 1.0 - old * old
    drive = (
        divergence(phase_pad, True)
        + old
        - old * old * old
        - coupling * square * square * (theta + conc)
    )
    new_phase = old + time_step * drive
    new_solute = conc + time_step * divergence(solute_pad, False) + rejection * (new_phase - old)
    return (new_phase, new_solute)


def table(fine, shift, columns):
    lower = jnp.floor_divide(2 * fine - 3, 8)
    frac = (2 * fine - 3 - 8 * lower).astype(jnp.float32) / 8.0
    first = lower + shift
    second = first + 1
    first = jnp.clip(first, 0, columns - 1)
    second = jnp.clip(second, 0, columns - 1)
    ticks = jnp.arange(columns, dtype=jnp.int32)
    lower_hit = (ticks[None, :] == first[:, None]).astype(jnp.float32)
    upper_hit = (ticks[None, :] == second[:, None]).astype(jnp.float32)
    return (1.0 - frac)[:, None] * lower_hit + frac[:, None] * upper_hit


def body(phase, solute, macro_temp):
    cells_x, cells_y, cells_z = phase.shape
    margin = 0
    fine_x = jnp.arange(cells_x + 2 * margin, dtype=jnp.int32) - margin
    fine_y = jnp.arange(cells_y + 2 * margin, dtype=jnp.int32) - margin
    fine_z = jnp.arange(cells_z, dtype=jnp.int32)
    swapped = lax.all_to_all(macro_temp, "gy", split_axis=1, concat_axis=2, tiled=True)
    framed = padded(swapped, (("gx", 0), ("gy", 1)), 1)
    x_table = table(fine_x, 1, framed.shape[0])
    y_table = table(fine_y, 1, framed.shape[1])
    z_table = table(fine_z, 0, framed.shape[2])
    highest = lax.Precision.HIGHEST
    theta = jnp.einsum("fk,kyz->fyz", x_table, framed, precision=highest)
    theta = jnp.einsum("gk,fkz->fgz", y_table, theta, precision=highest)
    theta = jnp.einsum("hk,fgk->fgh", z_table, theta, precision=highest)
    current_phase, current_solute = (phase, solute)
    for step in range(SUBSTEPS):
        extended = padded(jnp.stack([current_phase, current_solute]), (("gx", 1), ("gy", 2)), 2)
        current_phase, current_solute = substep(extended[0], extended[1], theta)
    change = 0.5 * (current_phase - phase)
    restricted = change.reshape(cells_x // 4, 4, cells_y // 4, 4, cells_z // 4, 4).mean(
        axis=(1, 3, 5)
    )
    latent = lax.all_to_all(restricted, "gy", split_axis=2, concat_axis=1, tiled=True)
    return (current_phase, current_solute, latent)


def solution(mesh):
    in_specs = (P("gx", "gy", None), P("gx", "gy", None), P("gx", None, "gy"))
    out_specs = (P("gx", "gy", None), P("gx", "gy", None), P("gx", None, "gy"))
    return jax.shard_map(body, mesh=mesh, in_specs=in_specs, out_specs=out_specs, check_vma=False)
```

profile of v0, /device:TPU:0, one launch (start us, length us, event | category | flops | bytes accessed | tf_op | source)
XLA Modules:
  0.0 97.7 jit_solution(6574144531123288300)
XLA Ops:
  0.6 0.8 copy.24
  1.5 0.7 reshape.170
  2.2 4.2 %all-to-all-start = ((f32[4,1,512]{2,1,0:T(1,128)}), f32[4,1,512]{2,1,0:T(1,128)S(1)}, u32[]{:S(2)}, u32[]{:S(2)}) async-start(f32[4,1,512]{2,1,0:T(1,128)} %reshape.170), calls=%async_computation | async-start | bytes 16384 | tf_op jit(solution)/shard_map/all_to_all | solution.py:87
  6.4 1.0 %pad_maximum_fusion.17 = (f32[2,2,32,256]{3,2,1,0:T(8,128)S(1)}, f32[2,2,32,256]{3,2,1,0:T(8,128)S(1)}) fusion(f32[1,16,32,256]{3,2,1,0:T(8,128)} %bitcast.49, f32[1,16,32,256]{3,2,1,0:T(8,128)} %bitcast.43), kind=kLoop, calls=%fused_computation.110 | loop fusion | flops 65536 | bytes 1310720 | tf_op jit(solution)/shard_map/slice | solution.py:19
  7.4 2.1 %collective-permute-start = (f32[2,2,32,256]{3,2,1,0:T(8,128)S(1)}, f32[2,2,32,256]{3,2,1,0:T(8,128)S(1)}, u32[]{:S(2)}, u32[]{:S(2)}) collective-permute-start(f32[2,2,32,256]{3,2,1,0:T(8,128)S(1)} %get-tuple-element.46), channel_id=1, source_target_pairs={{0,4},{4,8},{8,12},{12,16},{16,20},{20,24},{24,28},{28,0},{1,5},{5... | collective-permute-start | bytes 393224 | tf_op jit(solution)/shard_map/ppermute | solution.py:22
  9.5 3.1 %collective-permute-start.1 = (f32[2,2,32,256]{3,2,1,0:T(8,128)S(1)}, f32[2,2,32,256]{3,2,1,0:T(8,128)S(1)}, u32[]{:S(2)}, u32[]{:S(2)}) collective-permute-start(f32[2,2,32,256]{3,2,1,0:T(8,128)S(1)} %get-tuple-element.47), channel_id=1, source_target_pairs={{4,0},{8,4},{12,8},{16,12},{20,16},{24,20},{28,24},{0,28},{5,1},{9... | collective-permute-start | bytes 393224 | tf_op jit(solution)/shard_map/ppermute | solution.py:24
  12.7 0.5 broadcast.757
  13.3 0.7 reduce.16
  13.9 0.1 reshape.171
  14.3 4.7 %collective-permute-start.5 = (f32[1,8,64]{2,0,1:T(1,128)S(1)}, f32[1,8,64]{2,0,1:T(1,128)S(1)}, u32[]{:S(2)}, u32[]{:S(2)}) collective-permute-start(f32[1,8,64]{2,0,1:T(1,128)S(1)} %bitcast.60), channel_id=1, source_target_pairs={{4,0},{8,4},{12,8},{16,12},{20,16},{24,20},{28,24},{0,28},{5,1},{9... | collective-permute-start | bytes 6152 | tf_op jit(solution)/shard_map/ppermute | solution.py:24
  19.1 1.3 %collective-permute-done.4 = f32[1,8,64]{2,0,1:T(1,128)S(1)} collective-permute-done((f32[1,8,64]{2,0,1:T(1,128)S(1)}, f32[1,8,64]{2,0,1:T(1,128)S(1)}, u32[]{:S(2)}, u32[]{:S(2)}) %collective-permute-start.4) | collective-permute-done | bytes 2080 | tf_op jit(solution)/shard_map/ppermute | solution.py:22
  20.5 1.7 %collective-permute-start.7 = (f32[6,1,64]{2,0,1:T(8,128)S(1)}, f32[6,1,64]{2,0,1:T(8,128)S(1)}, u32[]{:S(2)}, u32[]{:S(2)}) collective-permute-start(f32[6,1,64]{2,0,1:T(8,128)S(1)} %get-tuple-element.51), channel_id=1, source_target_pairs={{1,0},{2,1},{3,2},{0,3},{5,4},{6,5},{7,6},{4,7},{9,8},{10,9},{11,1... | collective-permute-start | bytes 4616 | tf_op jit(solution)/shard_map/ppermute | solution.py:24
  22.3 1.3 %collective-permute-done.6 = f32[6,1,64]{2,0,1:T(8,128)S(1)} collective-permute-done((f32[6,1,64]{2,0,1:T(8,128)S(1)}, f32[6,1,64]{2,0,1:T(8,128)S(1)}, u32[]{:S(2)}, u32[]{:S(2)}) %collective-permute-start.6) | collective-permute-done | bytes 1568 | tf_op jit(solution)/shard_map/ppermute | solution.py:22
  23.6 0.3 fusion.57
  23.9 0.4 convolution_bitcast_fusion
  24.4 2.1 %collective-permute-start.2 = (f32[2,20,2,256]{3,2,1,0:T(2,128)S(1)}, f32[2,20,2,256]{3,2,1,0:T(2,128)S(1)}, u32[]{:S(2)}, u32[]{:S(2)}) collective-permute-start(f32[2,20,2,256]{3,2,1,0:T(2,128)S(1)} %get-tuple-element.34), channel_id=1, source_target_pairs={{0,1},{1,2},{2,3},{3,0},{4,5},{5,6},{6,7},{7,4},{8,9},{9,10},{10,1... | collective-permute-start | bytes 245768 | tf_op jit(solution)/shard_map/ppermute | solution.py:22
  26.5 0.6 fusion.52
  27.1 1.2 %collective-permute-done.2 = f32[2,20,2,256]{3,2,1,0:T(2,128)S(1)} collective-permute-done((f32[2,20,2,256]{3,2,1,0:T(2,128)S(1)}, f32[2,20,2,256]{3,2,1,0:T(2,128)S(1)}, u32[]{:S(2)}, u32[]{:S(2)}) %collective-permute-start.2) | collective-permute-done | bytes 81952 | tf_op jit(solution)/shard_map/ppermute | solution.py:22
  28.3 0.4 collective-permute-done.3
  28.7 0.2 pad_maximum_fusion
  28.9 0.1 slice_bitcast_fusion.3
  29.0 0.4 slice_reduce_fusion.7
  29.4 0.4 slice_reduce_fusion.4
  29.9 0.2 reshape.152
  30.1 0.2 reshape.151
  30.2 0.4 fusion.10
  30.7 0.2 reshape.149
  30.8 0.2 reshape.150
  31.0 0.9 pad_maximum_fusion.2
  31.9 1.2 %fusion.12 = (f32[18,34,258]{2,1,0:T(8,128)S(1)}, f32[18,34,258]{2,1,0:T(8,128)S(1)}) fusion(f32[20,36,260]{2,1,0:T(8,128)S(1)} %get-tuple-element.65), kind=kLoop, calls=%fused_computation.31 | loop fusion | flops 631584 | bytes 3789504 | tf_op jit(solution)/shard_map/mul | solution.py:33
  33.2 1.3 %fusion.47 = (f32[18,34,258]{2,1,0:T(8,128)S(1)}, f32[18,34,258]{2,1,0:T(8,128)S(1)}) fusion(f32[20,36,260]{2,1,0:T(8,128)S(1)} %get-tuple-element.64), kind=kLoop, calls=%fused_computation.103 | loop fusion | flops 3157920 | bytes 3789504 | tf_op jit(solution)/shard_map/mul | solution.py:44
  34.4 1.1 %fusion.48 = (f32[18,34,258]{2,1,0:T(8,128)S(1)}, f32[18,34,258]{2,1,0:T(8,128)S(1)}) fusion(f32[18,34,258]{2,1,0:T(8,128)S(1)} %get-tuple-element.27, f32[20,36,260]{2,1,0:T(8,128)S(1)} %get-tuple-element.64, f32[20,36,256]{2,1,0:T(8,128)S(1)} %get-tuple-element.30, f32[20,36,2]{2,1,0:T(8,128)S(1)} %reshape.149, f32[20,36,2]{2,1,0:T(8,128)S(1)} %reshape.150), kind=kLoop, calls=%fused_computation.104 | loop fusion | flops 1263168 | bytes 3906720 | tf_op jit(solution)/shard_map/mul | solution.py:45
  35.5 1.7 %fusion.41 = (f32[1,16,32,256]{3,2,1,0:T(8,128)S(1)}, f32[16,32,256]{2,1,0:T(8,128)S(1)}) fusion(f32[18,34,258]{2,1,0:T(8,128)S(1)} %fusion.10, f32[18,34,258]{2,1,0:T(8,128)S(1)} %get-tuple-element.39, f32[18,34,258]{2,1,0:T(8,128)S(1)} %get-tuple-element.38, f32[20,36,256]{2,1,0:T(8,128)S(1)} %get-tuple-element.31, ...), kind=kLoop, calls=%fused_computation.83 | loop fusion | flops 3670016 | bytes 8912896 | tf_op jit(solution)/shard_map/stack | solution.py:98
  37.3 4.9 %collective-permute-start.9 = (f32[2,2,32,256]{3,2,1,0:T(8,128)S(1)}, f32[2,2,32,256]{3,2,1,0:T(8,128)S(1)}, u32[]{:S(2)}, u32[]{:S(2)}) collective-permute-start(f32[2,2,32,256]{3,2,1,0:T(8,128)S(1)} %get-tuple-element.45), channel_id=1, source_target_pairs={{4,0},{8,4},{12,8},{16,12},{20,16},{24,20},{28,24},{0,28},{5,1},{9... | collective-permute-start | bytes 393224 | tf_op jit(solution)/shard_map/ppermute | solution.py:24
  42.2 3.3 %collective-permute-done.8 = f32[2,2,32,256]{3,2,1,0:T(8,128)S(1)} collective-permute-done((f32[2,2,32,256]{3,2,1,0:T(8,128)S(1)}, f32[2,2,32,256]{3,2,1,0:T(8,128)S(1)}, u32[]{:S(2)}, u32[]{:S(2)}) %collective-permute-start.8) | collective-permute-done | bytes 131104 | tf_op jit(solution)/shard_map/ppermute | solution.py:22
  45.6 0.9 collective-permute-start.10
  46.5 1.4 %collective-permute-start.11 = (f32[2,20,2,256]{3,2,1,0:T(2,128)S(1)}, f32[2,20,2,256]{3,2,1,0:T(2,128)S(1)}, u32[]{:S(2)}, u32[]{:S(2)}) collective-permute-start(f32[2,20,2,256]{3,2,1,0:T(2,128)S(1)} %get-tuple-element.33), channel_id=1, source_target_pairs={{1,0},{2,1},{3,2},{0,3},{5,4},{6,5},{7,6},{4,7},{9,8},{10,9},{11,1... | collective-permute-start | bytes 245768 | tf_op jit(solution)/shard_map/ppermute | solution.py:24
  47.9 1.9 %collective-permute-done.10 = f32[2,20,2,256]{3,2,1,0:T(2,128)S(1)} collective-permute-done((f32[2,20,2,256]{3,2,1,0:T(2,128)S(1)}, f32[2,20,2,256]{3,2,1,0:T(2,128)S(1)}, u32[]{:S(2)}, u32[]{:S(2)}) %collective-permute-start.10) | collective-permute-done | bytes 81952 | tf_op jit(solution)/shard_map/ppermute | solution.py:22
  49.8 0.7 collective-permute-done.11
  50.5 0.2 pad_maximum_fusion.1
  50.7 0.1 slice_bitcast_fusion.1
  50.8 0.4 slice_reduce_fusion
  51.3 0.2 reshape.156
  51.5 0.2 reshape.155
  51.6 1.5 %fusion.1 = f32[18,34,258]{2,1,0:T(8,128)} fusion(f32[20,36,256]{2,1,0:T(8,128)S(1)} %get-tuple-element.29, f32[20,36,2]{2,1,0:T(8,128)S(1)} %reshape.155, f32[20,36,2]{2,1,0:T(8,128)S(1)} %reshape.156), kind=kLoop, calls=%fused_computation.9 | loop fusion | flops 631584 | bytes 1380384 | tf_op jit(solution)/shard_map/mul | solution.py:35
  53.1 0.5 pad_maximum_fusion.5
  53.6 0.4 slice_reduce_fusion.3
  54.0 2.2 %fusion.3 = (f32[18,34,258]{2,1,0:T(8,128)S(1)}, f32[18,34,258]{2,1,0:T(8,128)}) fusion(f32[20,36,260]{2,1,0:T(8,128)S(1)} %pad_maximum_fusion.5), kind=kLoop, calls=%fused_computation.14 | loop fusion | flops 631584 | bytes 3789504 | tf_op jit(solution)/shard_map/mul | solution.py:33
  56.2 0.2 reshape.153
  56.4 0.2 reshape.154
  56.6 0.5 pad_maximum_fusion.4
  57.1 1.3 %fusion.49 = (f32[18,34,258]{2,1,0:T(8,128)S(1)}, f32[18,34,258]{2,1,0:T(8,128)S(1)}) fusion(f32[20,36,260]{2,1,0:T(8,128)S(1)} %pad_maximum_fusion.4), kind=kLoop, calls=%fused_computation.105 | loop fusion | flops 3157920 | bytes 3789504 | tf_op jit(solution)/shard_map/mul | solution.py:44
  58.3 1.1 %fusion.50 = (f32[18,34,258]{2,1,0:T(8,128)S(1)}, f32[18,34,258]{2,1,0:T(8,128)S(1)}) fusion(f32[18,34,258]{2,1,0:T(8,128)S(1)} %get-tuple-element.23, f32[20,36,260]{2,1,0:T(8,128)S(1)} %pad_maximum_fusion.4, f32[20,36,256]{2,1,0:T(8,128)S(1)} %get-tuple-element.28, f32[20,36,2]{2,1,0:T(8,128)S(1)} %reshape.153, f32[20,36,2]{2,1,0:T(8,128)S(1)} %reshape.154), kind=kLoop, calls=%fused_computation.106 | loop fusion | flops 1263168 | bytes 3906720 | tf_op jit(solution)/shard_map/mul | solution.py:45
  59.4 1.8 %subtract_multiply_fusion = (f32[16,32,256]{2,1,0:T(8,128)}, f32[16,32,256]{2,1,0:T(8,128)}) fusion(f32[16,32,256]{2,1,0:T(8,128)S(1)} %copy-done, f32[16,32,256]{2,1,0:T(8,128)S(1)} %fusion.52, f32[20,36,256]{2,1,0:T(8,128)S(1)} %get-tuple-element.29, f32[18,34,258]{2,1,0:T(8,128)S(1)} %get-tuple-element.41, f32[18,34,258]{2,1,0:T(8,128)S(1)} %get-tuple-element.40, ...), kind=kLoop, calls=%fused_computation.94 | loop fusion | flops 2621440 | bytes 6291456 | tf_op jit(solution)/shard_map/mul | solution.py:100
  61.3 19.5 %reshape.157 = f32[4,4,8,4,64,4]{5,4,3,2,1,0:T(8,128)} reshape(f32[16,32,256]{2,1,0:T(8,128)} %get-tuple-element.20) | data formatting | bytes 1048576 | tf_op jit(solution)/shard_map/reshape | solution.py:101
  80.7 7.1 %reduce_sum.9 = f32[4,8,64]{2,1,0:T(8,128)S(1)} reduce(f32[4,4,8,4,64,4]{5,4,3,2,1,0:T(8,128)} %reshape.157, f32[]{:T(128)} %constant.93.clone.1), dimensions={1,3,5}, to_apply=%region_0.1 | reduce | flops 129024 | bytes 532484 | tf_op jit(solution)/shard_map/reduce_sum | solution.py:101
  87.8 0.1 copy.33
  88.0 0.8 reshape.172
  88.7 3.5 %all-to-all-start.1 = ((f32[4,1,512]{2,1,0:T(1,128)}), f32[4,1,512]{2,1,0:T(1,128)S(1)}, u32[]{:S(2)}, u32[]{:S(2)}) async-start(f32[4,1,512]{2,1,0:T(1,128)} %reshape.172), calls=%async_computation.1 | async-start | bytes 16384 | tf_op jit(solution)/shard_map/all_to_all | solution.py:104
  92.2 3.5 %fusion.31 = f32[16,32,256]{2,1,0:T(8,128)} fusion(f32[18,34,258]{2,1,0:T(8,128)} %fusion.1, f32[18,34,258]{2,1,0:T(8,128)} %get-tuple-element.37, f32[18,34,258]{2,1,0:T(8,128)S(1)} %get-tuple-element.36, f32[16,32,256]{2,1,0:T(8,128)S(1)} %copy-done.2, f32[20,36,256]{2,1,0:T(8,128)S(1)} %get-tuple-element.29, f32[20,36,256]{2,1,0:T(8,128)S(1)} %get-tuple-element.28), kind=kLoop, calls=%fused_computation.67 | loop fusion | flops 1310720 | bytes 5242880 | tf_op jit(solution)/shard_map/add | solution.py:64
  95.7 0.3 all-to-all-done.1
  96.0 0.7 reduce.17
  96.7 0.2 reshape.173
  97.0 0.7 copy.36
  (36 shorter events, 0.8 us)
Async XLA Ops:
  2.2 10.5 %all-to-all-start = ((f32[4,1,512]{2,1,0:T(1,128)}), f32[4,1,512]{2,1,0:T(1,128)S(1)}, u32[]{:S(2)}, u32[]{:S(2)}) async-start(f32[4,1,512]{2,1,0:T(1,128)} %reshape.170), calls=%async_computation | async-start | bytes 16384 | tf_op jit(solution)/shard_map/all_to_all | solution.py:87
  6.4 17.9 %copy-start = (f32[16,32,256]{2,1,0:T(8,128)S(1)}, f32[16,32,256]{2,1,0:T(8,128)}, u32[]{:S(2)}) copy-start(f32[16,32,256]{2,1,0:T(8,128)} %param.3) | copy-start | bytes 1572868
  6.4 17.9 %copy-start.1 = (f32[16,32,256]{2,1,0:T(8,128)S(1)}, f32[16,32,256]{2,1,0:T(8,128)}, u32[]{:S(2)}) copy-start(f32[16,32,256]{2,1,0:T(8,128)} %param.4) | copy-start | bytes 1572868
  7.4 16.9 %collective-permute-start = (f32[2,2,32,256]{3,2,1,0:T(8,128)S(1)}, f32[2,2,32,256]{3,2,1,0:T(8,128)S(1)}, u32[]{:S(2)}, u32[]{:S(2)}) collective-permute-start(f32[2,2,32,256]{3,2,1,0:T(8,128)S(1)} %get-tuple-element.46), channel_id=1, source_target_pairs={{0,4},{4,8},{8,12},{12,16},{16,20},{20,24},{24,28},{28,0},{1,5},{5... | collective-permute-start | bytes 393224 | tf_op jit(solution)/shard_map/ppermute | solution.py:22
  9.5 14.8 %collective-permute-start.1 = (f32[2,2,32,256]{3,2,1,0:T(8,128)S(1)}, f32[2,2,32,256]{3,2,1,0:T(8,128)S(1)}, u32[]{:S(2)}, u32[]{:S(2)}) collective-permute-start(f32[2,2,32,256]{3,2,1,0:T(8,128)S(1)} %get-tuple-element.47), channel_id=1, source_target_pairs={{4,0},{8,4},{12,8},{16,12},{20,16},{24,20},{28,24},{0,28},{5,1},{9... | collective-permute-start | bytes 393224 | tf_op jit(solution)/shard_map/ppermute | solution.py:24
  14.2 6.3 %collective-permute-start.4 = (f32[1,8,64]{2,0,1:T(1,128)S(1)}, f32[1,8,64]{2,0,1:T(1,128)S(1)}, u32[]{:S(2)}, u32[]{:S(2)}) collective-permute-start(f32[1,8,64]{2,0,1:T(1,128)S(1)} %bitcast.59), channel_id=1, source_target_pairs={{0,4},{4,8},{8,12},{12,16},{16,20},{20,24},{24,28},{28,0},{1,5},{5... | collective-permute-start | bytes 6152 | tf_op jit(solution)/shard_map/ppermute | solution.py:22
  14.3 6.2 %collective-permute-start.5 = (f32[1,8,64]{2,0,1:T(1,128)S(1)}, f32[1,8,64]{2,0,1:T(1,128)S(1)}, u32[]{:S(2)}, u32[]{:S(2)}) collective-permute-start(f32[1,8,64]{2,0,1:T(1,128)S(1)} %bitcast.60), channel_id=1, source_target_pairs={{4,0},{8,4},{12,8},{16,12},{20,16},{24,20},{28,24},{0,28},{5,1},{9... | collective-permute-start | bytes 6152 | tf_op jit(solution)/shard_map/ppermute | solution.py:24
  20.5 3.1 %collective-permute-start.6 = (f32[6,1,64]{2,0,1:T(8,128)S(1)}, f32[6,1,64]{2,0,1:T(8,128)S(1)}, u32[]{:S(2)}, u32[]{:S(2)}) collective-permute-start(f32[6,1,64]{2,0,1:T(8,128)S(1)} %get-tuple-element.50), channel_id=1, source_target_pairs={{0,1},{1,2},{2,3},{3,0},{4,5},{5,6},{6,7},{7,4},{8,9},{9,10},{10,1... | collective-permute-start | bytes 4616 | tf_op jit(solution)/shard_map/ppermute | solution.py:22
  20.5 3.1 %collective-permute-start.7 = (f32[6,1,64]{2,0,1:T(8,128)S(1)}, f32[6,1,64]{2,0,1:T(8,128)S(1)}, u32[]{:S(2)}, u32[]{:S(2)}) collective-permute-start(f32[6,1,64]{2,0,1:T(8,128)S(1)} %get-tuple-element.51), channel_id=1, source_target_pairs={{1,0},{2,1},{3,2},{0,3},{5,4},{6,5},{7,6},{4,7},{9,8},{10,9},{11,1... | collective-permute-start | bytes 4616 | tf_op jit(solution)/shard_map/ppermute | solution.py:24
  24.4 3.9 %collective-permute-start.2 = (f32[2,20,2,256]{3,2,1,0:T(2,128)S(1)}, f32[2,20,2,256]{3,2,1,0:T(2,128)S(1)}, u32[]{:S(2)}, u32[]{:S(2)}) collective-permute-start(f32[2,20,2,256]{3,2,1,0:T(2,128)S(1)} %get-tuple-element.34), channel_id=1, source_target_pairs={{0,1},{1,2},{2,3},{3,0},{4,5},{5,6},{6,7},{7,4},{8,9},{9,10},{10,1... | collective-permute-start | bytes 245768 | tf_op jit(solution)/shard_map/ppermute | solution.py:22
  26.5 2.2 %collective-permute-start.3 = (f32[2,20,2,256]{3,2,1,0:T(2,128)S(1)}, f32[2,20,2,256]{3,2,1,0:T(2,128)S(1)}, u32[]{:S(2)}, u32[]{:S(2)}) collective-permute-start(f32[2,20,2,256]{3,2,1,0:T(2,128)S(1)} %get-tuple-element.35), channel_id=1, source_target_pairs={{1,0},{2,1},{3,2},{0,3},{5,4},{6,5},{7,6},{4,7},{9,8},{10,9},{11,1... | collective-permute-start | bytes 245768 | tf_op jit(solution)/shard_map/ppermute | solution.py:24
  37.3 8.2 %collective-permute-start.8 = (f32[2,2,32,256]{3,2,1,0:T(8,128)S(1)}, f32[2,2,32,256]{3,2,1,0:T(8,128)S(1)}, u32[]{:S(2)}, u32[]{:S(2)}) collective-permute-start(f32[2,2,32,256]{3,2,1,0:T(8,128)S(1)} %get-tuple-element.44), channel_id=1, source_target_pairs={{0,4},{4,8},{8,12},{12,16},{16,20},{20,24},{24,28},{28,0},{1,5},{5... | collective-permute-start | bytes 393224 | tf_op jit(solution)/shard_map/ppermute | solution.py:22
  37.3 8.2 %collective-permute-start.9 = (f32[2,2,32,256]{3,2,1,0:T(8,128)S(1)}, f32[2,2,32,256]{3,2,1,0:T(8,128)S(1)}, u32[]{:S(2)}, u32[]{:S(2)}) collective-permute-start(f32[2,2,32,256]{3,2,1,0:T(8,128)S(1)} %get-tuple-element.45), channel_id=1, source_target_pairs={{4,0},{8,4},{12,8},{16,12},{20,16},{24,20},{28,24},{0,28},{5,1},{9... | collective-permute-start | bytes 393224 | tf_op jit(solution)/shard_map/ppermute | solution.py:24
  45.6 4.2 %collective-permute-start.10 = (f32[2,20,2,256]{3,2,1,0:T(2,128)S(1)}, f32[2,20,2,256]{3,2,1,0:T(2,128)S(1)}, u32[]{:S(2)}, u32[]{:S(2)}) collective-permute-start(f32[2,20,2,256]{3,2,1,0:T(2,128)S(1)} %get-tuple-element.32), channel_id=1, source_target_pairs={{0,1},{1,2},{2,3},{3,0},{4,5},{5,6},{6,7},{7,4},{8,9},{9,10},{10,1... | collective-permute-start | bytes 245768 | tf_op jit(solution)/shard_map/ppermute | solution.py:22
  46.5 4.0 %collective-permute-start.11 = (f32[2,20,2,256]{3,2,1,0:T(2,128)S(1)}, f32[2,20,2,256]{3,2,1,0:T(2,128)S(1)}, u32[]{:S(2)}, u32[]{:S(2)}) collective-permute-start(f32[2,20,2,256]{3,2,1,0:T(2,128)S(1)} %get-tuple-element.33), channel_id=1, source_target_pairs={{1,0},{2,1},{3,2},{0,3},{5,4},{6,5},{7,6},{4,7},{9,8},{10,9},{11,1... | collective-permute-start | bytes 245768 | tf_op jit(solution)/shard_map/ppermute | solution.py:24
  80.7 11.5 %copy-start.2 = (f32[16,32,256]{2,1,0:T(8,128)S(1)}, f32[16,32,256]{2,1,0:T(8,128)}, u32[]{:S(2)}) copy-start(f32[16,32,256]{2,1,0:T(8,128)} %get-tuple-element.21) | copy-start | bytes 1572868
  88.7 7.3 %all-to-all-start.1 = ((f32[4,1,512]{2,1,0:T(1,128)}), f32[4,1,512]{2,1,0:T(1,128)S(1)}, u32[]{:S(2)}, u32[]{:S(2)}) async-start(f32[4,1,512]{2,1,0:T(1,128)} %reshape.172), calls=%async_computation.1 | async-start | bytes 16384 | tf_op jit(solution)/shard_map/all_to_all | solution.py:104
where the time goes:
time: 98.8 us; the launch traced here: 97.7 us
  other arithmetic  29.2 us (30%)
  starting transfers between devices  28.7 us (29%)
  local copies, waits for them, and re-layouts  27 us (27%)
  waiting for transfers between devices  10.5 us (11%)
  matrix products  1.25 us (1%)
  between operations  1.01 us (1%)
    reshape x1, local copies, waits for them, and re-layouts, body(): change.reshape(cells_x // 4, 4, cells_y // 4, 4, cells_z // 4, 4)  19.5 us
    ppermute x6, starting transfers between devices, padded(): lax.ppermute(head, axis, [((i + 1) % count, i) for i in range(count)])  15.8 us
    ppermute x6, waiting for transfers between devices, padded(): lax.ppermute(tail, axis, [(i, (i + 1) % count) for i in range(count)])  9.05 us
    reduce_sum x1, other arithmetic, body(): change.reshape(cells_x // 4, 4, cells_y // 4, 4, cells_z // 4, 4)  7.1 us
    ppermute x6, starting transfers between devices, padded(): lax.ppermute(tail, axis, [(i, (i + 1) % count) for i in range(count)])  5.23 us
    all_to_all x1, starting transfers between devices, body(): lax.all_to_all(macro_temp, 'gy', split_axis=1, concat_axis=2, tiled=True)  4.21 us
    add x1, other arithmetic, substep(): conc + time_step * divergence(solute_pad, False)  3.49 us
    all_to_all x1, starting transfers between devices, body(): lax.all_to_all(restricted, 'gy', split_axis=2, concat_axis=1, tiled=True)  3.49 us
  transfers between devices with their start and end apart: 14, of which 8 were waited for; matrix products, arithmetic and copies ran while one was open for 8% of the time, Pallas kernels for 0%

commit v1 on v0

v1 whole, which is shorter than its diff:
```python
import functools

import jax
import jax.numpy as jnp
from jax import lax
from jax.experimental import pallas as pl
from jax.experimental.pallas import tpu as pltpu
from jax.sharding import PartitionSpec as P

time_step = 0.1
anisotropy = 0.3
coupling = 2.0
rejection = 0.5

F32 = jnp.float32
HIGHEST = lax.Precision.HIGHEST
HALO = 4
ROWS = 8
LANES = 128
VMEM_LIMIT = 40 * 1024 * 1024


def vmem():
    return pl.BlockSpec(memory_space=pltpu.VMEM)


def hbm():
    return pl.BlockSpec(memory_space=pl.ANY)


def pairs(count, first):
    forward = [((first + k) % count, (first + k + 1) % count) for k in range(0, count, 2)]
    return forward + [(b, a) for a, b in forward]


def flips(me):
    odd = lax.rem(me, 2)
    return me, me + 1 - 2 * odd, lax.rem(me + 2, 4), 3 - me


def row_ids(shape):
    return lax.broadcasted_iota(jnp.int32, shape, len(shape) - 2)


def lane_ids(shape):
    return lax.broadcasted_iota(jnp.int32, shape, len(shape) - 1)


def pack_kernel(phase, solute, macro, face_a, face_b, side_a, side_b, table, low, high, sems):
    size_x, size_y, _ = phase.shape
    odd_x = lax.rem(lax.axis_index("gx"), 2)
    odd_y = lax.rem(lax.axis_index("gy"), 2)
    start_a = (1 - odd_x) * (size_x - HALO)
    start_b = odd_x * (size_x - HALO)
    copies = []
    for field, ref in enumerate((phase, solute)):
        copies.append((ref.at[:, pl.ds(0, ROWS), :], low.at[field]))
        copies.append((ref.at[:, pl.ds(size_y - ROWS, ROWS), :], high.at[field]))
        copies.append((ref.at[pl.ds(start_a, HALO)], face_a.at[field]))
        copies.append((ref.at[pl.ds(start_b, HALO)], face_b.at[field]))
    copies = [pltpu.make_async_copy(s, d, sems.at[n]) for n, (s, d) in enumerate(copies)]
    for copy in copies:
        copy.start()
    coarse_x, coarse_y, coarse_z = macro.shape
    wide = jnp.concatenate([macro[k] for k in range(coarse_x)], axis=1)
    wide = jnp.pad(wide, ((0, 0), (0, LANES - coarse_x * coarse_z)))
    table[...] = wide.reshape(table.shape)
    for copy in copies:
        copy.wait()
    shape = (size_x, ROWS, phase.shape[2])
    top = row_ids(shape) < HALO
    low_side = jnp.where(top, low[0], pltpu.roll(low[1], HALO, 1))
    high_side = jnp.where(top, pltpu.roll(high[1], HALO, 1), high[0])
    even = odd_y == 0
    side_a[...] = jnp.where(even, high_side, low_side)
    side_b[...] = jnp.where(even, low_side, high_side)


def pack(phase, solute, macro):
    size_x, size_y, size_z = phase.shape
    coarse_x, coarse_y, coarse_z = macro.shape
    face = jax.ShapeDtypeStruct((2, HALO, size_y, size_z), F32)
    side = jax.ShapeDtypeStruct((size_x, ROWS, size_z), F32)
    table = jax.ShapeDtypeStruct((coarse_y // ROWS, ROWS, LANES), F32)
    return pl.pallas_call(
        pack_kernel,
        out_shape=(face, face, side, side, table),
        in_specs=[hbm(), hbm(), vmem()],
        out_specs=[vmem()] * 5,
        scratch_shapes=[
            pltpu.VMEM((2, size_x, ROWS, size_z), F32),
            pltpu.VMEM((2, size_x, ROWS, size_z), F32),
            pltpu.SemaphoreType.DMA((8,)),
        ],
        compiler_params=pltpu.CompilerParams(vmem_limit_bytes=VMEM_LIMIT),
        cost_estimate=pl.CostEstimate(flops=10**5, bytes_accessed=2 * 10**6, transcendentals=0),
        name="pack",
    )(phase, solute, macro)


def corner_kernel(count, coarse_x, coarse_z, side_a, side_b, *rest):
    tables, (corner_a, corner_b, coarse) = rest[:count], rest[count:]
    size_x = side_a.shape[0]
    me = lax.axis_index("gy")
    even_x = lax.rem(lax.axis_index("gx"), 2) == 0
    even_y = lax.rem(me, 2) == 0
    groups = tables[0].shape[0]
    ranks = lax.axis_size("gy")
    if count == 4:
        owners = flips(me)
        pick = lambda s, g: tables[s][g]
    else:
        owners = tuple(range(ranks))
        groups = tables[0].shape[1]
        pick = lambda s, g: tables[0][s, g]
    lane = lane_ids((ROWS, LANES))
    parts = []
    for k in range(coarse_x):
        for g in range(3):
            group = lax.rem(me + g - 1 + groups, groups)
            total = jnp.zeros((ROWS, LANES), F32)
            for s, owner in enumerate(owners):
                at = owner * coarse_z
                shift = lax.rem(at - k * coarse_z + LANES, LANES)
                moved = pltpu.roll(pick(s, group), shift, 1)
                total = total + jnp.where((lane >= at) & (lane < at + coarse_z), moved, 0.0)
            coarse[k, pl.ds(g * ROWS, ROWS), :] = total
            parts.append(total)
    for corner, top_side in ((corner_a, even_x), (corner_b, jnp.logical_not(even_x))):
        layer = lambda ref, d: ref[jnp.where(top_side, size_x - d, d - 1)]
        row = row_ids(side_a.shape[1:])
        for n, keep in ((0, 5), (1, 2)):
            def one(d, n=n):
                first, second = layer(side_a, d), layer(side_b, d)
                return jnp.where(even_y, second, first) if n == 0 else jnp.where(even_y, first, second)

            third = pltpu.roll(one(3), 6 if n == 0 else 2, 0)
            corner[2 * n] = one(1)
            corner[2 * n + 1] = jnp.where(row == keep, third, one(2))
        edge = [jnp.where(top_side, parts[3 * (coarse_x - 1) + g], parts[g]) for g in range(3)]
        corner[4] = jnp.concatenate([edge[0] + pltpu.roll(edge[1], LANES // 2, 1), edge[2]], axis=1)


def corners(side_a, side_b, tables, coarse_x, coarse_z):
    size_x, _, size_z = side_a.shape
    corner = jax.ShapeDtypeStruct((5, ROWS, size_z), F32)
    coarse = jax.ShapeDtypeStruct((coarse_x, 3 * ROWS, LANES), F32)
    return pl.pallas_call(
        functools.partial(corner_kernel, len(tables), coarse_x, coarse_z),
        out_shape=(corner, corner, coarse),
        in_specs=[vmem()] * (2 + len(tables)),
        out_specs=[vmem()] * 3,
        compiler_params=pltpu.CompilerParams(vmem_limit_bytes=VMEM_LIMIT),
        cost_estimate=pl.CostEstimate(flops=10**5, bytes_accessed=4 * 10**5, transcendentals=0),
        name="corners",
    )(side_a, side_b, *tables)


def interpolation(fine, count, offset):
    lower = (2 * fine - 3 + 8 * 8) // 8 - 8
    frac = (2 * fine - 3 - 8 * lower).astype(F32) / 8.0
    tick = lane_ids(fine.shape)
    first = jnp.clip(lower + offset, 0, count - 1)
    second = jnp.clip(lower + 1 + offset, 0, count - 1)
    return jnp.where(tick == first, 1.0 - frac, 0.0) + jnp.where(tick == second, frac, 0.0)


def step_kernel(
    phase, solute, face_a, face_b, side_a, side_b, corner_a, corner_b, coarse,
    phase_out, solute_out, latent,
    p0, c0, p1, c1, gx, div, theta, weights, fan, sems,
):
    size_x, size_y, size_z = phase.shape
    coarse_x = coarse.shape[0]
    rows = size_y + 2 * HALO
    even_x = lax.rem(lax.axis_index("gx"), 2) == 0
    even_y = lax.rem(lax.axis_index("gy"), 2) == 0
    spot_a = jnp.where(even_x, size_x + HALO, 0)
    spot_b = jnp.where(even_x, 0, size_x + HALO)
    copies = []
    for n, (source, face) in enumerate(((phase, 0), (solute, 1))):
        field = (p0, c0)[n]
        own = field.at[pl.ds(HALO, size_x), pl.ds(0, size_y), :]
        copies.append((source, own))
        copies.append((face_a.at[face], field.at[pl.ds(spot_a, HALO), pl.ds(0, size_y), :]))
        copies.append((face_b.at[face], field.at[pl.ds(spot_b, HALO), pl.ds(0, size_y), :]))
    copies = [pltpu.make_async_copy(s, d, sems.at[n]) for n, (s, d) in enumerate(copies)]
    for copy in copies:
        copy.start()

    row = row_ids((ROWS, size_z))
    top = row < HALO

    def put(at, low, high):
        p0[at, pl.ds(size_y, ROWS), :] = jnp.where(top, high, low)
        c0[at, pl.ds(size_y, ROWS), :] = pltpu.roll(jnp.where(top, low, high), HALO, 0)

    for k in range(size_x):
        first, second = side_a[k], side_b[k]
        put(k + HALO, jnp.where(even_y, second, first), jnp.where(even_y, first, second))
    for above in (False, True):
        use_a = even_x if above else jnp.logical_not(even_x)
        tile = [jnp.where(use_a, corner_a[k], corner_b[k]) for k in range(5)]
        place = lambda d: size_x + HALO - 1 + d if above else HALO - d
        put(place(1), tile[0], tile[2])
        put(place(2), tile[1], tile[3])
        put(place(3), pltpu.roll(tile[1], 2, 0), pltpu.roll(tile[3], 6, 0))
        put(place(4), jnp.zeros_like(tile[0]), jnp.zeros_like(tile[0]))
        edge = coarse_x + 1 if above else 0
        weights[edge, pl.ds(0, ROWS), :] = tile[4][:, :LANES]
        weights[edge, pl.ds(ROWS, ROWS), :] = pltpu.roll(tile[4][:, :LANES], LANES // 2, 1)
        weights[edge, pl.ds(2 * ROWS, ROWS), :] = tile[4][:, LANES:]
    weights[pl.ds(1, coarse_x)] = coarse[...]

    half = LANES // 2
    fine_z = lax.broadcasted_iota(jnp.int32, (size_z, half), 0)
    along_z = interpolation(fine_z, size_z // 4, 0)
    fine_y = lax.broadcasted_iota(jnp.int32, (rows, 3 * ROWS), 0)
    fine_y = jnp.where(fine_y >= size_y + HALO, fine_y - rows, fine_y)
    along_y = interpolation(fine_y, 3 * ROWS, ROWS)
    block = weights[...].reshape((coarse_x + 2) * 3 * ROWS, LANES)[:, :half]
    deep = lax.dot_general(block, along_z, (((1,), (1,)), ((), ())), precision=HIGHEST, preferred_element_type=F32)
    for k in range(coarse_x + 2):
        fan[k] = lax.dot_general(
            along_y, deep[k * 3 * ROWS : (k + 1) * 3 * ROWS], (((1,), (0,)), ((), ())), precision=HIGHEST,
            preferred_element_type=F32,
        )
    for x in range(-2, size_x + 2):
        lower = (2 * x - 3) // 8
        frac = (2 * x - 3 - 8 * lower) / 8.0
        theta[x + 2] = (1.0 - frac) * fan[lower + 1] + frac * fan[lower + 2]

    for copy in copies:
        copy.wait()

    lane = lane_ids((rows, size_z))

    def turn(value, by, axis):
        return pltpu.roll(value, by % value.shape[axis], axis)

    def stiff_flux(old, shift, at):
        here = old[at + shift]
        along_x = old[at + shift + 1] - old[at + shift - 1]
        along_y = turn(here, -1, 0) - turn(here, 1, 0)
        after = jnp.where(lane == size_z - 1, here, turn(here, -1, 1))
        before = jnp.where(lane == 0, here, turn(here, 1, 1))
        along_z = after - before
        sq_x = along_x * along_x
        sq_y = along_y * along_y
        both = sq_x + sq_y
        inverse = 1.0 / (both + 4.0)
        factor = 1.0 + anisotropy * (both * both - 8.0 * (sq_x * sq_y)) * (inverse * inverse)
        stiff = (0.25 * time_step) * (factor * factor)
        return stiff * along_x, stiff * along_y, stiff * along_z

    def flux_step(old, shift, first, last):
        def run(n, _):
            flux_x, flux_y, flux_z = stiff_flux(old, shift + first, n)
            gx[n] = flux_x
            after = jnp.where(lane == size_z - 1, 0.0, turn(flux_z, -1, 1))
            before = jnp.where(lane == 0, 0.0, turn(flux_z, 1, 1))
            div[n] = (turn(flux_y, -1, 0) - turn(flux_y, 1, 0)) + (after - before)
            return 0

        lax.fori_loop(0, last - first, run, 0)

    def update(old, conc, n, drop):
        here = old[n + 2]
        centre = conc[n + 2]
        total = (gx[n + 2] - gx[n]) + div[n + 1]
        square = 1.0 - here * here
        drive = square * (here - (coupling * square) * (theta[n + drop] + centre))
        delta = total + time_step * drive
        laplace = conc[n + 4] + conc[n] + turn(centre, -2, 0) + turn(centre, 2, 0)
        ahead = jnp.where(lane >= size_z - 2, jnp.broadcast_to(centre[:, size_z - 1 :], centre.shape), turn(centre, -2, 1))
        behind = jnp.where(lane < 2, jnp.broadcast_to(centre[:, :1], centre.shape), turn(centre, 2, 1))
        laplace = laplace + ahead + behind - 6.0 * centre
        new_conc = centre + (0.25 * time_step) * laplace + rejection * delta
        return here + delta, new_conc

    flux_step(p0, HALO, -3, size_x + 3)

    def first_update(n, _):
        p1[n], c1[n] = update(p0, c0, n, 0)
        return 0

    lax.fori_loop(0, size_x + 4, first_update, 0)
    flux_step(p1, 2, -1, size_x + 1)

    def second_update(x, _):
        new_phase, new_conc = update(p1, c1, x, 2)
        phase_out[x] = new_phase[:size_y]
        solute_out[x] = new_conc[:size_y]
        return 0

    lax.fori_loop(0, size_x, second_update, 0)

    per = size_y // 4
    pool_y = (row_ids((per, size_y)) == lane_ids((per, size_y)) // 4).astype(F32)
    pool_z = (row_ids((size_z, LANES)) // 4 == lane_ids((size_z, LANES))).astype(F32)
    for k in range(coarse_x):
        change = jnp.zeros((size_y, size_z), F32)
        for x in range(4 * k, 4 * k + 4):
            change = change + (phase_out[x] - p0[x + HALO, pl.ds(0, size_y), :])
        change = jnp.dot(change, pool_z, precision=HIGHEST, preferred_element_type=F32)
        latent[k] = (0.5 / 64.0) * jnp.dot(pool_y, change, precision=HIGHEST, preferred_element_type=F32)


def steps(phase, solute, face_a, face_b, side_a, side_b, corner_a, corner_b, coarse):
    size_x, size_y, size_z = phase.shape
    coarse_x = coarse.shape[0]
    rows = size_y + 2 * HALO
    out = jax.ShapeDtypeStruct(phase.shape, F32)
    slabs = lambda count: pltpu.VMEM((count, rows, size_z), F32)
    return pl.pallas_call(
        step_kernel,
        out_shape=(out, out, jax.ShapeDtypeStruct((coarse_x, size_y // 4, LANES), F32)),
        in_specs=[hbm(), hbm()] + [vmem()] * 7,
        out_specs=[vmem()] * 3,
        scratch_shapes=[
            slabs(size_x + 8), slabs(size_x + 8), slabs(size_x + 4), slabs(size_x + 4),
            slabs(size_x + 6), slabs(size_x + 6), slabs(size_x + 4),
            pltpu.VMEM((coarse_x + 2, 3 * ROWS, LANES), F32),
            slabs(coarse_x + 2),
            pltpu.SemaphoreType.DMA((6,)),
        ],
        compiler_params=pltpu.CompilerParams(vmem_limit_bytes=VMEM_LIMIT),
        cost_estimate=pl.CostEstimate(flops=4 * 10**7, bytes_accessed=3 * 10**6, transcendentals=0),
        name="substeps",
    )(phase, solute, face_a, face_b, side_a, side_b, corner_a, corner_b, coarse)


def owner_kernel(coarse_z, mine, core, chip, far, out):
    me = lax.axis_index("gy")
    per = mine.shape[1]
    for source, ref in zip(flips(me), (mine, core, chip, far)):
        for k in range(mine.shape[0]):
            moved = pltpu.roll(ref[k], lax.rem(LANES - me * coarse_z, LANES), 1)
            out[k, pl.ds(pl.multiple_of(source * per, per), per), :] = moved[:, :coarse_z]


def owner(parts, coarse_y, coarse_z):
    coarse_x = parts[0].shape[0]
    return pl.pallas_call(
        functools.partial(owner_kernel, coarse_z),
        out_shape=jax.ShapeDtypeStruct((coarse_x, coarse_y, coarse_z), F32),
        in_specs=[vmem()] * 4,
        out_specs=vmem(),
        name="owner",
    )(*parts)


def body(phase, solute, macro_temp):
    count_x, count_y = lax.axis_size("gx"), lax.axis_size("gy")
    coarse_x, coarse_y, coarse_z = macro_temp.shape
    swap = lambda value, axis, table: lax.ppermute(value, axis, table)
    near_x, far_x = pairs(count_x, 0), pairs(count_x, 1)
    near_y, far_y = pairs(count_y, 0), pairs(count_y, 1)
    across = [(k, k ^ 2) for k in range(count_y)]
    face_a, face_b, side_a, side_b, table = pack(phase, solute, macro_temp)
    face_a = swap(face_a, "gx", near_x)
    face_b = swap(face_b, "gx", far_x)
    side_a = swap(side_a, "gy", near_y)
    side_b = swap(side_b, "gy", far_y)
    if count_y == 4:
        opposite = swap(table, "gy", across)
        core = swap(table, "gy", near_y)
        tables = (table, core, opposite, swap(opposite, "gy", near_y))
    else:
        tables = (lax.all_gather(table, "gy"),)
    corner_a, corner_b, coarse = corners(side_a, side_b, tables, coarse_x, coarse_z)
    corner_a = swap(corner_a, "gx", near_x)
    corner_b = swap(corner_b, "gx", far_x)
    phase_out, solute_out, latent = steps(
        phase, solute, face_a, face_b, side_a, side_b, corner_a, corner_b, coarse
    )
    if count_y == 4:
        opposite = swap(latent, "gy", across)
        core = swap(latent, "gy", near_y)
        latent = owner((latent, core, opposite, swap(opposite, "gy", near_y)), coarse_y, coarse_z)
    else:
        split = latent[:, :, : coarse_z * count_y].reshape(coarse_x, latent.shape[1], count_y, coarse_z)
        latent = lax.all_to_all(split, "gy", split_axis=2, concat_axis=1, tiled=True)
        latent = latent.reshape(coarse_x, coarse_y, coarse_z)
    return phase_out, solute_out, latent


def solution(mesh):
    in_specs = (P("gx", "gy", None), P("gx", "gy", None), P("gx", None, "gy"))
    out_specs = (P("gx", "gy", None), P("gx", "gy", None), P("gx", None, "gy"))
    return jax.shard_map(body, mesh=mesh, in_specs=in_specs, out_specs=out_specs, check_vma=False)
```

time: 98.8 us -> 48.9 us (0.49)
  other arithmetic: 29.2 us -> 0 us
  local copies, waits for them, and re-layouts: 27 us -> 5.06 us
  starting transfers between devices: 28.7 us -> 12.4 us
  Pallas kernels: 0 us -> 15.9 us
  waiting for transfers between devices: 10.5 us -> 14.5 us
  matrix products: 1.25 us -> 0 us
    reshape x9 -> x0, local copies, waits for them, and re-layouts: 20.7 us -> none  [the longest x1 19.5 us: body(): change.reshape(cells_x // 4, 4, cells_y // 4, 4, cells_z // 4, 4)]
    pallas_call x0 -> x4, Pallas kernels: none -> 15.9 us  [the longest x1 13.3 us: steps(): pl.pallas_call(step_kernel, out_shape=(out, out, jax.ShapeDtypeStruct((co...]
    mul x9 -> x0, other arithmetic: 11.9 us -> none  [the longest x2 3.45 us: divergence(): grad_x = 0.5 * (grid[2:, 1:-1, 1:-1] - grid[:-2, 1:-1, 1:-1])]
    ppermute x12, starting transfers between devices: 21.1 us -> 12.4 us  [body(): swap = lambda value, axis, table: lax.ppermute(value, axis, table)]
    all_to_all x2 -> x0, starting transfers between devices: 7.69 us -> none  [the longest x1 4.21 us: body(): lax.all_to_all(macro_temp, 'gy', split_axis=1, concat_axis=2, tiled=True)]
    reduce_sum x1 -> x0, other arithmetic: 7.1 us -> none  [body(): change.reshape(cells_x // 4, 4, cells_y // 4, 4, cells_z // 4, 4)]
    ppermute x12, waiting for transfers between devices: 10.2 us -> 14.5 us  [body(): swap = lambda value, axis, table: lax.ppermute(value, axis, table)]
    add x1 -> x0, other arithmetic: 3.49 us -> none  [substep(): conc + time_step * divergence(solute_pad, False)]
  transfers between devices with their start and end apart: 14 -> 12, of which waited for: 8 -> 7; matrix products, arithmetic and copies ran while one was open for 8% -> 0% of each run, Pallas kernels for 0% -> 0%
where the time goes in v1:
time: 48.9 us; the launch traced here: 48.5 us
  Pallas kernels  15.9 us (33%)
  waiting for transfers between devices  14.5 us (30%)
  starting transfers between devices  12.4 us (25%)
  local copies, waits for them, and re-layouts  5.06 us (10%)
  between operations  0.71 us (1%)
    ppermute x12, waiting for transfers between devices, body(): swap = lambda value, axis, table: lax.ppermute(value, axis, table)  14.5 us
    pallas_call x1, Pallas kernels, steps(): pl.pallas_call(step_kernel, out_shape=(out, out, jax.ShapeDtypeStruct((co...  13.3 us
    ppermute x12, starting transfers between devices, body(): swap = lambda value, axis, table: lax.ppermute(value, axis, table)  12.4 us
    unnamed x16, local copies, waits for them, and re-layouts  5.06 us
    pallas_call x1, Pallas kernels, owner(): pl.pallas_call(functools.partial(owner_kernel, coarse_z), out_shape=jax.S...  1.48 us
  transfers between devices with their start and end apart: 12, of which 7 were waited for; matrix products, arithmetic and copies ran while one was open for 0% of the time, Pallas kernels for 0%

profile of v1, /device:TPU:0, one launch (start us, length us, event | category | flops | bytes accessed | tf_op | source)
XLA Modules:
  0.0 48.5 jit_solution(3231831870438934769)
XLA Ops:
  0.6 0.8 %copy.6.macro = f32[4,32,16]{2,1,0:T(8,128)S(1)} copy(f32[4,32,16]{1,2,0:T(8,128)} %param.5) | data formatting | bytes 16384 | tf_op args[2]
  1.5 0.0 copy-start
  1.5 1.0 %copy-done = f32[16,32,256]{2,1,0:T(8,128)S(1)} copy-done((f32[16,32,256]{2,1,0:T(8,128)S(1)}, f32[16,32,256]{2,1,0:T(8,128)}, u32[]{:S(2)}) %copy-start) | copy-done | bytes 524312
  2.5 0.0 copy-start.2
  2.5 1.0 %copy-done.2 = f32[16,32,256]{2,1,0:T(8,128)S(1)} copy-done((f32[16,32,256]{2,1,0:T(8,128)S(1)}, f32[16,32,256]{2,1,0:T(8,128)}, u32[]{:S(2)}) %copy-start.2) | copy-done | bytes 524312
  3.6 0.0 copy-start.1
  3.6 1.0 %pack.1 = (f32[2,4,32,256]{3,2,1,0:T(8,128)S(1)}, f32[2,4,32,256]{3,2,1,0:T(8,128)S(1)}, f32[16,8,256]{2,1,0:T(8,128)S(1)}, f32[16,8,256]{2,1,0:T(8,128)S(1)}, f32[4,8,128]{2,1,0:T(8,128)S(1)}) custom-call(f32[16,32,256]{2,1,0:T(8,128)S(1)} %copy-done, f32[16,32,256]{2,1,0:T(8,128)S(1)} %copy-done.2, f32[4,32,16]{2,1,0:T(8,128)S(1)} %copy.6.macro), custom_call_target="tpu_custom_call" | custom-call | flops 100000 | bytes 2000000 | tf_op jit(solution)/shard_map/pack/pallas_call | solution.py:85
  4.5 3.0 %collective-permute-start = (f32[2,4,32,256]{3,2,1,0:T(8,128)S(1)}, f32[2,4,32,256]{3,2,1,0:T(8,128)S(1)}, u32[]{:S(2)}, u32[]{:S(2)}) collective-permute-start(f32[2,4,32,256]{3,2,1,0:T(8,128)S(1)} %get-tuple-element.14), channel_id=1, source_target_pairs={{0,4},{8,12},{16,20},{24,28},{4,0},{12,8},{20,16},{28,24},{1,5},{9... | collective-permute-start | bytes 786440 | tf_op jit(solution)/shard_map/ppermute | solution.py:356
  7.6 3.5 %collective-permute-start.1 = (f32[2,4,32,256]{3,2,1,0:T(8,128)S(1)}, f32[2,4,32,256]{3,2,1,0:T(8,128)S(1)}, u32[]{:S(2)}, u32[]{:S(2)}) collective-permute-start(f32[2,4,32,256]{3,2,1,0:T(8,128)S(1)} %get-tuple-element.15), channel_id=1, source_target_pairs={{4,8},{12,16},{20,24},{28,0},{8,4},{16,12},{24,20},{0,28},{5,9},{1... | collective-permute-start | bytes 786440 | tf_op jit(solution)/shard_map/ppermute | solution.py:356
  11.1 0.0 collective-permute-start.2
  11.1 1.6 %collective-permute-start.3 = (f32[16,8,256]{2,1,0:T(8,128)S(1)}, f32[16,8,256]{2,1,0:T(8,128)S(1)}, u32[]{:S(2)}, u32[]{:S(2)}) collective-permute-start(f32[16,8,256]{2,1,0:T(8,128)S(1)} %get-tuple-element.17), channel_id=1, source_target_pairs={{1,2},{3,0},{2,1},{0,3},{5,6},{7,4},{6,5},{4,7},{9,10},{11,8},{10,... | collective-permute-start | bytes 393224 | tf_op jit(solution)/shard_map/ppermute | solution.py:356
  12.7 0.5 %collective-permute-start.5 = (f32[4,8,128]{2,1,0:T(8,128)S(1)}, f32[4,8,128]{2,1,0:T(8,128)S(1)}, u32[]{:S(2)}, u32[]{:S(2)}) collective-permute-start(f32[4,8,128]{2,1,0:T(8,128)S(1)} %get-tuple-element.18.rest_0_), channel_id=1, source_target_pairs={{0,2},{1,3},{2,0},{3,1},{4,6},{5,7},{6,4},{7,5},{8,10},{9,11},{10,... | collective-permute-start | bytes 49160 | tf_op jit(solution)/shard_map/ppermute | solution.py:356
  13.2 4.0 %collective-permute-done.5.rest_2_ = f32[4,8,128]{2,1,0:T(8,128)S(1)} collective-permute-done((f32[4,8,128]{2,1,0:T(8,128)S(1)}, f32[4,8,128]{2,1,0:T(8,128)S(1)}, u32[]{:S(2)}, u32[]{:S(2)}) %collective-permute-start.5) | collective-permute-done | bytes 16416 | tf_op jit(solution)/shard_map/ppermute | solution.py:356
  17.3 0.0 collective-permute-start.4
  17.3 1.2 %collective-permute-done.4.rest_1_ = f32[4,8,128]{2,1,0:T(8,128)S(1)} collective-permute-done((f32[4,8,128]{2,1,0:T(8,128)S(1)}, f32[4,8,128]{2,1,0:T(8,128)S(1)}, u32[]{:S(2)}, u32[]{:S(2)}) %collective-permute-start.4) | collective-permute-done | bytes 16416 | tf_op jit(solution)/shard_map/ppermute | solution.py:356
  18.4 0.2 collective-permute-start.6
  18.6 1.0 %collective-permute-done.6.rest_3_ = f32[4,8,128]{2,1,0:T(8,128)S(1)} collective-permute-done((f32[4,8,128]{2,1,0:T(8,128)S(1)}, f32[4,8,128]{2,1,0:T(8,128)S(1)}, u32[]{:S(2)}, u32[]{:S(2)}) %collective-permute-start.6) | collective-permute-done | bytes 16416 | tf_op jit(solution)/shard_map/ppermute | solution.py:356
  19.6 0.0 collective-permute-done.2.side_a
  19.6 0.0 collective-permute-done.3.side_b
  19.6 0.2 corners.1
  19.8 0.0 collective-permute-start.7
  19.8 1.9 %collective-permute-start.8 = (f32[5,8,256]{2,1,0:T(8,128)S(1)}, f32[5,8,256]{2,1,0:T(8,128)S(1)}, u32[]{:S(2)}, u32[]{:S(2)}) collective-permute-start(f32[5,8,256]{2,1,0:T(8,128)S(1)} %get-tuple-element.20), channel_id=1, source_target_pairs={{4,8},{12,16},{20,24},{28,0},{8,4},{16,12},{24,20},{0,28},{5,9},{1... | collective-permute-start | bytes 122888 | tf_op jit(solution)/shard_map/ppermute | solution.py:356
  21.7 2.1 %collective-permute-done.7.corner_a = f32[5,8,256]{2,1,0:T(8,128)S(1)} collective-permute-done((f32[5,8,256]{2,1,0:T(8,128)S(1)}, f32[5,8,256]{2,1,0:T(8,128)S(1)}, u32[]{:S(2)}, u32[]{:S(2)}) %collective-permute-start.7) | collective-permute-done | bytes 40992 | tf_op jit(solution)/shard_map/ppermute | solution.py:356
  23.8 2.8 %collective-permute-done.8.corner_b = f32[5,8,256]{2,1,0:T(8,128)S(1)} collective-permute-done((f32[5,8,256]{2,1,0:T(8,128)S(1)}, f32[5,8,256]{2,1,0:T(8,128)S(1)}, u32[]{:S(2)}, u32[]{:S(2)}) %collective-permute-start.8) | collective-permute-done | bytes 40992 | tf_op jit(solution)/shard_map/ppermute | solution.py:356
  26.6 0.0 collective-permute-done.face_a
  26.6 0.0 collective-permute-done.1.face_b
  26.6 0.0 copy-done.1
  26.6 13.3 %substeps.1 = (f32[16,32,256]{2,1,0:T(8,128)}, f32[16,32,256]{2,1,0:T(8,128)}, f32[4,8,128]{2,1,0:T(8,128)S(1)}) custom-call(f32[16,32,256]{2,1,0:T(8,128)S(1)} %copy-done.1, f32[16,32,256]{2,1,0:T(8,128)S(1)} %copy-done.2, f32[2,4,32,256]{3,2,1,0:T(8,128)S(1)} %collective-permute-done.face_a, f32[2,4,32,256]{3,2,1,0:T(8,128)S(1)} %collective-permute-done.1.face_b, ...), custom_call_target="tpu_custom_call" | custom-call | flops 40000000 | bytes 3000000 | tf_op jit(solution)/shard_map/substeps/pallas_call | solution.py:315
  39.9 0.0 copy-start.3
  39.9 1.6 %collective-permute-start.10 = (f32[4,8,128]{2,1,0:T(8,128)S(1)}, f32[4,8,128]{2,1,0:T(8,128)S(1)}, u32[]{:S(2)}, u32[]{:S(2)}) collective-permute-start(f32[4,8,128]{2,1,0:T(8,128)S(1)} %get-tuple-element.24.mine), channel_id=1, source_target_pairs={{0,2},{1,3},{2,0},{3,1},{4,6},{5,7},{6,4},{7,5},{8,10},{9,11},{10,... | collective-permute-start | bytes 49160 | tf_op jit(solution)/shard_map/ppermute | solution.py:356
  41.5 0.0 collective-permute-start.9
  41.5 2.2 %collective-permute-done.10.chip = f32[4,8,128]{2,1,0:T(8,128)S(1)} collective-permute-done((f32[4,8,128]{2,1,0:T(8,128)S(1)}, f32[4,8,128]{2,1,0:T(8,128)S(1)}, u32[]{:S(2)}, u32[]{:S(2)}) %collective-permute-start.10) | collective-permute-done | bytes 16416 | tf_op jit(solution)/shard_map/ppermute | solution.py:356
  43.7 0.0 copy-start.4
  43.7 0.0 collective-permute-start.11
  43.7 0.0 collective-permute-done.9.core
  43.7 0.0 copy-start.5
  43.7 1.2 %collective-permute-done.11.far = f32[4,8,128]{2,1,0:T(8,128)S(1)} collective-permute-done((f32[4,8,128]{2,1,0:T(8,128)S(1)}, f32[4,8,128]{2,1,0:T(8,128)S(1)}, u32[]{:S(2)}, u32[]{:S(2)}) %collective-permute-start.11) | collective-permute-done | bytes 16416 | tf_op jit(solution)/shard_map/ppermute | solution.py:356
  44.9 0.0 copy-done.3
  44.9 0.0 copy-done.4
  44.9 0.0 copy-done.5
  44.9 0.0 copy-start.6
  44.9 0.6 %copy-done.6 = f32[4,8,128]{2,1,0:T(8,128)} copy-done((f32[4,8,128]{2,1,0:T(8,128)}, f32[4,8,128]{2,1,0:T(8,128)S(1)}, u32[]{:S(2)}) %copy-start.6) | copy-done | bytes 16408
  45.5 1.5 %owner.1 = f32[4,32,16]{2,1,0:T(8,128)} custom-call(f32[4,8,128]{2,1,0:T(8,128)} %copy-done.3, f32[4,8,128]{2,1,0:T(8,128)} %copy-done.5, f32[4,8,128]{2,1,0:T(8,128)} %copy-done.4, f32[4,8,128]{2,1,0:T(8,128)} %copy-done.6), custom_call_target="tpu_custom_call" | custom-call | tf_op jit(solution)/shard_map/owner/pallas_call | solution.py:344
  47.0 1.5 %copy.7 = f32[4,32,16]{1,2,0:T(8,128)} copy(f32[4,32,16]{2,1,0:T(8,128)} %owner.1) | data formatting | bytes 16384
Async XLA Ops:
  1.5 1.1 %copy-start = (f32[16,32,256]{2,1,0:T(8,128)S(1)}, f32[16,32,256]{2,1,0:T(8,128)}, u32[]{:S(2)}) copy-start(f32[16,32,256]{2,1,0:T(8,128)} %phase.3) | copy-start | bytes 1572868
  2.5 1.0 %copy-start.2 = (f32[16,32,256]{2,1,0:T(8,128)S(1)}, f32[16,32,256]{2,1,0:T(8,128)}, u32[]{:S(2)}) copy-start(f32[16,32,256]{2,1,0:T(8,128)} %solute.3) | copy-start | bytes 1572868
  3.6 23.1 %copy-start.1 = (f32[16,32,256]{2,1,0:T(8,128)S(1)}, f32[16,32,256]{2,1,0:T(8,128)}, u32[]{:S(2)}) copy-start(f32[16,32,256]{2,1,0:T(8,128)} %phase.3) | copy-start | bytes 1572868
  4.5 22.1 %collective-permute-start = (f32[2,4,32,256]{3,2,1,0:T(8,128)S(1)}, f32[2,4,32,256]{3,2,1,0:T(8,128)S(1)}, u32[]{:S(2)}, u32[]{:S(2)}) collective-permute-start(f32[2,4,32,256]{3,2,1,0:T(8,128)S(1)} %get-tuple-element.14), channel_id=1, source_target_pairs={{0,4},{8,12},{16,20},{24,28},{4,0},{12,8},{20,16},{28,24},{1,5},{9... | collective-permute-start | bytes 786440 | tf_op jit(solution)/shard_map/ppermute | solution.py:356
  7.6 19.1 %collective-permute-start.1 = (f32[2,4,32,256]{3,2,1,0:T(8,128)S(1)}, f32[2,4,32,256]{3,2,1,0:T(8,128)S(1)}, u32[]{:S(2)}, u32[]{:S(2)}) collective-permute-start(f32[2,4,32,256]{3,2,1,0:T(8,128)S(1)} %get-tuple-element.15), channel_id=1, source_target_pairs={{4,8},{12,16},{20,24},{28,0},{8,4},{16,12},{24,20},{0,28},{5,9},{1... | collective-permute-start | bytes 786440 | tf_op jit(solution)/shard_map/ppermute | solution.py:356
  11.1 8.5 %collective-permute-start.2 = (f32[16,8,256]{2,1,0:T(8,128)S(1)}, f32[16,8,256]{2,1,0:T(8,128)S(1)}, u32[]{:S(2)}, u32[]{:S(2)}) collective-permute-start(f32[16,8,256]{2,1,0:T(8,128)S(1)} %get-tuple-element.16), channel_id=1, source_target_pairs={{0,1},{2,3},{1,0},{3,2},{4,5},{6,7},{5,4},{7,6},{8,9},{10,11},{9,8... | collective-permute-start | bytes 393224 | tf_op jit(solution)/shard_map/ppermute | solution.py:356
  11.1 8.5 %collective-permute-start.3 = (f32[16,8,256]{2,1,0:T(8,128)S(1)}, f32[16,8,256]{2,1,0:T(8,128)S(1)}, u32[]{:S(2)}, u32[]{:S(2)}) collective-permute-start(f32[16,8,256]{2,1,0:T(8,128)S(1)} %get-tuple-element.17), channel_id=1, source_target_pairs={{1,2},{3,0},{2,1},{0,3},{5,6},{7,4},{6,5},{4,7},{9,10},{11,8},{10,... | collective-permute-start | bytes 393224 | tf_op jit(solution)/shard_map/ppermute | solution.py:356
  12.7 4.5 %collective-permute-start.5 = (f32[4,8,128]{2,1,0:T(8,128)S(1)}, f32[4,8,128]{2,1,0:T(8,128)S(1)}, u32[]{:S(2)}, u32[]{:S(2)}) collective-permute-start(f32[4,8,128]{2,1,0:T(8,128)S(1)} %get-tuple-element.18.rest_0_), channel_id=1, source_target_pairs={{0,2},{1,3},{2,0},{3,1},{4,6},{5,7},{6,4},{7,5},{8,10},{9,11},{10,... | collective-permute-start | bytes 49160 | tf_op jit(solution)/shard_map/ppermute | solution.py:356
  17.3 1.2 %collective-permute-start.4 = (f32[4,8,128]{2,1,0:T(8,128)S(1)}, f32[4,8,128]{2,1,0:T(8,128)S(1)}, u32[]{:S(2)}, u32[]{:S(2)}) collective-permute-start(f32[4,8,128]{2,1,0:T(8,128)S(1)} %get-tuple-element.18.rest_0_), channel_id=1, source_target_pairs={{0,1},{2,3},{1,0},{3,2},{4,5},{6,7},{5,4},{7,6},{8,9},{10,11},{9,8... | collective-permute-start | bytes 49160 | tf_op jit(solution)/shard_map/ppermute | solution.py:356
  18.4 1.2 %collective-permute-start.6 = (f32[4,8,128]{2,1,0:T(8,128)S(1)}, f32[4,8,128]{2,1,0:T(8,128)S(1)}, u32[]{:S(2)}, u32[]{:S(2)}) collective-permute-start(f32[4,8,128]{2,1,0:T(8,128)S(1)} %collective-permute-done.5.rest_2_), channel_id=1, source_target_pairs={{0,1},{2,3},{1,0},{3,2},{4,5},{6,7},{5,4},{7,6},{8,9},{10,11},{9,8... | collective-permute-start | bytes 49160 | tf_op jit(solution)/shard_map/ppermute | solution.py:356
  19.8 4.0 %collective-permute-start.7 = (f32[5,8,256]{2,1,0:T(8,128)S(1)}, f32[5,8,256]{2,1,0:T(8,128)S(1)}, u32[]{:S(2)}, u32[]{:S(2)}) collective-permute-start(f32[5,8,256]{2,1,0:T(8,128)S(1)} %get-tuple-element.19), channel_id=1, source_target_pairs={{0,4},{8,12},{16,20},{24,28},{4,0},{12,8},{20,16},{28,24},{1,5},{9... | collective-permute-start | bytes 122888 | tf_op jit(solution)/shard_map/ppermute | solution.py:356
  19.8 6.8 %collective-permute-start.8 = (f32[5,8,256]{2,1,0:T(8,128)S(1)}, f32[5,8,256]{2,1,0:T(8,128)S(1)}, u32[]{:S(2)}, u32[]{:S(2)}) collective-permute-start(f32[5,8,256]{2,1,0:T(8,128)S(1)} %get-tuple-element.20), channel_id=1, source_target_pairs={{4,8},{12,16},{20,24},{28,0},{8,4},{16,12},{24,20},{0,28},{5,9},{1... | collective-permute-start | bytes 122888 | tf_op jit(solution)/shard_map/ppermute | solution.py:356
  39.9 5.0 %copy-start.3 = (f32[4,8,128]{2,1,0:T(8,128)}, f32[4,8,128]{2,1,0:T(8,128)S(1)}, u32[]{:S(2)}) copy-start(f32[4,8,128]{2,1,0:T(8,128)S(1)} %get-tuple-element.24.mine) | copy-start | bytes 49156
  39.9 3.8 %collective-permute-start.10 = (f32[4,8,128]{2,1,0:T(8,128)S(1)}, f32[4,8,128]{2,1,0:T(8,128)S(1)}, u32[]{:S(2)}, u32[]{:S(2)}) collective-permute-start(f32[4,8,128]{2,1,0:T(8,128)S(1)} %get-tuple-element.24.mine), channel_id=1, source_target_pairs={{0,2},{1,3},{2,0},{3,1},{4,6},{5,7},{6,4},{7,5},{8,10},{9,11},{10,... | collective-permute-start | bytes 49160 | tf_op jit(solution)/shard_map/ppermute | solution.py:356
  41.5 2.3 %collective-permute-start.9 = (f32[4,8,128]{2,1,0:T(8,128)S(1)}, f32[4,8,128]{2,1,0:T(8,128)S(1)}, u32[]{:S(2)}, u32[]{:S(2)}) collective-permute-start(f32[4,8,128]{2,1,0:T(8,128)S(1)} %get-tuple-element.24.mine), channel_id=1, source_target_pairs={{0,1},{2,3},{1,0},{3,2},{4,5},{6,7},{5,4},{7,6},{8,9},{10,11},{9,8... | collective-permute-start | bytes 49160 | tf_op jit(solution)/shard_map/ppermute | solution.py:356
  43.7 1.2 %copy-start.4 = (f32[4,8,128]{2,1,0:T(8,128)}, f32[4,8,128]{2,1,0:T(8,128)S(1)}, u32[]{:S(2)}) copy-start(f32[4,8,128]{2,1,0:T(8,128)S(1)} %collective-permute-done.10.chip) | copy-start | bytes 49156
  43.7 1.2 %collective-permute-start.11 = (f32[4,8,128]{2,1,0:T(8,128)S(1)}, f32[4,8,128]{2,1,0:T(8,128)S(1)}, u32[]{:S(2)}, u32[]{:S(2)}) collective-permute-start(f32[4,8,128]{2,1,0:T(8,128)S(1)} %collective-permute-done.10.chip), channel_id=1, source_target_pairs={{0,1},{2,3},{1,0},{3,2},{4,5},{6,7},{5,4},{7,6},{8,9},{10,11},{9,8... | collective-permute-start | bytes 49160 | tf_op jit(solution)/shard_map/ppermute | solution.py:356
  43.7 1.2 %copy-start.5 = (f32[4,8,128]{2,1,0:T(8,128)}, f32[4,8,128]{2,1,0:T(8,128)S(1)}, u32[]{:S(2)}) copy-start(f32[4,8,128]{2,1,0:T(8,128)S(1)} %collective-permute-done.9.core) | copy-start | bytes 49156
  44.9 0.6 %copy-start.6 = (f32[4,8,128]{2,1,0:T(8,128)}, f32[4,8,128]{2,1,0:T(8,128)S(1)}, u32[]{:S(2)}) copy-start(f32[4,8,128]{2,1,0:T(8,128)S(1)} %collective-permute-done.11.far) | copy-start | bytes 49156

commit v2 on v0

v2 whole, which is shorter than its diff:
```python
import functools

import jax
import jax.numpy as jnp
from jax import lax
from jax.experimental import pallas as pl
from jax.experimental.pallas import tpu as pltpu
from jax.sharding import PartitionSpec as P

time_step = 0.1
anisotropy = 0.3
coupling = 2.0
rejection = 0.5

F32 = jnp.float32
HIGHEST = lax.Precision.HIGHEST
HALO = 4
ROWS = 8
LANES = 128
VMEM_LIMIT = 24 * 1024 * 1024


def vmem():
    return pl.BlockSpec(memory_space=pltpu.VMEM)


def anywhere():
    return pl.BlockSpec(memory_space=pl.ANY)


def hbm():
    return pl.BlockSpec(memory_space=pltpu.HBM)


def pairs(count, first):
    forward = [((first + k) % count, (first + k + 1) % count) for k in range(0, count, 2)]
    return forward + [(b, a) for a, b in forward]


def flips(me):
    odd = lax.rem(me, 2)
    return me, me + 1 - 2 * odd, lax.rem(me + 2, 4), 3 - me


def row_ids(shape):
    return lax.broadcasted_iota(jnp.int32, shape, len(shape) - 2)


def lane_ids(shape):
    return lax.broadcasted_iota(jnp.int32, shape, len(shape) - 1)


def start_all(copies, sems):
    copies = [pltpu.make_async_copy(source, target, sems.at[n]) for n, (source, target) in enumerate(copies)]
    for copy in copies:
        copy.start()
    return copies


def wait_all(copies):
    for copy in copies:
        copy.wait()


def fold(table):
    half = table.shape[0] // 2
    return jnp.concatenate([table[:half], table[half:]], axis=1)


def unfold(tile):
    return jnp.concatenate([tile[:, :LANES], tile[:, LANES:]], axis=0)


def pack_kernel(phase, solute, macro, face_a, face_b, side_a, side_b, table, low, high, sems):
    size_x, size_y, size_z = phase.shape
    odd_x = lax.rem(lax.axis_index("gx"), 2)
    even_y = lax.rem(lax.axis_index("gy"), 2) == 0
    start_a = (1 - odd_x) * (size_x - HALO)
    start_b = odd_x * (size_x - HALO)
    copies = []
    for field, ref in enumerate((phase, solute)):
        copies.append((ref.at[pl.ds(start_a, HALO)], face_a.at[field]))
        copies.append((ref.at[pl.ds(start_b, HALO)], face_b.at[field]))
        copies.append((ref.at[:, pl.ds(0, ROWS), :], low.at[field]))
        copies.append((ref.at[:, pl.ds(size_y - ROWS, ROWS), :], high.at[field]))
    copies = start_all(copies, sems)
    wide = jnp.concatenate([macro[k] for k in range(macro.shape[0])], axis=1)
    table[...] = wide
    wait_all(copies)
    top = row_ids((size_x, ROWS, size_z)) < HALO
    low_side = jnp.where(top, low[0], pltpu.roll(low[1], HALO, 1))
    high_side = jnp.where(top, pltpu.roll(high[1], HALO, 1), high[0])
    side_a[pl.ds(0, size_x)] = jnp.where(even_y, high_side, low_side)
    side_b[pl.ds(0, size_x)] = jnp.where(even_y, low_side, high_side)
    if side_a.shape[0] > size_x:
        side_a[size_x] = fold(wide)
        side_b[size_x] = fold(wide)


def pack(phase, solute, macro, ride):
    size_x, size_y, size_z = phase.shape
    coarse_x, coarse_z, coarse_y = macro.shape
    face = jax.ShapeDtypeStruct((2, HALO, size_y, size_z), F32)
    side = jax.ShapeDtypeStruct((size_x + (1 if ride else 0), ROWS, size_z), F32)
    table = jax.ShapeDtypeStruct((coarse_z, coarse_x * coarse_y), F32)
    return pl.pallas_call(
        pack_kernel,
        out_shape=(face, face, side, side, table),
        in_specs=[hbm(), hbm(), vmem()],
        out_specs=[vmem()] * 5,
        scratch_shapes=[
            pltpu.VMEM((2, size_x, ROWS, size_z), F32),
            pltpu.VMEM((2, size_x, ROWS, size_z), F32),
            pltpu.SemaphoreType.DMA((8,)),
        ],
        compiler_params=pltpu.CompilerParams(vmem_limit_bytes=VMEM_LIMIT),
        cost_estimate=pl.CostEstimate(flops=10**5, bytes_accessed=2 * 10**6, transcendentals=0),
        name="pack",
    )(phase, solute, macro)


def corner_kernel(coarse_y, gathered, side_a, side_b, *rest):
    size_x = side_a.shape[0] - (0 if gathered else 1)
    me = lax.axis_index("gy")
    even_x = lax.rem(lax.axis_index("gx"), 2) == 0
    even_y = lax.rem(me, 2) == 0
    if gathered:
        coarse, corner_a, corner_b = rest
    else:
        mine, across, coarse, corner_a, corner_b = rest
        depth = mine.shape[0]
        near, opposite, far = flips(me)[1:]
        for source, tile in (
            (me, mine[...]),
            (opposite, across[...]),
            (near, unfold(side_a[size_x])),
            (far, unfold(side_b[size_x])),
        ):
            coarse[pl.ds(pl.multiple_of(source * depth, depth), depth), :] = tile
    block = coarse[...]
    depth, width = block.shape
    stack = LANES // coarse_y
    height = depth // stack
    row = row_ids(side_a.shape[1:])
    for corner, top_side in ((corner_a, even_x), (corner_b, jnp.logical_not(even_x))):
        for n, keep in ((0, 5), (1, 2)):
            def layer(d, n=n):
                at = jnp.where(top_side, size_x - d, d - 1)
                first, second = side_a[at], side_b[at]
                return jnp.where(even_y, second, first) if n == 0 else jnp.where(even_y, first, second)

            corner[2 * n] = layer(1)
            corner[2 * n + 1] = jnp.where(row == keep, pltpu.roll(layer(3), 6 if n == 0 else 2, 0), layer(2))
        edge = jnp.where(top_side, block[:, width - coarse_y :], block[:, :coarse_y])
        edge = jnp.concatenate([edge[q * height : (q + 1) * height] for q in range(stack)], axis=1)
        corner[pl.ds(4, height // 16)] = fold(edge).reshape(height // 16, ROWS, 2 * LANES)


def corners(side_a, side_b, tables, coarse_y, coarse_shape):
    size_z = side_a.shape[2]
    gathered = len(tables) == 1
    height = coarse_shape[0] * coarse_y // LANES
    corner = jax.ShapeDtypeStruct((4 + height // 16, ROWS, size_z), F32)
    coarse = jax.ShapeDtypeStruct(coarse_shape, F32)
    out = pl.pallas_call(
        functools.partial(corner_kernel, coarse_y, gathered),
        out_shape=(corner, corner) if gathered else (coarse, corner, corner),
        in_specs=[vmem()] * (2 + len(tables)),
        out_specs=[vmem()] * (2 if gathered else 3),
        compiler_params=pltpu.CompilerParams(vmem_limit_bytes=VMEM_LIMIT),
        cost_estimate=pl.CostEstimate(flops=10**5, bytes_accessed=4 * 10**5, transcendentals=0),
        name="corners",
    )(side_a, side_b, *tables)
    return (*tables, *out) if gathered else out


def weights(lower, frac, shape, tick):
    first, second = lower
    return jnp.where(tick == first, 1.0 - frac, 0.0) + jnp.where(tick == second, frac, 0.0)


def interpolate(block, coarse_y, size_y, size_z):
    depth, width = block.shape
    rows = size_y + 2 * HALO
    shape = (depth, size_z)
    fine = lane_ids(shape)
    lower = (2 * fine + 5) // 8 - 1
    frac = (2 * fine - 3 - 8 * lower).astype(F32) / 8.0
    ends = jnp.clip(lower, 0, depth - 1), jnp.clip(lower + 1, 0, depth - 1)
    along_z = weights(ends, frac, shape, row_ids(shape))
    deep = lax.dot_general(block, along_z, (((0,), (0,)), ((), ())), precision=HIGHEST, preferred_element_type=F32)
    shape = (rows, coarse_y)
    fine = row_ids(shape)
    fine = jnp.where(fine >= size_y + HALO, fine - rows, fine)
    local = (2 * fine + 13) // 8 - 2
    frac = (2 * fine - 3 - 8 * local).astype(F32) / 8.0
    lower = local + lax.axis_index("gy") * (size_y // 4) + coarse_y
    ends = lax.rem(lower, coarse_y), lax.rem(lower + 1, coarse_y)
    along_y = weights(ends, frac, shape, lane_ids(shape))
    return [
        jnp.dot(along_y, deep[k * coarse_y : (k + 1) * coarse_y], precision=HIGHEST, preferred_element_type=F32)
        for k in range(width // coarse_y)
    ]


def blend(x, fans):
    lower = (2 * x - 3) // 8
    frac = (2 * x - 3 - 8 * lower) / 8.0
    return (1.0 - frac) * fans[lower] + frac * fans[lower + 1]


def turn(value, by, axis):
    return pltpu.roll(value, by % value.shape[axis], axis)


def z_matrices(size_z):
    shape = (size_z, size_z)
    source, target = row_ids(shape), lane_ids(shape)
    hit = lambda at: (source == at).astype(F32)
    end = size_z - 1
    gradient = hit(jnp.minimum(target + 1, end)) - hit(jnp.maximum(target - 1, 0))
    difference = hit(target + 1) - hit(target - 1)
    laplace = hit(jnp.minimum(target + 2, end)) + hit(jnp.maximum(target - 2, 0)) - 6.0 * hit(target)
    return tuple(m.astype(jnp.bfloat16) for m in (gradient, difference, laplace))


def along(slabs, matrix):
    value = slabs.reshape(-1, slabs.shape[-1])
    coarse = value.astype(jnp.bfloat16)
    rest = (value - coarse.astype(F32)).astype(jnp.bfloat16)
    product = jnp.dot(coarse, matrix, preferred_element_type=F32) + jnp.dot(rest, matrix, preferred_element_type=F32)
    return product.reshape(slabs.shape)


def flux(before, here, after, along_z):
    along_x = after - before
    along_y = turn(here, -1, 0) - turn(here, 1, 0)
    sq_x = along_x * along_x
    sq_y = along_y * along_y
    both = sq_x + sq_y
    inverse = 1.0 / (both + 4.0)
    factor = 1.0 + anisotropy * (both * both - 8.0 * (sq_x * sq_y)) * (inverse * inverse)
    stiff = (0.25 * time_step) * (factor * factor)
    return stiff * along_x, stiff * along_y, stiff * along_z


def spread(flux_y):
    return turn(flux_y, -1, 0) - turn(flux_y, 1, 0)


def phase_change(here, conc, theta, divergence):
    square = 1.0 - here * here
    drive = square * (here - (coupling * square) * (theta + conc))
    return divergence + time_step * drive


def solute_step(conc, beyond_x, beyond_y, along_z, change):
    return conc + (0.25 * time_step) * (beyond_x + beyond_y + along_z) + rejection * change


def next_row(conc):
    return turn(conc, -2, 0) + turn(conc, 2, 0)


def pools(size_y, size_z):
    pool_y = (row_ids((size_y // 4, size_y)) == lane_ids((size_y // 4, size_y)) // 4).astype(F32)
    pool_z = (row_ids((size_z, LANES)) // 4 == lane_ids((size_z, LANES))).astype(F32)
    return pool_y, pool_z


def restrict(change, pool):
    pool_y, pool_z = pool
    change = jnp.dot(change, pool_z, precision=HIGHEST, preferred_element_type=F32)
    return (0.5 / 64.0) * jnp.dot(pool_y, change, precision=HIGHEST, preferred_element_type=F32)


KEPT = ("p0", "c0", "dz0", "cz0", "gx0", "dv0", "p1", "c1", "dz1", "cz1", "gx1", "dv1", "th")


def spans(size_x):
    ranges = dict(
        p0=(0, size_x), c0=(0, size_x), dz0=(0, size_x), cz0=(0, size_x), gx0=(1, size_x - 1), dv0=(1, size_x - 1),
        p1=(2, size_x - 2), c1=(2, size_x - 2), dz1=(2, size_x - 2), cz1=(2, size_x - 2),
        gx1=(3, size_x - 3), dv1=(3, size_x - 3), th=(2, size_x - 2),
    )
    return {name: ranges[name] for name in KEPT}


def inner_kernel(coarse_y, phase, solute, side_a, side_b, coarse, phase_out, solute_out, latent, *rest):
    kept = dict(zip(KEPT, rest[: len(KEPT)]))
    fz, phase_new, solute_new, sems, out_sems = rest[len(KEPT) :]
    size_x, size_y, size_z = phase.shape
    span = spans(size_x)
    even_y = lax.rem(lax.axis_index("gy"), 2) == 0
    at = lambda name, x: kept[name].at[x - span[name][0]]
    get = lambda name, x: kept[name][x - span[name][0]]
    copies = start_all(
        [(ref, kept[name].at[:, pl.ds(0, size_y), :]) for name, ref in (("p0", phase), ("c0", solute))], sems
    )
    top = row_ids((size_x, ROWS, size_z)) < HALO
    first, second = side_a[pl.ds(0, size_x)], side_b[pl.ds(0, size_x)]
    low, high = jnp.where(even_y, second, first), jnp.where(even_y, first, second)
    kept["p0"][:, pl.ds(size_y, ROWS), :] = jnp.where(top, high, low)
    kept["c0"][:, pl.ds(size_y, ROWS), :] = pltpu.roll(jnp.where(top, low, high), HALO, 1)
    fans = dict(enumerate(interpolate(coarse[...], coarse_y, size_y, size_z)))
    for x in range(*span["th"]):
        at("th", x)[...] = blend(x, fans)
    gradient, difference, laplace = z_matrices(size_z)
    wait_all(copies)

    for step in "01":
        p, c, dz, cz, gx, dv = (name + step for name in ("p", "c", "dz", "cz", "gx", "dv"))
        kept[dz][...] = along(kept[p][...], gradient)
        kept[cz][...] = along(kept[c][...], laplace)
        begin, end = span[gx]
        for x in range(begin, end):
            flux_x, flux_y, flux_z = flux(get(p, x - 1), get(p, x), get(p, x + 1), get(dz, x))
            at(gx, x)[...] = flux_x
            at(dv, x)[...] = spread(flux_y)
            fz[x - begin] = flux_z
        kept[dv][...] += along(fz[pl.ds(0, end - begin)], difference)
        take = (lambda v: v) if step == "0" else (lambda v: v[:size_y])
        for x in range(begin + 1, end - 1):
            here, conc = take(get(p, x)), get(c, x)
            divergence = take(get(gx, x + 1)) - take(get(gx, x - 1)) + take(get(dv, x))
            change = phase_change(here, take(conc), take(get("th", x)), divergence)
            beyond = take(get(c, x + 2)) + take(get(c, x - 2))
            new_conc = solute_step(take(conc), beyond, take(next_row(conc)), take(get(cz, x)), change)
            if step == "0":
                at("p1", x)[...] = here + change
                at("c1", x)[...] = new_conc
            else:
                phase_new[x - begin - 1] = here + change
                solute_new[x - begin - 1] = new_conc
    count = size_x - 8
    copies = start_all(
        [(phase_new, phase_out.at[pl.ds(4, count)]), (solute_new, solute_out.at[pl.ds(4, count)])], out_sems
    )
    pool = pools(size_y, size_z)
    for k in range(1, size_x // 4 - 1):
        change = jnp.zeros((size_y, size_z), F32)
        for x in range(4 * k, 4 * k + 4):
            change = change + (phase_new[x - 4] - get("p0", x)[:size_y])
        latent[k - 1] = restrict(change, pool)
    wait_all(copies)


def inner(phase, solute, side_a, side_b, coarse, coarse_y):
    size_x, size_y, size_z = phase.shape
    rows = size_y + 2 * HALO
    out = jax.ShapeDtypeStruct(phase.shape, F32)
    kept = [jax.ShapeDtypeStruct((end - begin, rows, size_z), F32) for begin, end in spans(size_x).values()]
    latent = jax.ShapeDtypeStruct((size_x // 4 - 2, size_y // 4, LANES), F32)
    part = pltpu.VMEM((size_x - 8, size_y, size_z), F32)
    return pl.pallas_call(
        functools.partial(inner_kernel, coarse_y),
        out_shape=(out, out, latent, *kept),
        in_specs=[anywhere(), anywhere()] + [vmem()] * 3,
        out_specs=[hbm(), hbm()] + [vmem()] * (1 + len(kept)),
        scratch_shapes=[
            pltpu.VMEM((size_x - 2, rows, size_z), F32), part, part,
            pltpu.SemaphoreType.DMA((2,)), pltpu.SemaphoreType.DMA((2,)),
        ],
        compiler_params=pltpu.CompilerParams(vmem_limit_bytes=VMEM_LIMIT),
        cost_estimate=pl.CostEstimate(flops=2 * 10**7, bytes_accessed=3 * 10**6, transcendentals=0),
        name="inner",
    )(phase, solute, side_a, side_b, coarse)


def rim_kernel(coarse_y, phase_in, solute_in, face_a, face_b, corner_a, corner_b, coarse, inner_latent, *rest):
    kept = dict(zip(KEPT, rest[: len(KEPT)]))
    phase_out, solute_out, latent = rest[len(KEPT) : len(KEPT) + 3]
    hp0, hc0, p1, c1, gx, dv, dz, cz, fz, th, phase_new, solute_new, sems, out_sems = rest[len(KEPT) + 3 :]
    size_x = latent.shape[0] * 4
    size_y, size_z = phase_out.shape[1:]
    span = spans(size_x)
    even_x = lax.rem(lax.axis_index("gx"), 2) == 0
    spot_a = jnp.where(even_x, HALO, 0)
    spot_b = HALO - spot_a
    copies = []
    for n, field in enumerate((hp0, hc0)):
        copies.append((face_a.at[n], field.at[pl.ds(spot_a, HALO), pl.ds(0, size_y), :]))
        copies.append((face_b.at[n], field.at[pl.ds(spot_b, HALO), pl.ds(0, size_y), :]))
    copies = start_all(copies, sems)

    top = row_ids((ROWS, size_z)) < HALO

    def put(at, low, high):
        hp0[at, pl.ds(size_y, ROWS), :] = jnp.where(top, high, low)
        hc0[at, pl.ds(size_y, ROWS), :] = pltpu.roll(jnp.where(top, low, high), HALO, 0)

    edges = []
    for above in (False, True):
        use_a = even_x if above else jnp.logical_not(even_x)
        tile = jnp.where(use_a, corner_a[...], corner_b[...])
        place = lambda d: HALO - 1 + d if above else HALO - d
        put(place(1), tile[0], tile[2])
        put(place(2), tile[1], tile[3])
        put(place(3), pltpu.roll(tile[1], 2, 0), pltpu.roll(tile[3], 6, 0))
        put(place(4), jnp.zeros_like(tile[0]), jnp.zeros_like(tile[0]))
        edge = unfold(tile[4:].reshape(-1, 2 * LANES))
        stack = LANES // coarse_y
        edges.append(
            jnp.concatenate([edge[:, q * coarse_y : (q + 1) * coarse_y] for q in range(stack)], axis=0)
        )
    width = coarse.shape[1]
    below = jnp.concatenate([edges[0], coarse[:, :coarse_y]], axis=1)
    above = jnp.concatenate([coarse[:, width - coarse_y :], edges[1]], axis=1)
    fans = interpolate(jnp.concatenate([below, above], axis=1), coarse_y, size_y, size_z)
    last = size_x // 4
    fans = {-1: fans[0], 0: fans[1], last - 1: fans[2], last: fans[3]}
    gradient, difference, laplace = z_matrices(size_z)

    def ref(array, begin, x):
        half = array.shape[0] // 2
        return array.at[x - begin] if x < size_x // 2 else array.at[half + x - (size_x - half - begin)]

    def get(name, x):
        begin, end = span[name]
        if begin <= x < end:
            return kept[name][x - begin]
        own, first = dict(
            p0=(hp0, -4), c0=(hc0, -4), dz0=(dz, -3), cz0=(cz, -2), gx0=(gx, -3), dv0=(dv, -2),
            p1=(p1, -2), c1=(c1, -2), dz1=(dz, -1), cz1=(cz, 0), gx1=(gx, -1), dv1=(dv, 0), th=(th, -2),
        )[name]
        return ref(own, first, x)[...]

    rim = lambda begin, end: [*range(begin, end), *range(size_x - end, size_x - begin)]
    for x in rim(-2, 2):
        ref(th, -2, x)[...] = blend(x, fans)
    wait_all(copies)

    for step, begin in (("0", -3), ("1", -1)):
        p, c, gx_, dv_, dz_, cz_ = (name + step for name in ("p", "c", "gx", "dv", "dz", "cz"))
        fields = (hp0[pl.ds(1, 6)], hc0[pl.ds(2, 4)]) if step == "0" else (p1[pl.ds(1, 6)], c1[pl.ds(2, 4)])
        dz[...] = along(fields[0], gradient)
        cz[...] = along(fields[1], laplace)
        for x in rim(begin, begin + 4):
            flux_x, flux_y, flux_z = flux(get(p, x - 1), get(p, x), get(p, x + 1), get(dz_, x))
            ref(gx, begin, x)[...] = flux_x
            if x not in (begin, size_x - 1 - begin):
                ref(dv, begin + 1, x)[...] = spread(flux_y)
                ref(fz, begin + 1, x)[...] = flux_z
        dv[...] += along(fz[...], difference)
        take = (lambda v: v) if step == "0" else (lambda v: v[:size_y])
        for x in rim(begin + 1, begin + 5):
            here, conc = take(get(p, x)), get(c, x)
            divergence = take(get(gx_, x + 1)) - take(get(gx_, x - 1)) + take(get(dv_, x))
            change = phase_change(here, take(conc), take(get("th", x)), divergence)
            beyond = take(get(c, x + 2)) + take(get(c, x - 2))
            new_conc = solute_step(take(conc), beyond, take(next_row(conc)), take(get(cz_, x)), change)
            if step == "0":
                ref(p1, -2, x)[...] = here + change
                ref(c1, -2, x)[...] = new_conc
            else:
                ref(phase_new, 0, x)[...] = here + change
                ref(solute_new, 0, x)[...] = new_conc
    copies = []
    for n, (new, out) in enumerate(((phase_new, phase_out), (solute_new, solute_out))):
        copies.append((new.at[pl.ds(0, 4)], out.at[pl.ds(0, 4)]))
        copies.append((new.at[pl.ds(4, 4)], out.at[pl.ds(size_x - 4, 4)]))
    copies = start_all(copies, out_sems)
    pool = pools(size_y, size_z)
    latent[pl.ds(1, last - 2)] = inner_latent[...]
    for k in (0, last - 1):
        change = jnp.zeros((size_y, size_z), F32)
        for x in range(4 * k, 4 * k + 4):
            change = change + (ref(phase_new, 0, x)[...] - get("p0", x)[:size_y])
        latent[k] = restrict(change, pool)
    wait_all(copies)


def rims(phase, solute, face_a, face_b, corner_a, corner_b, coarse, inner_latent, kept, coarse_y):
    size_x, size_y, size_z = phase.shape
    rows = size_y + 2 * HALO
    out = jax.ShapeDtypeStruct(phase.shape, F32)
    slabs = lambda count: pltpu.VMEM((count, rows, size_z), F32)
    part = pltpu.VMEM((8, size_y, size_z), F32)
    return pl.pallas_call(
        functools.partial(rim_kernel, coarse_y),
        out_shape=(out, out, jax.ShapeDtypeStruct((size_x // 4, size_y // 4, LANES), F32)),
        in_specs=[hbm(), hbm()] + [vmem()] * (6 + len(kept)),
        out_specs=[hbm(), hbm(), vmem()],
        scratch_shapes=[
            slabs(8), slabs(8), slabs(8), slabs(8), slabs(8), slabs(6), slabs(6), slabs(4), slabs(6), slabs(8), part, part,
            pltpu.SemaphoreType.DMA((4,)), pltpu.SemaphoreType.DMA((4,)),
        ],
        input_output_aliases={0: 0, 1: 1},
        compiler_params=pltpu.CompilerParams(vmem_limit_bytes=VMEM_LIMIT),
        cost_estimate=pl.CostEstimate(flops=2 * 10**7, bytes_accessed=3 * 10**6, transcendentals=0),
        name="rims",
    )(phase, solute, face_a, face_b, corner_a, corner_b, coarse, inner_latent, *kept)


def owner_kernel(coarse_z, mine, core, chip, far, out):
    me = lax.axis_index("gy")
    coarse_x, per, _ = mine.shape
    lane = lane_ids((coarse_x, coarse_z, coarse_x * per))
    total = jnp.zeros(lane.shape, F32)
    shift = lax.rem(LANES - me * coarse_z, LANES)
    for source, ref in zip(flips(me), (mine, core, chip, far)):
        block = jnp.stack([pltpu.roll(ref[k], shift, 1)[:, :coarse_z] for k in range(coarse_x)])
        block = jnp.swapaxes(block, 1, 2)
        block = jnp.concatenate([block] * 4, axis=2)
        total = jnp.where((lane >= source * per) & (lane < (source + 1) * per), block, total)
    out[...] = total


def owner(parts, coarse_y, coarse_z):
    coarse_x = parts[0].shape[0]
    return pl.pallas_call(
        functools.partial(owner_kernel, coarse_z),
        out_shape=jax.ShapeDtypeStruct((coarse_x, coarse_z, coarse_y), F32),
        in_specs=[vmem()] * 4,
        out_specs=vmem(),
        compiler_params=pltpu.CompilerParams(vmem_limit_bytes=VMEM_LIMIT),
        name="owner",
    )(*parts)


def body(phase, solute, macro_temp):
    count_x, count_y = lax.axis_size("gx"), lax.axis_size("gy")
    coarse_x, coarse_y, coarse_z = macro_temp.shape
    near_x, far_x = pairs(count_x, 0), pairs(count_x, 1)
    near_y, far_y = pairs(count_y, 0), pairs(count_y, 1)
    across = [(k, (k + count_y // 2) % count_y) for k in range(count_y)]
    ride = count_y == 4
    macro = jnp.swapaxes(macro_temp, 1, 2)
    face_a, face_b, side_a, side_b, table = pack(phase, solute, macro, ride)
    face_a = lax.ppermute(face_a, "gx", near_x)
    face_b = lax.ppermute(face_b, "gx", far_x)
    side_b = lax.ppermute(side_b, "gy", far_y)
    side_a = lax.ppermute(side_a, "gy", near_y)
    coarse_shape = (coarse_z * count_y, coarse_x * coarse_y)
    if ride:
        tables = (table, lax.ppermute(table, "gy", across))
    else:
        tables = (lax.all_gather(table, "gy").reshape(coarse_shape),)
    coarse, corner_a, corner_b = corners(side_a, side_b, tables, coarse_y, coarse_shape)
    corner_a = lax.ppermute(corner_a, "gx", near_x)
    corner_b = lax.ppermute(corner_b, "gx", far_x)
    phase_out, solute_out, inner_latent, *kept = inner(phase, solute, side_a, side_b, coarse, coarse_y)
    phase_out, solute_out, latent = rims(
        phase_out, solute_out, face_a, face_b, corner_a, corner_b, coarse, inner_latent, kept, coarse_y
    )
    if ride:
        chip = lax.ppermute(latent, "gy", across)
        core = lax.ppermute(latent, "gy", near_y)
        latent = owner((latent, core, chip, lax.ppermute(chip, "gy", near_y)), coarse_y, coarse_z)
        latent = jnp.swapaxes(latent, 1, 2)
    else:
        split = latent[:, :, : coarse_z * count_y].reshape(coarse_x, latent.shape[1], count_y, coarse_z)
        latent = lax.all_to_all(split, "gy", split_axis=2, concat_axis=1, tiled=True)
        latent = latent.reshape(coarse_x, coarse_y, coarse_z)
    return phase_out, solute_out, latent


def solution(mesh):
    in_specs = (P("gx", "gy", None), P("gx", "gy", None), P("gx", None, "gy"))
    out_specs = (P("gx", "gy", None), P("gx", "gy", None), P("gx", None, "gy"))
    return jax.shard_map(body, mesh=mesh, in_specs=in_specs, out_specs=out_specs, check_vma=False)
```

time: 98.8 us -> 34.2 us (0.35)
  other arithmetic: 29.2 us -> 0 us
  local copies, waits for them, and re-layouts: 27 us -> 2.84 us
  starting transfers between devices: 28.7 us -> 12.2 us
  Pallas kernels: 0 us -> 10.1 us
  waiting for transfers between devices: 10.5 us -> 8.09 us
  matrix products: 1.25 us -> 0 us
    reshape x9 -> x0, local copies, waits for them, and re-layouts: 20.7 us -> none  [the longest x1 19.5 us: body(): change.reshape(cells_x // 4, 4, cells_y // 4, 4, cells_z // 4, 4)]
    mul x9 -> x0, other arithmetic: 11.9 us -> none  [the longest x2 3.45 us: divergence(): grad_x = 0.5 * (grid[2:, 1:-1, 1:-1] - grid[:-2, 1:-1, 1:-1])]
    pallas_call x0 -> x5, Pallas kernels: none -> 10.1 us  [the longest x1 4.2 us: inner(): pl.pallas_call(functools.partial(inner_kernel, coarse_y), out_shape=(out,...]
    ppermute x12 -> x10, starting transfers between devices: 21.1 us -> 12.2 us  [the longest x1 3.54 us: body(): face_b = lax.ppermute(face_b, 'gx', far_x)]
    all_to_all x2 -> x0, starting transfers between devices: 7.69 us -> none  [the longest x1 4.21 us: body(): lax.all_to_all(macro_temp, 'gy', split_axis=1, concat_axis=2, tiled=True)]
    reduce_sum x1 -> x0, other arithmetic: 7.1 us -> none  [body(): change.reshape(cells_x // 4, 4, cells_y // 4, 4, cells_z // 4, 4)]
    add x1 -> x0, other arithmetic: 3.49 us -> none  [substep(): conc + time_step * divergence(solute_pad, False)]
    concatenate x5 -> x0, other arithmetic: 2.36 us -> none  [the longest x3 1.91 us: divergence(): grid = jnp.pad(pad_field, ((0, 0), (0, 0), (2, 2)), mode='edge')]
  transfers between devices with their start and end apart: 14 -> 10, of which waited for: 8 -> 4; matrix products, arithmetic and copies ran while one was open for 8% -> 0% of each run, Pallas kernels for 0% -> 13%
where the time goes in v2:
time: 34.2 us; the launch traced here: 33.9 us
  starting transfers between devices  12.2 us (36%)
  Pallas kernels  10.1 us (30%)
  waiting for transfers between devices  8.09 us (24%)
  local copies, waits for them, and re-layouts  2.84 us (8%)
  between operations  0.69 us (2%)
    pallas_call x1, Pallas kernels, inner(): pl.pallas_call(functools.partial(inner_kernel, coarse_y), out_shape=(out,...  4.2 us
    ppermute x1, waiting for transfers between devices, body(): tables = (table, lax.ppermute(table, 'gy', across))  4.01 us
    pallas_call x1, Pallas kernels, rims(): pl.pallas_call(functools.partial(rim_kernel, coarse_y), out_shape=(out, o...  3.66 us
    ppermute x1, starting transfers between devices, body(): face_b = lax.ppermute(face_b, 'gx', far_x)  3.54 us
    ppermute x1, starting transfers between devices, body(): face_a = lax.ppermute(face_a, 'gx', near_x)  3.03 us
    unnamed x8, local copies, waits for them, and re-layouts  2.84 us
    ppermute x1, waiting for transfers between devices, body(): chip = lax.ppermute(latent, 'gy', across)  2.24 us
    ppermute x1, starting transfers between devices, body(): corner_b = lax.ppermute(corner_b, 'gx', far_x)  1.9 us
  transfers between devices with their start and end apart: 10, of which 4 were waited for; matrix products, arithmetic and copies ran while one was open for 0% of the time, Pallas kernels for 13%

profile of v2, /device:TPU:0, one launch (start us, length us, event | category | flops | bytes accessed | tf_op | source)
XLA Modules:
  0.0 33.9 jit_solution(588047870397655863)
XLA Ops:
  0.6 0.0 copy-start
  0.6 1.0 %copy-done = f32[16,32,256]{2,1,0:T(8,128)S(1)} copy-done((f32[16,32,256]{2,1,0:T(8,128)S(1)}, f32[16,32,256]{2,1,0:T(8,128)}, u32[]{:S(2)}) %copy-start) | copy-done | bytes 524312
  1.7 0.0 copy-start.2
  1.7 1.0 %copy-done.2 = f32[16,32,256]{2,1,0:T(8,128)S(1)} copy-done((f32[16,32,256]{2,1,0:T(8,128)S(1)}, f32[16,32,256]{2,1,0:T(8,128)}, u32[]{:S(2)}) %copy-start.2) | copy-done | bytes 524312
  2.7 0.0 copy-start.3
  2.7 0.8 %copy-done.3 = f32[4,32,16]{1,2,0:T(8,128)S(1)} copy-done((f32[4,32,16]{1,2,0:T(8,128)S(1)}, f32[4,32,16]{1,2,0:T(8,128)}, u32[]{:S(2)}) %copy-start.3) | copy-done | bytes 8216
  3.5 0.0 copy-start.1
  3.5 0.9 %pack.1 = (f32[2,4,32,256]{3,2,1,0:T(8,128)S(1)}, f32[2,4,32,256]{3,2,1,0:T(8,128)S(1)}, f32[17,8,256]{2,1,0:T(8,128)S(1)}, f32[17,8,256]{2,1,0:T(8,128)S(1)}, f32[16,128]{1,0:T(8,128)S(1)}) custom-call(f32[16,32,256]{2,1,0:T(8,128)S(1)} %copy-done, f32[16,32,256]{2,1,0:T(8,128)S(1)} %copy-done.2, f32[4,16,32]{2,1,0:T(8,128)S(1)} %bitcast.2), custom_call_target="tpu_custom_call" | custom-call | flops 100000 | bytes 2000000 | tf_op jit(solution)/shard_map/pack/pallas_call | solution.py:106
  4.4 3.0 %collective-permute-start.3 = (f32[2,4,32,256]{3,2,1,0:T(8,128)S(1)}, f32[2,4,32,256]{3,2,1,0:T(8,128)S(1)}, u32[]{:S(2)}, u32[]{:S(2)}) collective-permute-start(f32[2,4,32,256]{3,2,1,0:T(8,128)S(1)} %get-tuple-element.36), channel_id=1, source_target_pairs={{0,4},{8,12},{16,20},{24,28},{4,0},{12,8},{20,16},{28,24},{1,5},{9... | collective-permute-start | bytes 786440 | tf_op jit(solution)/shard_map/ppermute | solution.py:530
  7.4 3.5 %collective-permute-start.4 = (f32[2,4,32,256]{3,2,1,0:T(8,128)S(1)}, f32[2,4,32,256]{3,2,1,0:T(8,128)S(1)}, u32[]{:S(2)}, u32[]{:S(2)}) collective-permute-start(f32[2,4,32,256]{3,2,1,0:T(8,128)S(1)} %get-tuple-element.37), channel_id=1, source_target_pairs={{4,8},{12,16},{20,24},{28,0},{8,4},{16,12},{24,20},{0,28},{5,9},{1... | collective-permute-start | bytes 786440 | tf_op jit(solution)/shard_map/ppermute | solution.py:531
  11.0 0.0 collective-permute-start
  11.0 1.6 %collective-permute-start.1 = (f32[17,8,256]{2,1,0:T(8,128)S(1)}, f32[17,8,256]{2,1,0:T(8,128)S(1)}, u32[]{:S(2)}, u32[]{:S(2)}) collective-permute-start(f32[17,8,256]{2,1,0:T(8,128)S(1)} %get-tuple-element.31), channel_id=1, source_target_pairs={{1,2},{3,0},{2,1},{0,3},{5,6},{7,4},{6,5},{4,7},{9,10},{11,8},{10,... | collective-permute-start | bytes 417800 | tf_op jit(solution)/shard_map/ppermute | solution.py:532
  12.6 0.5 %collective-permute-start.2 = (f32[16,128]{1,0:T(8,128)S(1)}, f32[16,128]{1,0:T(8,128)S(1)}, u32[]{:S(2)}, u32[]{:S(2)}) collective-permute-start(f32[16,128]{1,0:T(8,128)S(1)} %get-tuple-element.32.rest_0_), channel_id=1, source_target_pairs={{0,2},{1,3},{2,0},{3,1},{4,6},{5,7},{6,4},{7,5},{8,10},{9,11},{10,... | collective-permute-start | bytes 24584 | tf_op jit(solution)/shard_map/ppermute | solution.py:536
  13.1 4.0 %collective-permute-done.2.rest_1_ = f32[16,128]{1,0:T(8,128)S(1)} collective-permute-done((f32[16,128]{1,0:T(8,128)S(1)}, f32[16,128]{1,0:T(8,128)S(1)}, u32[]{:S(2)}, u32[]{:S(2)}) %collective-permute-start.2) | collective-permute-done | bytes 8224 | tf_op jit(solution)/shard_map/ppermute | solution.py:536
  17.1 0.0 collective-permute-done.side_a
  17.1 0.0 collective-permute-done.1.side_b
  17.1 0.2 corners.1
  17.3 0.1 collective-permute-start.5
  17.4 1.9 %collective-permute-start.6 = (f32[5,8,256]{2,1,0:T(8,128)S(1)}, f32[5,8,256]{2,1,0:T(8,128)S(1)}, u32[]{:S(2)}, u32[]{:S(2)}) collective-permute-start(f32[5,8,256]{2,1,0:T(8,128)S(1)} %get-tuple-element.39), channel_id=1, source_target_pairs={{4,8},{12,16},{20,24},{28,0},{8,4},{16,12},{24,20},{0,28},{5,9},{1... | collective-permute-start | bytes 122888 | tf_op jit(solution)/shard_map/ppermute | solution.py:541
  19.3 0.0 copy-done.1
  19.3 4.2 %inner.1 = (f32[16,32,256]{2,1,0:T(8,128)}, f32[16,32,256]{2,1,0:T(8,128)}, f32[2,8,128]{2,1,0:T(8,128)S(1)}, f32[16,40,256]{2,1,0:T(8,128)S(1)}, f32[16,40,256]...) custom-call(f32[16,32,256]{2,1,0:T(8,128)S(1)} %copy-done.1, ...), custom_call_target="tpu_custom_call" | custom-call | flops 20000000 | bytes 3000000 | tf_op jit(solution)/shard_map/inner/pallas_call | solution.py:355
  23.5 0.0 collective-permute-done.5.corner_a
  23.5 0.6 %collective-permute-done.6.corner_b = f32[5,8,256]{2,1,0:T(8,128)S(1)} collective-permute-done((f32[5,8,256]{2,1,0:T(8,128)S(1)}, f32[5,8,256]{2,1,0:T(8,128)S(1)}, u32[]{:S(2)}, u32[]{:S(2)}) %collective-permute-start.6) | collective-permute-done | bytes 40992 | tf_op jit(solution)/shard_map/ppermute | solution.py:541
  24.1 0.0 collective-permute-done.3.face_a
  24.1 0.0 collective-permute-done.4.face_b
  24.1 3.7 %rims.1 = (f32[16,32,256]{2,1,0:T(8,128)}, f32[16,32,256]{2,1,0:T(8,128)}, f32[4,8,128]{2,1,0:T(8,128)S(1)}) custom-call(f32[16,32,256]{2,1,0:T(8,128)} %get-tuple-element.34.phase_in, f32[16,32,256]{2,1,0:T(8,128)} %get-tuple-element.35.solute_in, ...), custom_call_target="tpu_custom_call", output_to_operand_aliasing={{0}: (0, {}), {1}: (1, {})} | custom-call | flops 20000000 | bytes 3000000 | tf_op jit(solution)/shard_map/rims/pallas_call | solution.py:479
  27.8 1.6 %collective-permute-start.8 = (f32[4,8,128]{2,1,0:T(8,128)S(1)}, f32[4,8,128]{2,1,0:T(8,128)S(1)}, u32[]{:S(2)}, u32[]{:S(2)}) collective-permute-start(f32[4,8,128]{2,1,0:T(8,128)S(1)} %get-tuple-element.56.mine), channel_id=1, source_target_pairs={{0,2},{1,3},{2,0},{3,1},{4,6},{5,7},{6,4},{7,5},{8,10},{9,11},{10,... | collective-permute-start | bytes 49160 | tf_op jit(solution)/shard_map/ppermute | solution.py:547
  29.4 0.0 collective-permute-start.7
  29.4 2.2 %collective-permute-done.8.chip = f32[4,8,128]{2,1,0:T(8,128)S(1)} collective-permute-done((f32[4,8,128]{2,1,0:T(8,128)S(1)}, f32[4,8,128]{2,1,0:T(8,128)S(1)}, u32[]{:S(2)}, u32[]{:S(2)}) %collective-permute-start.8) | collective-permute-done | bytes 16416 | tf_op jit(solution)/shard_map/ppermute | solution.py:547
  31.6 0.0 collective-permute-start.9
  31.6 0.0 collective-permute-done.7.core
  31.6 1.2 %collective-permute-done.9.far = f32[4,8,128]{2,1,0:T(8,128)S(1)} collective-permute-done((f32[4,8,128]{2,1,0:T(8,128)S(1)}, f32[4,8,128]{2,1,0:T(8,128)S(1)}, u32[]{:S(2)}, u32[]{:S(2)}) %collective-permute-start.9) | collective-permute-done | bytes 16416 | tf_op jit(solution)/shard_map/ppermute | solution.py:549
  32.8 1.1 %owner.1 = f32[4,16,32]{2,1,0:T(8,128)} custom-call(f32[4,8,128]{2,1,0:T(8,128)S(1)} %get-tuple-element.56.mine, f32[4,8,128]{2,1,0:T(8,128)S(1)} %collective-permute-done.7.core, f32[4,8,128]{2,1,0:T(8,128)S(1)} %collective-permute-done.8.chip, f32[4,8,128]{2,1,0:T(8,128)S(1)} %collective-permute-done.9.far), custom_call_target="tpu_custom_call" | custom-call | tf_op jit(solution)/shard_map/owner/pallas_call | solution.py:511
Async XLA Ops:
  0.6 1.0 %copy-start = (f32[16,32,256]{2,1,0:T(8,128)S(1)}, f32[16,32,256]{2,1,0:T(8,128)}, u32[]{:S(2)}) copy-start(f32[16,32,256]{2,1,0:T(8,128)} %phase.3) | copy-start | bytes 1572868
  1.7 1.0 %copy-start.2 = (f32[16,32,256]{2,1,0:T(8,128)S(1)}, f32[16,32,256]{2,1,0:T(8,128)}, u32[]{:S(2)}) copy-start(f32[16,32,256]{2,1,0:T(8,128)} %solute.3) | copy-start | bytes 1572868
  2.7 0.8 %copy-start.3 = (f32[4,32,16]{1,2,0:T(8,128)S(1)}, f32[4,32,16]{1,2,0:T(8,128)}, u32[]{:S(2)}) copy-start(f32[4,32,16]{1,2,0:T(8,128)} %param.5) | copy-start | bytes 24580
  3.5 15.8 %copy-start.1 = (f32[16,32,256]{2,1,0:T(8,128)S(1)}, f32[16,32,256]{2,1,0:T(8,128)}, u32[]{:S(2)}) copy-start(f32[16,32,256]{2,1,0:T(8,128)} %phase.3) | copy-start | bytes 1572868
  4.4 19.7 %collective-permute-start.3 = (f32[2,4,32,256]{3,2,1,0:T(8,128)S(1)}, f32[2,4,32,256]{3,2,1,0:T(8,128)S(1)}, u32[]{:S(2)}, u32[]{:S(2)}) collective-permute-start(f32[2,4,32,256]{3,2,1,0:T(8,128)S(1)} %get-tuple-element.36), channel_id=1, source_target_pairs={{0,4},{8,12},{16,20},{24,28},{4,0},{12,8},{20,16},{28,24},{1,5},{9... | collective-permute-start | bytes 786440 | tf_op jit(solution)/shard_map/ppermute | solution.py:530
  7.4 16.7 %collective-permute-start.4 = (f32[2,4,32,256]{3,2,1,0:T(8,128)S(1)}, f32[2,4,32,256]{3,2,1,0:T(8,128)S(1)}, u32[]{:S(2)}, u32[]{:S(2)}) collective-permute-start(f32[2,4,32,256]{3,2,1,0:T(8,128)S(1)} %get-tuple-element.37), channel_id=1, source_target_pairs={{4,8},{12,16},{20,24},{28,0},{8,4},{16,12},{24,20},{0,28},{5,9},{1... | collective-permute-start | bytes 786440 | tf_op jit(solution)/shard_map/ppermute | solution.py:531
  11.0 6.2 %collective-permute-start = (f32[17,8,256]{2,1,0:T(8,128)S(1)}, f32[17,8,256]{2,1,0:T(8,128)S(1)}, u32[]{:S(2)}, u32[]{:S(2)}) collective-permute-start(f32[17,8,256]{2,1,0:T(8,128)S(1)} %get-tuple-element.30), channel_id=1, source_target_pairs={{0,1},{2,3},{1,0},{3,2},{4,5},{6,7},{5,4},{7,6},{8,9},{10,11},{9,8... | collective-permute-start | bytes 417800 | tf_op jit(solution)/shard_map/ppermute | solution.py:533
  11.0 6.2 %collective-permute-start.1 = (f32[17,8,256]{2,1,0:T(8,128)S(1)}, f32[17,8,256]{2,1,0:T(8,128)S(1)}, u32[]{:S(2)}, u32[]{:S(2)}) collective-permute-start(f32[17,8,256]{2,1,0:T(8,128)S(1)} %get-tuple-element.31), channel_id=1, source_target_pairs={{1,2},{3,0},{2,1},{0,3},{5,6},{7,4},{6,5},{4,7},{9,10},{11,8},{10,... | collective-permute-start | bytes 417800 | tf_op jit(solution)/shard_map/ppermute | solution.py:532
  12.6 4.5 %collective-permute-start.2 = (f32[16,128]{1,0:T(8,128)S(1)}, f32[16,128]{1,0:T(8,128)S(1)}, u32[]{:S(2)}, u32[]{:S(2)}) collective-permute-start(f32[16,128]{1,0:T(8,128)S(1)} %get-tuple-element.32.rest_0_), channel_id=1, source_target_pairs={{0,2},{1,3},{2,0},{3,1},{4,6},{5,7},{6,4},{7,5},{8,10},{9,11},{10,... | collective-permute-start | bytes 24584 | tf_op jit(solution)/shard_map/ppermute | solution.py:536
  17.3 6.2 %collective-permute-start.5 = (f32[5,8,256]{2,1,0:T(8,128)S(1)}, f32[5,8,256]{2,1,0:T(8,128)S(1)}, u32[]{:S(2)}, u32[]{:S(2)}) collective-permute-start(f32[5,8,256]{2,1,0:T(8,128)S(1)} %get-tuple-element.38), channel_id=1, source_target_pairs={{0,4},{8,12},{16,20},{24,28},{4,0},{12,8},{20,16},{28,24},{1,5},{9... | collective-permute-start | bytes 122888 | tf_op jit(solution)/shard_map/ppermute | solution.py:540
  17.4 6.8 %collective-permute-start.6 = (f32[5,8,256]{2,1,0:T(8,128)S(1)}, f32[5,8,256]{2,1,0:T(8,128)S(1)}, u32[]{:S(2)}, u32[]{:S(2)}) collective-permute-start(f32[5,8,256]{2,1,0:T(8,128)S(1)} %get-tuple-element.39), channel_id=1, source_target_pairs={{4,8},{12,16},{20,24},{28,0},{8,4},{16,12},{24,20},{0,28},{5,9},{1... | collective-permute-start | bytes 122888 | tf_op jit(solution)/shard_map/ppermute | solution.py:541
  27.8 3.8 %collective-permute-start.8 = (f32[4,8,128]{2,1,0:T(8,128)S(1)}, f32[4,8,128]{2,1,0:T(8,128)S(1)}, u32[]{:S(2)}, u32[]{:S(2)}) collective-permute-start(f32[4,8,128]{2,1,0:T(8,128)S(1)} %get-tuple-element.56.mine), channel_id=1, source_target_pairs={{0,2},{1,3},{2,0},{3,1},{4,6},{5,7},{6,4},{7,5},{8,10},{9,11},{10,... | collective-permute-start | bytes 49160 | tf_op jit(solution)/shard_map/ppermute | solution.py:547
  29.4 2.3 %collective-permute-start.7 = (f32[4,8,128]{2,1,0:T(8,128)S(1)}, f32[4,8,128]{2,1,0:T(8,128)S(1)}, u32[]{:S(2)}, u32[]{:S(2)}) collective-permute-start(f32[4,8,128]{2,1,0:T(8,128)S(1)} %get-tuple-element.56.mine), channel_id=1, source_target_pairs={{0,1},{2,3},{1,0},{3,2},{4,5},{6,7},{5,4},{7,6},{8,9},{10,11},{9,8... | collective-permute-start | bytes 49160 | tf_op jit(solution)/shard_map/ppermute | solution.py:548
  31.6 1.2 %collective-permute-start.9 = (f32[4,8,128]{2,1,0:T(8,128)S(1)}, f32[4,8,128]{2,1,0:T(8,128)S(1)}, u32[]{:S(2)}, u32[]{:S(2)}) collective-permute-start(f32[4,8,128]{2,1,0:T(8,128)S(1)} %collective-permute-done.8.chip), channel_id=1, source_target_pairs={{0,1},{2,3},{1,0},{3,2},{4,5},{6,7},{5,4},{7,6},{8,9},{10,11},{9,8... | collective-permute-start | bytes 49160 | tf_op jit(solution)/shard_map/ppermute | solution.py:549

commit v3 on v2

v3 whole, which is shorter than its diff:
```python
import functools

import jax
import jax.numpy as jnp
from jax import lax
from jax.experimental import pallas as pl
from jax.experimental.pallas import tpu as pltpu
from jax.sharding import PartitionSpec as P

time_step = 0.1
anisotropy = 0.3
coupling = 2.0
rejection = 0.5

F32 = jnp.float32
HIGHEST = lax.Precision.HIGHEST
HALO = 4
ROWS = 8
LANES = 128
VMEM_LIMIT = 24 * 1024 * 1024


def vmem():
    return pl.BlockSpec(memory_space=pltpu.VMEM)


def anywhere():
    return pl.BlockSpec(memory_space=pl.ANY)


def hbm():
    return pl.BlockSpec(memory_space=pltpu.HBM)


def pairs(count, first):
    forward = [((first + k) % count, (first + k + 1) % count) for k in range(0, count, 2)]
    return forward + [(b, a) for a, b in forward]


def flips(me):
    odd = lax.rem(me, 2)
    return me, me + 1 - 2 * odd, lax.rem(me + 2, 4), 3 - me


def row_ids(shape):
    return lax.broadcasted_iota(jnp.int32, shape, len(shape) - 2)


def lane_ids(shape):
    return lax.broadcasted_iota(jnp.int32, shape, len(shape) - 1)


def start_all(copies, sems):
    copies = [pltpu.make_async_copy(source, target, sems.at[n]) for n, (source, target) in enumerate(copies)]
    for copy in copies:
        copy.start()
    return copies


def wait_all(copies):
    for copy in copies:
        copy.wait()


def fold(table):
    half = table.shape[0] // 2
    return jnp.concatenate([table[:half], table[half:]], axis=1)


def unfold(tile):
    return jnp.concatenate([tile[:, :LANES], tile[:, LANES:]], axis=0)


def pack_kernel(phase, solute, macro, face_a, face_b, side_a, side_b, table, low, high, local, sems):
    size_x, size_y, size_z = phase.shape
    odd_x = lax.rem(lax.axis_index("gx"), 2)
    even_y = lax.rem(lax.axis_index("gy"), 2) == 0
    start_a = (1 - odd_x) * (size_x - HALO)
    start_b = odd_x * (size_x - HALO)
    copies = []
    for field, ref in enumerate((phase, solute)):
        copies.append((ref.at[pl.ds(start_a, HALO)], face_a.at[field]))
        copies.append((ref.at[:, pl.ds(0, ROWS), :], low.at[field]))
        copies.append((ref.at[:, pl.ds(size_y - ROWS, ROWS), :], high.at[field]))
        copies.append((ref.at[pl.ds(start_b, HALO)], face_b.at[field]))
    copies.append((macro, local))
    copies = start_all(copies, sems)
    wait_all(copies)
    wide = jnp.concatenate([local[k] for k in range(local.shape[0])], axis=1)
    table[...] = wide
    top = row_ids((size_x, ROWS, size_z)) < HALO
    low_side = jnp.where(top, low[0], pltpu.roll(low[1], HALO, 1))
    high_side = jnp.where(top, pltpu.roll(high[1], HALO, 1), high[0])
    side_a[pl.ds(0, size_x)] = jnp.where(even_y, high_side, low_side)
    side_b[pl.ds(0, size_x)] = jnp.where(even_y, low_side, high_side)
    if side_a.shape[0] > size_x:
        side_a[size_x] = fold(wide)
        side_b[size_x] = fold(wide)


def pack(phase, solute, macro, ride):
    size_x, size_y, size_z = phase.shape
    coarse_x, coarse_z, coarse_y = macro.shape
    face = jax.ShapeDtypeStruct((2, HALO, size_y, size_z), F32)
    sides = [jax.ShapeDtypeStruct((size_x + extra, ROWS, size_z), F32) for extra in ((1, 2) if ride else (0, 0))]
    table = jax.ShapeDtypeStruct((coarse_z, coarse_x * coarse_y), F32)
    return pl.pallas_call(
        pack_kernel,
        out_shape=(face, face, *sides, table),
        in_specs=[hbm()] * 3,
        out_specs=[vmem()] * 5,
        scratch_shapes=[
            pltpu.VMEM((2, size_x, ROWS, size_z), F32),
            pltpu.VMEM((2, size_x, ROWS, size_z), F32),
            pltpu.VMEM(macro.shape, F32),
            pltpu.SemaphoreType.DMA((9,)),
        ],
        compiler_params=pltpu.CompilerParams(vmem_limit_bytes=VMEM_LIMIT),
        cost_estimate=pl.CostEstimate(flops=10**5, bytes_accessed=2 * 10**6, transcendentals=0),
        name="pack",
    )(phase, solute, macro)


def append_kernel(arrived, side, out):
    out[side.shape[0] - 1] = arrived[arrived.shape[0] - 1]


def append(arrived, side):
    return pl.pallas_call(
        append_kernel,
        out_shape=jax.ShapeDtypeStruct(side.shape, F32),
        in_specs=[vmem(), vmem()],
        out_specs=vmem(),
        input_output_aliases={1: 0},
        compiler_params=pltpu.CompilerParams(vmem_limit_bytes=VMEM_LIMIT),
        cost_estimate=pl.CostEstimate(flops=0, bytes_accessed=10**5, transcendentals=0),
        name="append",
    )(arrived, side)


def corner_kernel(coarse_y, gathered, side_a, side_b, table, coarse, corner_a, corner_b):
    size_x = side_a.shape[0] - (0 if gathered else 1)
    me = lax.axis_index("gy")
    even_x = lax.rem(lax.axis_index("gx"), 2) == 0
    even_y = lax.rem(me, 2) == 0
    block = table[...]
    if not gathered:
        near, across, far = flips(me)[1:]
        depth = table.shape[0]
        tiles = (me, block), (near, unfold(side_a[size_x])), (far, unfold(side_b[size_x])), (across, unfold(side_b[size_x + 1]))
        for source, tile in tiles:
            coarse[pl.ds(pl.multiple_of(source * depth, depth), depth), :] = tile
        block = coarse[...]
    depth, width = block.shape
    flipped = [block[:, at : at + coarse_y] for at in range(width - coarse_y, -1, -coarse_y)]
    block = jnp.where(even_x, block, jnp.concatenate(flipped, axis=1))
    coarse[...] = block
    stack = LANES // coarse_y
    height = depth // stack
    row = row_ids(side_a.shape[1:])
    edges = block[:, width - coarse_y :], block[:, :coarse_y]
    for corner, top_side, edge in ((corner_a, even_x, edges[0]), (corner_b, jnp.logical_not(even_x), edges[1])):
        for n, keep in ((0, 5), (1, 2)):
            def layer(d, n=n):
                at = jnp.where(top_side, size_x - d, d - 1)
                first, second = side_a[at], side_b[at]
                return jnp.where(even_y, second, first) if n == 0 else jnp.where(even_y, first, second)

            corner[2 * n] = layer(1)
            corner[2 * n + 1] = jnp.where(row == keep, pltpu.roll(layer(3), 6 if n == 0 else 2, 0), layer(2))
        edge = jnp.concatenate([edge[q * height : (q + 1) * height] for q in range(stack)], axis=1)
        corner[pl.ds(4, height // 16)] = fold(edge).reshape(height // 16, ROWS, 2 * LANES)


def corners(side_a, side_b, table, coarse_y, coarse_shape):
    size_z = side_a.shape[2]
    height = coarse_shape[0] * coarse_y // LANES
    corner = jax.ShapeDtypeStruct((4 + height // 16, ROWS, size_z), F32)
    coarse = jax.ShapeDtypeStruct(coarse_shape, F32)
    return pl.pallas_call(
        functools.partial(corner_kernel, coarse_y, table.shape == coarse_shape),
        out_shape=(coarse, corner, corner),
        in_specs=[vmem()] * 3,
        out_specs=[vmem()] * 3,
        compiler_params=pltpu.CompilerParams(vmem_limit_bytes=VMEM_LIMIT),
        cost_estimate=pl.CostEstimate(flops=10**5, bytes_accessed=4 * 10**5, transcendentals=0),
        name="corners",
    )(side_a, side_b, table)


def weights(lower, frac, shape, tick):
    first, second = lower
    return jnp.where(tick == first, 1.0 - frac, 0.0) + jnp.where(tick == second, frac, 0.0)


def interpolate(block, coarse_y, size_y, size_z):
    depth, width = block.shape
    rows = size_y + 2 * HALO
    shape = (depth, size_z)
    fine = lane_ids(shape)
    lower = (2 * fine + 5) // 8 - 1
    frac = (2 * fine - 3 - 8 * lower).astype(F32) / 8.0
    ends = jnp.clip(lower, 0, depth - 1), jnp.clip(lower + 1, 0, depth - 1)
    along_z = weights(ends, frac, shape, row_ids(shape))
    deep = lax.dot_general(block, along_z, (((0,), (0,)), ((), ())), precision=HIGHEST, preferred_element_type=F32)
    shape = (rows, coarse_y)
    fine = row_ids(shape)
    fine = jnp.where(fine >= size_y + HALO, fine - rows, fine)
    local = (2 * fine + 13) // 8 - 2
    frac = (2 * fine - 3 - 8 * local).astype(F32) / 8.0
    lower = local + lax.axis_index("gy") * (size_y // 4) + coarse_y
    ends = lax.rem(lower, coarse_y), lax.rem(lower + 1, coarse_y)
    along_y = weights(ends, frac, shape, lane_ids(shape))
    return [
        jnp.dot(along_y, deep[k * coarse_y : (k + 1) * coarse_y], precision=HIGHEST, preferred_element_type=F32)
        for k in range(width // coarse_y)
    ]


def blend(x, fans):
    lower = (2 * x - 3) // 8
    frac = (2 * x - 3 - 8 * lower) / 8.0
    return (1.0 - frac) * fans[lower] + frac * fans[lower + 1]


def turn(value, by, axis):
    return pltpu.roll(value, by % value.shape[axis], axis)


def z_matrices(size_z):
    shape = (size_z, size_z)
    source, target = row_ids(shape), lane_ids(shape)
    hit = lambda at: (source == at).astype(F32)
    end = size_z - 1
    gradient = hit(jnp.minimum(target + 1, end)) - hit(jnp.maximum(target - 1, 0))
    difference = hit(target + 1) - hit(target - 1)
    laplace = hit(jnp.minimum(target + 2, end)) + hit(jnp.maximum(target - 2, 0)) - 6.0 * hit(target)
    return tuple(m.astype(jnp.bfloat16) for m in (gradient, difference, laplace))


def matrix_kernel(size_z, tile, out):
    for n, matrix in enumerate(z_matrices(size_z)):
        out[n] = matrix


def z_products(size_z, tile):
    return pl.pallas_call(
        functools.partial(matrix_kernel, size_z),
        out_shape=jax.ShapeDtypeStruct((3, size_z, size_z), jnp.bfloat16),
        in_specs=[anywhere()],
        out_specs=vmem(),
        compiler_params=pltpu.CompilerParams(vmem_limit_bytes=VMEM_LIMIT),
        cost_estimate=pl.CostEstimate(flops=10**6, bytes_accessed=4 * 10**5, transcendentals=0),
        name="products",
    )(tile)


def along(slabs, matrix):
    value = slabs.reshape(-1, slabs.shape[-1])
    coarse = value.astype(jnp.bfloat16)
    rest = (value - coarse.astype(F32)).astype(jnp.bfloat16)
    product = jnp.dot(coarse, matrix, preferred_element_type=F32) + jnp.dot(rest, matrix, preferred_element_type=F32)
    return product.reshape(slabs.shape)


def flux(before, here, after, along_z):
    along_x = after - before
    along_y = turn(here, -1, 0) - turn(here, 1, 0)
    sq_x = along_x * along_x
    sq_y = along_y * along_y
    both = sq_x + sq_y
    inverse = 1.0 / (both + 4.0)
    factor = 1.0 + anisotropy * (both * both - 8.0 * (sq_x * sq_y)) * (inverse * inverse)
    stiff = (0.25 * time_step) * (factor * factor)
    return stiff * along_x, stiff * along_y, stiff * along_z


def spread(flux_y):
    return turn(flux_y, -1, 0) - turn(flux_y, 1, 0)


def phase_change(here, conc, theta, divergence):
    square = 1.0 - here * here
    drive = square * (here - (coupling * square) * (theta + conc))
    return divergence + time_step * drive


def solute_step(conc, beyond_x, beyond_y, along_z, change):
    return conc + (0.25 * time_step) * (beyond_x + beyond_y + along_z) + rejection * change


def next_row(conc):
    return turn(conc, -2, 0) + turn(conc, 2, 0)


def pools(size_y, size_z):
    pool_y = (row_ids((size_y // 4, size_y)) == lane_ids((size_y // 4, size_y)) // 4).astype(F32)
    pool_z = (row_ids((size_z, LANES)) // 4 == lane_ids((size_z, LANES))).astype(F32)
    return pool_y, pool_z


def restrict(change, pool):
    pool_y, pool_z = pool
    change = jnp.dot(change, pool_z, precision=HIGHEST, preferred_element_type=F32)
    return (0.5 / 64.0) * jnp.dot(pool_y, change, precision=HIGHEST, preferred_element_type=F32)


KEPT = ("p0", "c0", "dz0", "cz0", "gx0", "dv0", "p1", "c1", "dz1", "cz1", "gx1", "dv1", "th")


def spans(size_x):
    widths = dict(p0=0, c0=0, dz0=0, cz0=0, gx0=1, dv0=1, p1=2, c1=2, dz1=2, cz1=2, gx1=3, dv1=3, th=2)
    return {name: (widths[name], size_x - widths[name]) for name in KEPT}


def halo_rows(tile, top):
    zero = jnp.zeros_like(tile[0])
    low = tile[0], tile[1], pltpu.roll(tile[1], 2, 0), zero
    high = tile[2], tile[3], pltpu.roll(tile[3], 6, 0), zero
    return [
        (jnp.where(top, h, l), pltpu.roll(jnp.where(top, l, h), HALO, 0)) for l, h in zip(low, high)
    ]


def edge_block(tiles, coarse_y):
    edge = unfold(tiles.reshape(-1, 2 * LANES))
    return jnp.concatenate([edge[:, at : at + coarse_y] for at in range(0, LANES, coarse_y)], axis=0)


def inner_kernel(coarse_y, phase, solute, side_a, side_b, coarse, matrices, phase_out, solute_out, latent, *rest):
    kept = dict(zip(KEPT, rest[: len(KEPT)]))
    fz, phase_new, solute_new, out_sems = rest[len(KEPT) :]
    size_x, size_y, size_z = phase.shape
    span = spans(size_x)
    odd_x = lax.rem(lax.axis_index("gx"), 2)
    even_y = lax.rem(lax.axis_index("gy"), 2) == 0
    at = lambda name, u: kept[name].at[u - span[name][0]]
    get = lambda name, u: kept[name][u - span[name][0]]
    place = lambda u: u + odd_x * (size_x - 1 - 2 * u)
    top = row_ids((ROWS, size_z)) < HALO
    for u in range(size_x):
        first, second = side_a[place(u)], side_b[place(u)]
        low, high = jnp.where(even_y, second, first), jnp.where(even_y, first, second)
        at("p0", u)[pl.ds(0, size_y), :] = phase[place(u)]
        at("c0", u)[pl.ds(0, size_y), :] = solute[place(u)]
        at("p0", u)[pl.ds(size_y, ROWS), :] = jnp.where(top, high, low)
        at("c0", u)[pl.ds(size_y, ROWS), :] = pltpu.roll(jnp.where(top, low, high), HALO, 0)
    fans = dict(enumerate(interpolate(coarse[...], coarse_y, size_y, size_z)))
    for u in range(*span["th"]):
        at("th", u)[...] = blend(u, fans)

    for step in "01":
        p, c, dz, cz, gx, dv = (name + step for name in ("p", "c", "dz", "cz", "gx", "dv"))
        kept[dz][...] = along(kept[p][...], matrices[0])
        kept[cz][...] = along(kept[c][...], matrices[2])
        begin, end = span[gx]
        for u in range(begin, end):
            flux_x, flux_y, flux_z = flux(get(p, u - 1), get(p, u), get(p, u + 1), get(dz, u))
            at(gx, u)[...] = flux_x
            at(dv, u)[...] = spread(flux_y)
            fz[u - begin] = flux_z
        kept[dv][...] += along(fz[pl.ds(0, end - begin)], matrices[1])
        take = (lambda v: v) if step == "0" else (lambda v: v[:size_y])
        for u in range(begin + 1, end - 1):
            here, conc = take(get(p, u)), get(c, u)
            divergence = take(get(gx, u + 1)) - take(get(gx, u - 1)) + take(get(dv, u))
            change = phase_change(here, take(conc), take(get("th", u)), divergence)
            beyond = take(get(c, u + 2)) + take(get(c, u - 2))
            new_conc = solute_step(take(conc), beyond, take(next_row(conc)), take(get(cz, u)), change)
            if step == "0":
                at("p1", u)[...] = here + change
                at("c1", u)[...] = new_conc
            else:
                phase_new[place(u) - HALO] = here + change
                solute_new[place(u) - HALO] = new_conc
    middle = pl.ds(HALO, size_x - 2 * HALO)
    copies = start_all([(phase_new, phase_out.at[middle]), (solute_new, solute_out.at[middle])], out_sems)
    pool = pools(size_y, size_z)
    for k in range(1, size_x // 4 - 1):
        change = jnp.zeros((size_y, size_z), F32)
        for u in range(4 * k, 4 * k + 4):
            change = change + (phase_new[place(u) - HALO] - get("p0", u)[:size_y])
        latent[k - 1] = restrict(change, pool)
    wait_all(copies)


def inner(phase, solute, side_a, side_b, coarse, matrices, coarse_y):
    size_x, size_y, size_z = phase.shape
    rows = size_y + 2 * HALO
    out = jax.ShapeDtypeStruct(phase.shape, F32)
    kept = [jax.ShapeDtypeStruct((end - begin, rows, size_z), F32) for begin, end in spans(size_x).values()]
    latent = jax.ShapeDtypeStruct((size_x // 4 - 2, size_y // 4, LANES), F32)
    part = pltpu.VMEM((size_x - 2 * HALO, size_y, size_z), F32)
    return pl.pallas_call(
        functools.partial(inner_kernel, coarse_y),
        out_shape=(out, out, latent, *kept),
        in_specs=[vmem()] * 6,
        out_specs=[hbm(), hbm()] + [vmem()] * (1 + len(kept)),
        scratch_shapes=[pltpu.VMEM((size_x - 2, rows, size_z), F32), part, part, pltpu.SemaphoreType.DMA((2,))],
        compiler_params=pltpu.CompilerParams(vmem_limit_bytes=VMEM_LIMIT),
        cost_estimate=pl.CostEstimate(flops=10**8, bytes_accessed=10**6, transcendentals=0),
        name="inner",
    )(phase, solute, side_a, side_b, coarse, matrices)


def rim_steps(coarse_y, near, size_x, face, corner, coarse, matrices, kept, scratch, phase_new, solute_new):
    hp0, hc0, p1, c1, gx, dv, dz, cz, fz, th = scratch
    _, size_y, size_z = phase_new.shape
    span = spans(size_x)
    odd_x = lax.rem(lax.axis_index("gx"), 2)
    flip = odd_x if near else 1 - odd_x
    top = row_ids((ROWS, size_z)) < HALO
    for d, (p_rows, c_rows) in enumerate(halo_rows(corner, top)):
        layer = d + flip * (HALO - 1 - 2 * d)
        for n, (field, rows) in enumerate(((hp0, p_rows), (hc0, c_rows))):
            field[HALO - 1 - d, pl.ds(0, size_y), :] = face[n, layer]
            field[HALO - 1 - d, pl.ds(size_y, ROWS), :] = rows
    own = coarse[:, coarse.shape[1] - coarse_y :] if near else coarse[:, :coarse_y]
    block = jnp.concatenate([edge_block(corner[4:], coarse_y), own], axis=1)
    fans = dict(enumerate(interpolate(block, coarse_y, size_y, size_z), -1))
    for v in range(-2, 2):
        th[v + 2] = blend(v, fans)

    def get(name, v):
        begin, end = span[name]
        if v >= begin:
            found = kept[name][(size_x - 1 - v if near else v) - begin]
            return -found if near and name.startswith("gx") else found
        own, first = dict(
            p0=(hp0, -4), c0=(hc0, -4), dz0=(dz, -3), cz0=(cz, -2), gx0=(gx, -3), dv0=(dv, -2),
            p1=(p1, -2), c1=(c1, -2), dz1=(dz, -1), cz1=(cz, 0), gx1=(gx, -1), dv1=(dv, 0), th=(th, -2),
        )[name]
        return own[v - first]

    for step, begin in (("0", -3), ("1", -1)):
        p, c, gx_, dv_, dz_, cz_ = (name + step for name in ("p", "c", "gx", "dv", "dz", "cz"))
        fields = (hp0[pl.ds(1, 3)], hc0[pl.ds(2, 2)]) if step == "0" else (p1[pl.ds(1, 3)], c1[pl.ds(2, 2)])
        dz[...] = along(fields[0], matrices[0])
        cz[...] = along(fields[1], matrices[2])
        for v in range(begin, begin + 4):
            flux_x, flux_y, flux_z = flux(get(p, v - 1), get(p, v), get(p, v + 1), get(dz_, v))
            gx[v - begin] = flux_x
            if v > begin:
                dv[v - begin - 1] = spread(flux_y)
                fz[v - begin - 1] = flux_z
        dv[...] += along(fz[...], matrices[1])
        take = (lambda w: w) if step == "0" else (lambda w: w[:size_y])
        for v in range(begin + 1, begin + 5):
            here, conc = take(get(p, v)), get(c, v)
            divergence = take(get(gx_, v + 1)) - take(get(gx_, v - 1)) + take(get(dv_, v))
            change = phase_change(here, take(conc), take(get("th", v)), divergence)
            beyond = take(get(c, v + 2)) + take(get(c, v - 2))
            new_conc = solute_step(take(conc), beyond, take(next_row(conc)), take(get(cz_, v)), change)
            new = (p1, c1) if step == "0" else (phase_new, solute_new)
            new[0][v - begin - 1] = here + change
            new[1][v - begin - 1] = new_conc
    change = jnp.zeros((size_y, size_z), F32)
    for v in range(HALO):
        change = change + (phase_new[v] - get("p0", v)[:size_y])
    return restrict(change, pools(size_y, size_z))


def near_kernel(coarse_y, size_x, face, corner, coarse, matrices, *rest):
    kept = dict(zip(KEPT, rest[: len(KEPT)]))
    phase_new, solute_new, latent = rest[len(KEPT) : len(KEPT) + 3]
    latent[...] = rim_steps(
        coarse_y, True, size_x, face, corner, coarse, matrices, kept, rest[len(KEPT) + 3 :], phase_new, solute_new
    )


def far_kernel(
    coarse_y, phase_in, solute_in, face, corner, coarse, matrices, inner_latent, near_latent, near_phase, near_solute,
    *rest
):
    kept = dict(zip(KEPT, rest[: len(KEPT)]))
    phase_out, solute_out, latent = rest[len(KEPT) : len(KEPT) + 3]
    *scratch, phase_new, solute_new, sems = rest[len(KEPT) + 3 :]
    size_x = phase_out.shape[0]
    last = size_x // 4 - 1
    odd_x = lax.rem(lax.axis_index("gx"), 2)
    place = lambda u: u + odd_x * (size_x - 1 - 2 * u)
    copies = []
    for v in range(HALO):
        copies.append((near_phase.at[v], phase_out.at[place(size_x - 1 - v)]))
        copies.append((near_solute.at[v], solute_out.at[place(size_x - 1 - v)]))
    copies = start_all(copies, sems)
    total = rim_steps(coarse_y, False, size_x, face, corner, coarse, matrices, kept, scratch, phase_new, solute_new)
    more = []
    for v in range(HALO):
        more.append((phase_new.at[v], phase_out.at[place(v)]))
        more.append((solute_new.at[v], solute_out.at[place(v)]))
    more = start_all(more, sems.at[pl.ds(2 * HALO, 2 * HALO)])
    for k in range(last + 1):
        source = total if k == 0 else near_latent[...] if k == last else inner_latent[k - 1]
        latent[k + odd_x * (last - 2 * k)] = source
    wait_all(copies)
    wait_all(more)


def rim_scratch(size_y, size_z):
    counts = 4, 4, 4, 4, 4, 3, 3, 2, 3, 4
    return [pltpu.VMEM((count, size_y + 2 * HALO, size_z), F32) for count in counts]


def near_rim(shape, face, corner, coarse, matrices, kept, coarse_y):
    size_x, size_y, size_z = shape
    part = jax.ShapeDtypeStruct((HALO, size_y, size_z), F32)
    return pl.pallas_call(
        functools.partial(near_kernel, coarse_y, size_x),
        out_shape=(part, part, jax.ShapeDtypeStruct((size_y // 4, LANES), F32)),
        in_specs=[vmem()] * (4 + len(kept)),
        out_specs=[vmem()] * 3,
        scratch_shapes=rim_scratch(size_y, size_z),
        compiler_params=pltpu.CompilerParams(vmem_limit_bytes=VMEM_LIMIT),
        cost_estimate=pl.CostEstimate(flops=10**9, bytes_accessed=10**7, transcendentals=0),
        name="near",
    )(face, corner, coarse, matrices, *kept)


def far_rim(phase, solute, face, corner, coarse, matrices, inner_latent, near, kept, coarse_y):
    size_x, size_y, size_z = phase.shape
    out = jax.ShapeDtypeStruct(phase.shape, F32)
    near_phase, near_solute, near_latent = near
    part = pltpu.VMEM((HALO, size_y, size_z), F32)
    return pl.pallas_call(
        functools.partial(far_kernel, coarse_y),
        out_shape=(out, out, jax.ShapeDtypeStruct((size_x // 4, size_y // 4, LANES), F32)),
        in_specs=[hbm(), hbm()] + [vmem()] * (8 + len(kept)),
        out_specs=[hbm(), hbm(), vmem()],
        scratch_shapes=[*rim_scratch(size_y, size_z), part, part, pltpu.SemaphoreType.DMA((4 * HALO,))],
        input_output_aliases={0: 0, 1: 1},
        compiler_params=pltpu.CompilerParams(vmem_limit_bytes=VMEM_LIMIT),
        cost_estimate=pl.CostEstimate(flops=10**7, bytes_accessed=3 * 10**6, transcendentals=0),
        name="far",
    )(phase, solute, face, corner, coarse, matrices, inner_latent, near_latent, near_phase, near_solute, *kept)


def owner_kernel(coarse_z, mine, core, chip, far, out):
    me = lax.axis_index("gy")
    coarse_x, per, _ = mine.shape
    lane = lane_ids((coarse_x, coarse_z, coarse_x * per))
    total = jnp.zeros(lane.shape, F32)
    shift = lax.rem(LANES - me * coarse_z, LANES)
    for source, ref in zip(flips(me), (mine, core, chip, far)):
        block = jnp.stack([pltpu.roll(ref[k], shift, 1)[:, :coarse_z] for k in range(coarse_x)])
        block = jnp.swapaxes(block, 1, 2)
        block = jnp.concatenate([block] * 4, axis=2)
        total = jnp.where((lane >= source * per) & (lane < (source + 1) * per), block, total)
    out[...] = total


def owner(parts, coarse_y, coarse_z):
    coarse_x = parts[0].shape[0]
    return pl.pallas_call(
        functools.partial(owner_kernel, coarse_z),
        out_shape=jax.ShapeDtypeStruct((coarse_x, coarse_z, coarse_y), F32),
        in_specs=[vmem()] * 4,
        out_specs=vmem(),
        compiler_params=pltpu.CompilerParams(vmem_limit_bytes=VMEM_LIMIT),
        name="owner",
    )(*parts)


def body(phase, solute, macro_temp):
    count_x, count_y = lax.axis_size("gx"), lax.axis_size("gy")
    coarse_x, coarse_y, coarse_z = macro_temp.shape
    near_x, far_x = pairs(count_x, 0), pairs(count_x, 1)
    near_y, far_y = pairs(count_y, 0), pairs(count_y, 1)
    across = [(k, (k + count_y // 2) % count_y) for k in range(count_y)]
    ride = count_y == 4
    macro = jnp.swapaxes(macro_temp, 1, 2)
    still = [pltpu.with_memory_space_constraint(v, pltpu.HBM) for v in (phase, solute, macro)]
    face_a, face_b, side_a, side_b, table = pack(*still, ride)
    coarse_shape = (coarse_z * count_y, coarse_x * coarse_y)
    face_a = lax.ppermute(face_a, "gx", near_x)
    side_a = lax.ppermute(side_a, "gy", near_y)
    if ride:
        side_b = append(side_a, side_b)
    else:
        table = lax.all_gather(table, "gy").reshape(coarse_shape)
    matrices = z_products(phase.shape[2], side_b)
    face_b, matrices = lax.optimization_barrier((face_b, matrices))
    side_b = lax.ppermute(side_b, "gy", far_y)
    face_b = lax.ppermute(face_b, "gx", far_x)
    coarse, corner_a, corner_b = corners(side_a, side_b, table, coarse_y, coarse_shape)
    corner_a = lax.ppermute(corner_a, "gx", near_x)
    corner_b = lax.ppermute(corner_b, "gx", far_x)
    phase_out, solute_out, inner_latent, *kept = inner(phase, solute, side_a, side_b, coarse, matrices, coarse_y)
    near = near_rim(phase.shape, face_a, corner_a, coarse, matrices, kept, coarse_y)
    phase_out, solute_out, latent = far_rim(
        phase_out, solute_out, face_b, corner_b, coarse, matrices, inner_latent, near, kept, coarse_y
    )
    if ride:
        chip = lax.ppermute(latent, "gy", across)
        core = lax.ppermute(latent, "gy", near_y)
        latent = owner((latent, core, chip, lax.ppermute(chip, "gy", near_y)), coarse_y, coarse_z)
        latent = jnp.swapaxes(latent, 1, 2)
    else:
        split = latent[:, :, : coarse_z * count_y].reshape(coarse_x, latent.shape[1], count_y, coarse_z)
        latent = lax.all_to_all(split, "gy", split_axis=2, concat_axis=1, tiled=True)
        latent = latent.reshape(coarse_x, coarse_y, coarse_z)
    return phase_out, solute_out, latent


def solution(mesh):
    in_specs = (P("gx", "gy", None), P("gx", "gy", None), P("gx", None, "gy"))
    out_specs = (P("gx", "gy", None), P("gx", "gy", None), P("gx", None, "gy"))
    return jax.shard_map(body, mesh=mesh, in_specs=in_specs, out_specs=out_specs, check_vma=False)
```

time: 34.2 us -> 29.8 us (0.87)
  waiting for transfers between devices: 8.09 us -> 3.55 us
  starting transfers between devices: 12.2 us -> 15.4 us
  local copies, waits for them, and re-layouts: 2.84 us -> 0.01 us
    ppermute x1 -> x0, waiting for transfers between devices: 4.01 us -> none  [body(): tables = (table, lax.ppermute(table, 'gy', across))]
    unnamed x8 -> x4, local copies, waits for them, and re-layouts: 2.84 us -> 0.01 us
    ppermute x1, starting transfers between devices: 1.9 us -> 3.84 us  [body(): corner_b = lax.ppermute(corner_b, 'gx', far_x)]
    ppermute x1, starting transfers between devices: 0.07 us -> 1.24 us  [body(): corner_a = lax.ppermute(corner_a, 'gx', near_x)]
    ppermute x1, starting transfers between devices: 3.54 us -> 4.31 us  [body(): face_b = lax.ppermute(face_b, 'gx', far_x)]
    ppermute x1, waiting for transfers between devices: 0.65 us -> 0.01 us  [body(): corner_b = lax.ppermute(corner_b, 'gx', far_x)]
    pallas_call x1, Pallas kernels: 4.2 us -> 3.56 us  [inner(): pl.pallas_call(functools.partial(inner_kernel, coarse_y), out_shape=(out,...]
    pallas_call x3 -> x6, Pallas kernels: 4.73 us -> 5.32 us  [the longest x1 2.09 us: far_rim(): pl.pallas_call(functools.partial(far_kernel, coarse_y), out_shape=(out, o...]
  transfers between devices with their start and end apart: 10 -> 9, of which waited for: 4 -> 3; matrix products, arithmetic and copies ran while one was open for 0% -> 0% of each run, Pallas kernels for 13% -> 18%
where the time goes in v3:
time: 29.8 us; the launch traced here: 29.6 us
  starting transfers between devices  15.4 us (52%)
  Pallas kernels  10 us (34%)
  waiting for transfers between devices  3.55 us (12%)
  between operations  0.69 us (2%)
    ppermute x1, starting transfers between devices, body(): face_b = lax.ppermute(face_b, 'gx', far_x)  4.31 us
    ppermute x1, starting transfers between devices, body(): corner_b = lax.ppermute(corner_b, 'gx', far_x)  3.84 us
    pallas_call x1, Pallas kernels, inner(): pl.pallas_call(functools.partial(inner_kernel, coarse_y), out_shape=(out,...  3.56 us
    ppermute x1, starting transfers between devices, body(): face_a = lax.ppermute(face_a, 'gx', near_x)  2.59 us
    ppermute x1, waiting for transfers between devices, body(): chip = lax.ppermute(latent, 'gy', across)  2.24 us
    pallas_call x1, Pallas kernels, far_rim(): pl.pallas_call(functools.partial(far_kernel, coarse_y), out_shape=(out, o...  2.09 us
    ppermute x1, starting transfers between devices, body(): chip = lax.ppermute(latent, 'gy', across)  1.56 us
    pallas_call x1, Pallas kernels, pack(): pl.pallas_call(pack_kernel, out_shape=(face, face, *sides, table), in_spe...  1.48 us
  transfers between devices with their start and end apart: 9, of which 3 were waited for; matrix products, arithmetic and copies ran while one was open for 0% of the time, Pallas kernels for 18%

profile of v3, /device:TPU:0, one launch (start us, length us, event | category | flops | bytes accessed | tf_op | source)
XLA Modules:
  0.0 29.6 jit_solution(473182415663349349)
XLA Ops:
  0.6 1.5 %pack.1 = (f32[2,4,32,256]{3,2,1,0:T(8,128)S(1)}, f32[2,4,32,256]{3,2,1,0:T(8,128)S(1)}, f32[17,8,256]{2,1,0:T(8,128)S(1)}, f32[18,8,256]{2,1,0:T(8,128)S(1)}, f32[16,128]{1,0:T(8,128)S(1)}) custom-call(f32[16,32,256]{2,1,0:T(8,128)} %phase.3, f32[16,32,256]{2,1,0:T(8,128)} %solute.3, f32[4,16,32]{2,1,0:T(8,128)} %bitcast.2), custom_call_target="tpu_custom_call" | custom-call | flops 100000 | bytes 2000000 | tf_op jit(solution)/shard_map/pack/pallas_call | solution.py:107
  2.1 0.5 %collective-permute-start = (f32[17,8,256]{2,1,0:T(8,128)S(1)}, f32[17,8,256]{2,1,0:T(8,128)S(1)}, u32[]{:S(2)}, u32[]{:S(2)}) collective-permute-start(f32[17,8,256]{2,1,0:T(8,128)S(1)} %get-tuple-element.35), channel_id=1, source_target_pairs={{0,1},{2,3},{1,0},{3,2},{4,5},{6,7},{5,4},{7,6},{8,9},{10,11},{9,8... | collective-permute-start | bytes 417800 | tf_op jit(solution)/shard_map/ppermute | solution.py:576
  2.6 2.6 %collective-permute-start.4 = (f32[2,4,32,256]{3,2,1,0:T(8,128)S(1)}, f32[2,4,32,256]{3,2,1,0:T(8,128)S(1)}, u32[]{:S(2)}, u32[]{:S(2)}) collective-permute-start(f32[2,4,32,256]{3,2,1,0:T(8,128)S(1)} %get-tuple-element.46), channel_id=1, source_target_pairs={{0,4},{8,12},{16,20},{24,28},{4,0},{12,8},{20,16},{28,24},{1,5},{9... | collective-permute-start | bytes 786440 | tf_op jit(solution)/shard_map/ppermute | solution.py:575
  5.2 0.0 collective-permute-done.arrived.side_a
  5.2 0.0 copy-start.1
  5.2 0.0 copy-start
  5.2 1.3 %collective-permute-start.1 = (f32[18,8,256]{2,1,0:T(8,128)S(1)}, f32[18,8,256]{2,1,0:T(8,128)S(1)}, u32[]{:S(2)}, u32[]{:S(2)}) collective-permute-start(f32[18,8,256]{2,1,0:T(8,128)S(1)} %append.1.tile), channel_id=1, source_target_pairs={{1,2},{3,0},{2,1},{0,3},{5,6},{7,4},{6,5},{4,7},{9,10},{11,8},{10,... | collective-permute-start | bytes 442376 | tf_op jit(solution)/shard_map/ppermute | solution.py:583
  6.6 0.1 products.1.matrices
  6.7 4.3 %collective-permute-start.2 = (f32[2,4,32,256]{3,2,1,0:T(8,128)S(1)}, f32[2,4,32,256]{3,2,1,0:T(8,128)S(1)}, u32[]{:S(2)}, u32[]{:S(2)}) collective-permute-start(f32[2,4,32,256]{3,2,1,0:T(8,128)S(1)} %get-tuple-element.43), channel_id=1, source_target_pairs={{4,8},{12,16},{20,24},{28,0},{8,4},{16,12},{24,20},{0,28},{5,9},{1... | collective-permute-start | bytes 786440 | tf_op jit(solution)/shard_map/ppermute | solution.py:584
  11.0 0.1 collective-permute-done.1.side_b
  11.1 0.2 corners.1
  11.3 1.2 %collective-permute-start.5 = (f32[5,8,256]{2,1,0:T(8,128)S(1)}, f32[5,8,256]{2,1,0:T(8,128)S(1)}, u32[]{:S(2)}, u32[]{:S(2)}) collective-permute-start(f32[5,8,256]{2,1,0:T(8,128)S(1)} %get-tuple-element.47), channel_id=1, source_target_pairs={{0,4},{8,12},{16,20},{24,28},{4,0},{12,8},{20,16},{28,24},{1,5},{9... | collective-permute-start | bytes 122888 | tf_op jit(solution)/shard_map/ppermute | solution.py:586
  12.5 3.8 %collective-permute-start.3 = (f32[5,8,256]{2,1,0:T(8,128)S(1)}, f32[5,8,256]{2,1,0:T(8,128)S(1)}, u32[]{:S(2)}, u32[]{:S(2)}) collective-permute-start(f32[5,8,256]{2,1,0:T(8,128)S(1)} %get-tuple-element.44), channel_id=1, source_target_pairs={{4,8},{12,16},{20,24},{28,0},{8,4},{16,12},{24,20},{0,28},{5,9},{1... | collective-permute-start | bytes 122888 | tf_op jit(solution)/shard_map/ppermute | solution.py:587
  16.4 0.0 copy-done.1
  16.4 0.0 copy-done
  16.4 3.6 %inner.1 = (f32[16,32,256]{2,1,0:T(8,128)}, f32[16,32,256]{2,1,0:T(8,128)}, f32[2,8,128]{2,1,0:T(8,128)S(1)}, f32[16,40,256]{2,1,0:T(8,128)S(1)}, f32[16,40,256]...) custom-call(f32[16,32,256]{2,1,0:T(8,128)S(1)} %copy-done, ...), custom_call_target="tpu_custom_call" | custom-call | flops 100000000 | bytes 1000000 | tf_op jit(solution)/shard_map/inner/pallas_call | solution.py:394
  19.9 0.0 collective-permute-done.4.face
  19.9 0.0 collective-permute-done.5.corner
  19.9 1.5 %near.1 = (f32[4,32,256]{2,1,0:T(8,128)S(1)}, f32[4,32,256]{2,1,0:T(8,128)S(1)}, f32[8,128]{1,0:T(8,128)S(1)}) custom-call(f32[2,4,32,256]{3,2,1,0:T(8,128)S(1)} %collective-permute-done.4.face, f32[5,8,256]{2,1,0:T(8,128)S(1)} %collective-permute-done.5.corner, f32[64,128]{1,0:T(8,128)S(1)} %get-tuple-element.38.coarse, ...), custom_call_target="tpu_custom_call" | custom-call | flops 1000000000 | bytes 10000000 | tf_op jit(solution)/shard_map/near/pallas_call | solution.py:508
  21.4 0.0 collective-permute-done.3.corner
  21.4 0.0 collective-permute-done.2.face
  21.4 2.1 %far.1 = (f32[16,32,256]{2,1,0:T(8,128)}, f32[16,32,256]{2,1,0:T(8,128)}, f32[4,8,128]{2,1,0:T(8,128)S(1)}) custom-call(f32[16,32,256]{2,1,0:T(8,128)} %get-tuple-element.41.phase_in, f32[16,32,256]{2,1,0:T(8,128)} %get-tuple-element.42.solute_in, f32[2,4,32,256]{3,2,1,0:T(8,128)S(1)} %collective-permute-done.2.face, ...), custom_call_target="tpu_custom_call", output_to_operand_aliasing={{0}: (0, {}), {1}: (1, {})} | custom-call | flops 10000000 | bytes 3000000 | tf_op jit(solution)/shard_map/far/pallas_call | solution.py:525
  23.5 1.6 %collective-permute-start.7 = (f32[4,8,128]{2,1,0:T(8,128)S(1)}, f32[4,8,128]{2,1,0:T(8,128)S(1)}, u32[]{:S(2)}, u32[]{:S(2)}) collective-permute-start(f32[4,8,128]{2,1,0:T(8,128)S(1)} %get-tuple-element.66.mine), channel_id=1, source_target_pairs={{0,2},{1,3},{2,0},{3,1},{4,6},{5,7},{6,4},{7,5},{8,10},{9,11},{10,... | collective-permute-start | bytes 49160 | tf_op jit(solution)/shard_map/ppermute | solution.py:594
  25.1 0.0 collective-permute-start.6
  25.1 2.2 %collective-permute-done.7.chip = f32[4,8,128]{2,1,0:T(8,128)S(1)} collective-permute-done((f32[4,8,128]{2,1,0:T(8,128)S(1)}, f32[4,8,128]{2,1,0:T(8,128)S(1)}, u32[]{:S(2)}, u32[]{:S(2)}) %collective-permute-start.7) | collective-permute-done | bytes 16416 | tf_op jit(solution)/shard_map/ppermute | solution.py:594
  27.3 0.0 collective-permute-start.8
  27.3 0.0 collective-permute-done.6.core
  27.3 1.2 %collective-permute-done.8.far = f32[4,8,128]{2,1,0:T(8,128)S(1)} collective-permute-done((f32[4,8,128]{2,1,0:T(8,128)S(1)}, f32[4,8,128]{2,1,0:T(8,128)S(1)}, u32[]{:S(2)}, u32[]{:S(2)}) %collective-permute-start.8) | collective-permute-done | bytes 16416 | tf_op jit(solution)/shard_map/ppermute | solution.py:596
  28.5 1.1 %owner.1 = f32[4,16,32]{2,1,0:T(8,128)} custom-call(f32[4,8,128]{2,1,0:T(8,128)S(1)} %get-tuple-element.66.mine, f32[4,8,128]{2,1,0:T(8,128)S(1)} %collective-permute-done.6.core, f32[4,8,128]{2,1,0:T(8,128)S(1)} %collective-permute-done.7.chip, f32[4,8,128]{2,1,0:T(8,128)S(1)} %collective-permute-done.8.far), custom_call_target="tpu_custom_call" | custom-call | tf_op jit(solution)/shard_map/owner/pallas_call | solution.py:554
  (1 shorter events, 0.0 us)
Async XLA Ops:
  2.1 3.1 %collective-permute-start = (f32[17,8,256]{2,1,0:T(8,128)S(1)}, f32[17,8,256]{2,1,0:T(8,128)S(1)}, u32[]{:S(2)}, u32[]{:S(2)}) collective-permute-start(f32[17,8,256]{2,1,0:T(8,128)S(1)} %get-tuple-element.35), channel_id=1, source_target_pairs={{0,1},{2,3},{1,0},{3,2},{4,5},{6,7},{5,4},{7,6},{8,9},{10,11},{9,8... | collective-permute-start | bytes 417800 | tf_op jit(solution)/shard_map/ppermute | solution.py:576
  2.6 17.3 %collective-permute-start.4 = (f32[2,4,32,256]{3,2,1,0:T(8,128)S(1)}, f32[2,4,32,256]{3,2,1,0:T(8,128)S(1)}, u32[]{:S(2)}, u32[]{:S(2)}) collective-permute-start(f32[2,4,32,256]{3,2,1,0:T(8,128)S(1)} %get-tuple-element.46), channel_id=1, source_target_pairs={{0,4},{8,12},{16,20},{24,28},{4,0},{12,8},{20,16},{28,24},{1,5},{9... | collective-permute-start | bytes 786440 | tf_op jit(solution)/shard_map/ppermute | solution.py:575
  5.2 11.1 %copy-start.1 = (f32[16,32,256]{2,1,0:T(8,128)S(1)}, f32[16,32,256]{2,1,0:T(8,128)}, u32[]{:S(2)}) copy-start(f32[16,32,256]{2,1,0:T(8,128)} %solute.3) | copy-start | bytes 1572868
  5.2 11.1 %copy-start = (f32[16,32,256]{2,1,0:T(8,128)S(1)}, f32[16,32,256]{2,1,0:T(8,128)}, u32[]{:S(2)}) copy-start(f32[16,32,256]{2,1,0:T(8,128)} %phase.3) | copy-start | bytes 1572868
  5.2 5.9 %collective-permute-start.1 = (f32[18,8,256]{2,1,0:T(8,128)S(1)}, f32[18,8,256]{2,1,0:T(8,128)S(1)}, u32[]{:S(2)}, u32[]{:S(2)}) collective-permute-start(f32[18,8,256]{2,1,0:T(8,128)S(1)} %append.1.tile), channel_id=1, source_target_pairs={{1,2},{3,0},{2,1},{0,3},{5,6},{7,4},{6,5},{4,7},{9,10},{11,8},{10,... | collective-permute-start | bytes 442376 | tf_op jit(solution)/shard_map/ppermute | solution.py:583
  6.7 14.7 %collective-permute-start.2 = (f32[2,4,32,256]{3,2,1,0:T(8,128)S(1)}, f32[2,4,32,256]{3,2,1,0:T(8,128)S(1)}, u32[]{:S(2)}, u32[]{:S(2)}) collective-permute-start(f32[2,4,32,256]{3,2,1,0:T(8,128)S(1)} %get-tuple-element.43), channel_id=1, source_target_pairs={{4,8},{12,16},{20,24},{28,0},{8,4},{16,12},{24,20},{0,28},{5,9},{1... | collective-permute-start | bytes 786440 | tf_op jit(solution)/shard_map/ppermute | solution.py:584
  11.3 8.7 %collective-permute-start.5 = (f32[5,8,256]{2,1,0:T(8,128)S(1)}, f32[5,8,256]{2,1,0:T(8,128)S(1)}, u32[]{:S(2)}, u32[]{:S(2)}) collective-permute-start(f32[5,8,256]{2,1,0:T(8,128)S(1)} %get-tuple-element.47), channel_id=1, source_target_pairs={{0,4},{8,12},{16,20},{24,28},{4,0},{12,8},{20,16},{28,24},{1,5},{9... | collective-permute-start | bytes 122888 | tf_op jit(solution)/shard_map/ppermute | solution.py:586
  12.5 8.9 %collective-permute-start.3 = (f32[5,8,256]{2,1,0:T(8,128)S(1)}, f32[5,8,256]{2,1,0:T(8,128)S(1)}, u32[]{:S(2)}, u32[]{:S(2)}) collective-permute-start(f32[5,8,256]{2,1,0:T(8,128)S(1)} %get-tuple-element.44), channel_id=1, source_target_pairs={{4,8},{12,16},{20,24},{28,0},{8,4},{16,12},{24,20},{0,28},{5,9},{1... | collective-permute-start | bytes 122888 | tf_op jit(solution)/shard_map/ppermute | solution.py:587
  23.5 3.8 %collective-permute-start.7 = (f32[4,8,128]{2,1,0:T(8,128)S(1)}, f32[4,8,128]{2,1,0:T(8,128)S(1)}, u32[]{:S(2)}, u32[]{:S(2)}) collective-permute-start(f32[4,8,128]{2,1,0:T(8,128)S(1)} %get-tuple-element.66.mine), channel_id=1, source_target_pairs={{0,2},{1,3},{2,0},{3,1},{4,6},{5,7},{6,4},{7,5},{8,10},{9,11},{10,... | collective-permute-start | bytes 49160 | tf_op jit(solution)/shard_map/ppermute | solution.py:594
  25.1 2.3 %collective-permute-start.6 = (f32[4,8,128]{2,1,0:T(8,128)S(1)}, f32[4,8,128]{2,1,0:T(8,128)S(1)}, u32[]{:S(2)}, u32[]{:S(2)}) collective-permute-start(f32[4,8,128]{2,1,0:T(8,128)S(1)} %get-tuple-element.66.mine), channel_id=1, source_target_pairs={{0,1},{2,3},{1,0},{3,2},{4,5},{6,7},{5,4},{7,6},{8,9},{10,11},{9,8... | collective-permute-start | bytes 49160 | tf_op jit(solution)/shard_map/ppermute | solution.py:595
  27.3 1.2 %collective-permute-start.8 = (f32[4,8,128]{2,1,0:T(8,128)S(1)}, f32[4,8,128]{2,1,0:T(8,128)S(1)}, u32[]{:S(2)}, u32[]{:S(2)}) collective-permute-start(f32[4,8,128]{2,1,0:T(8,128)S(1)} %collective-permute-done.7.chip), channel_id=1, source_target_pairs={{0,1},{2,3},{1,0},{3,2},{4,5},{6,7},{5,4},{7,6},{8,9},{10,11},{9,8... | collective-permute-start | bytes 49160 | tf_op jit(solution)/shard_map/ppermute | solution.py:596

commit v4 on v3

v4 whole, which is shorter than its diff:
```python
import functools

import jax
import jax.numpy as jnp
from jax import lax
from jax.experimental import pallas as pl
from jax.experimental.pallas import tpu as pltpu
from jax.sharding import PartitionSpec as P

time_step = 0.1
anisotropy = 0.3
coupling = 2.0
rejection = 0.5

F32 = jnp.float32
HIGHEST = lax.Precision.HIGHEST
HALO = 4
STRIP = 4
ROWS = 8
LANES = 128
VMEM_LIMIT = 24 * 1024 * 1024


def vmem():
    return pl.BlockSpec(memory_space=pltpu.VMEM)


def anywhere():
    return pl.BlockSpec(memory_space=pl.ANY)


def hbm():
    return pl.BlockSpec(memory_space=pltpu.HBM)


def pairs(count, first):
    forward = [((first + k) % count, (first + k + 1) % count) for k in range(0, count, 2)]
    return forward + [(b, a) for a, b in forward]


def flips(me):
    odd = lax.rem(me, 2)
    return me, me + 1 - 2 * odd, lax.rem(me + 2, 4), 3 - me


def row_ids(shape):
    return lax.broadcasted_iota(jnp.int32, shape, len(shape) - 2)


def lane_ids(shape):
    return lax.broadcasted_iota(jnp.int32, shape, len(shape) - 1)


def start_all(copies, sems):
    copies = [pltpu.make_async_copy(source, target, sems.at[n]) for n, (source, target) in enumerate(copies)]
    for copy in copies:
        copy.start()
    return copies


def wait_all(copies):
    for copy in copies:
        copy.wait()


def fold(table):
    half = table.shape[0] // 2
    return jnp.concatenate([table[:half], table[half:]], axis=1)


def unfold(tile):
    return jnp.concatenate([tile[:, :LANES], tile[:, LANES:]], axis=0)


def pack_kernel(
    phase, solute, macro, phase_here, solute_here, face_a, face_b, side_a, strip_b, rest_b, table, local, sems
):
    size_x, size_y, size_z = phase.shape
    odd_x = lax.rem(lax.axis_index("gx"), 2)
    even_y = lax.rem(lax.axis_index("gy"), 2) == 0
    copies = []
    for at in range(0, size_x, HALO):
        for ref, here in ((phase, phase_here), (solute, solute_here)):
            copies.append((ref.at[pl.ds(at, HALO)], here.at[pl.ds(at, HALO)]))
    copies.append((macro, local))
    copies = start_all(copies, sems)
    wait_all(copies)
    for field, here in enumerate((phase_here, solute_here)):
        face_a[field] = here[pl.ds((1 - odd_x) * (size_x - HALO), HALO)]
        face_b[field] = here[pl.ds(odd_x * (size_x - HALO), HALO)]
    low = [here[:, pl.ds(0, ROWS), :] for here in (phase_here, solute_here)]
    high = [here[:, pl.ds(size_y - ROWS, ROWS), :] for here in (phase_here, solute_here)]
    wide = jnp.concatenate([local[k] for k in range(local.shape[0])], axis=1)
    table[...] = wide
    top = row_ids((size_x, ROWS, size_z)) < HALO
    low_side = jnp.where(top, low[0], pltpu.roll(low[1], HALO, 1))
    high_side = jnp.where(top, pltpu.roll(high[1], HALO, 1), high[0])
    side_a[pl.ds(0, size_x)] = jnp.where(even_y, high_side, low_side)
    side_b = jnp.where(even_y, low_side, high_side)
    strip_b[pl.ds(0, STRIP)] = side_b[:STRIP]
    strip_b[pl.ds(STRIP, STRIP)] = side_b[size_x - STRIP :]
    rest_b[...] = side_b[STRIP : size_x - STRIP]
    if side_a.shape[0] > size_x:
        side_a[size_x] = fold(wide)
        strip_b[2 * STRIP] = fold(wide)


def pack(phase, solute, macro, ride):
    size_x, size_y, size_z = phase.shape
    coarse_x, coarse_z, coarse_y = macro.shape
    field = jax.ShapeDtypeStruct(phase.shape, F32)
    face = jax.ShapeDtypeStruct((2, HALO, size_y, size_z), F32)
    counts = (size_x, 2 * STRIP, size_x - 2 * STRIP)
    extra = (1, 2, 0) if ride else (0, 0, 0)
    sides = [jax.ShapeDtypeStruct((count + more, ROWS, size_z), F32) for count, more in zip(counts, extra)]
    table = jax.ShapeDtypeStruct((coarse_z, coarse_x * coarse_y), F32)
    return pl.pallas_call(
        pack_kernel,
        out_shape=(field, field, face, face, *sides, table),
        in_specs=[hbm()] * 3,
        out_specs=[vmem()] * 8,
        scratch_shapes=[pltpu.VMEM(macro.shape, F32), pltpu.SemaphoreType.DMA((1 + 2 * (size_x // HALO),))],
        compiler_params=pltpu.CompilerParams(vmem_limit_bytes=VMEM_LIMIT),
        cost_estimate=pl.CostEstimate(flops=10**5, bytes_accessed=2 * 10**6, transcendentals=0),
        name="pack",
    )(phase, solute, macro)


def append_kernel(arrived, side, out):
    out[side.shape[0] - 1] = arrived[arrived.shape[0] - 1]


def append(arrived, side):
    return pl.pallas_call(
        append_kernel,
        out_shape=jax.ShapeDtypeStruct(side.shape, F32),
        in_specs=[vmem(), vmem()],
        out_specs=vmem(),
        input_output_aliases={1: 0},
        compiler_params=pltpu.CompilerParams(vmem_limit_bytes=VMEM_LIMIT),
        cost_estimate=pl.CostEstimate(flops=0, bytes_accessed=10**5, transcendentals=0),
        name="append",
    )(arrived, side)


def near_rows(block, coarse_y):
    shape = (2 * ROWS, coarse_y)
    wanted = lax.rem(row_ids(shape) + lax.axis_index("gy") * ROWS + coarse_y - 1, coarse_y)
    pick = (lane_ids(shape) == wanted).astype(F32)
    return lax.dot_general(pick, block, (((1,), (1,)), ((), ())), precision=HIGHEST, preferred_element_type=F32)


def pack_edge(rows):
    pieces = rows[:ROWS], pltpu.roll(rows[:ROWS], 4, 0), rows[ROWS:], pltpu.roll(rows[ROWS:], 4, 0)
    return jnp.concatenate(pieces, axis=1)


def unpack_edge(tile):
    quarter = tile.shape[1] // 4
    pieces = [tile[:, at : at + quarter] for at in range(0, tile.shape[1], quarter)]
    top = row_ids(pieces[0].shape) < 4
    halves = [jnp.where(top, pieces[n], pltpu.roll(pieces[n + 1], 4, 0)) for n in (0, 2)]
    return jnp.concatenate(halves, axis=0)


def corner_kernel(coarse_y, gathered, side_a, strip_b, table, coarse, corner_a, corner_b):
    size_x = side_a.shape[0] - (0 if gathered else 1)
    me = lax.axis_index("gy")
    even_x = lax.rem(lax.axis_index("gx"), 2) == 0
    even_y = lax.rem(me, 2) == 0
    block = table[...]
    if not gathered:
        near, across, far = flips(me)[1:]
        depth = table.shape[0]
        tiles = (me, block), (near, unfold(side_a[size_x])), (far, unfold(strip_b[2 * STRIP])), (across, unfold(strip_b[2 * STRIP + 1]))
        for source, tile in tiles:
            coarse[pl.ds(pl.multiple_of(source * depth, depth), depth), :] = tile
        block = coarse[...]
    depth, width = block.shape
    flipped = [block[:, at : at + coarse_y] for at in range(width - coarse_y, -1, -coarse_y)]
    block = jnp.where(even_x, block, jnp.concatenate(flipped, axis=1))
    coarse[...] = block
    row = row_ids(side_a.shape[1:])
    edges = block[:, width - coarse_y :], block[:, :coarse_y]
    for corner, top_side, edge in ((corner_a, even_x, edges[0]), (corner_b, jnp.logical_not(even_x), edges[1])):

        def layer(d, high):
            first = side_a[jnp.where(top_side, size_x - d, d - 1)]
            second = strip_b[jnp.where(top_side, 2 * STRIP - d, d - 1)]
            return jnp.where(even_y, first, second) if high else jnp.where(even_y, second, first)

        spare = pack_edge(near_rows(edge, coarse_y))
        tile = jnp.where(row == 4, pltpu.roll(layer(3, False), 5, 0), layer(1, False))
        corner[0] = jnp.where(row < 2, spare, tile)
        tile = jnp.where(row == 3, pltpu.roll(layer(3, True), 3, 0), layer(1, True))
        corner[1] = jnp.where(row >= 6, pltpu.roll(spare, 4, 0), tile)
        corner[2] = jnp.where(row % 4 < 2, layer(2, True), layer(2, False))


def corners(side_a, strip_b, table, coarse_y, coarse_shape):
    size_z = side_a.shape[2]
    corner = jax.ShapeDtypeStruct((3, ROWS, size_z), F32)
    coarse = jax.ShapeDtypeStruct(coarse_shape, F32)
    return pl.pallas_call(
        functools.partial(corner_kernel, coarse_y, table.shape == coarse_shape),
        out_shape=(coarse, corner, corner),
        in_specs=[vmem()] * 3,
        out_specs=[vmem()] * 3,
        compiler_params=pltpu.CompilerParams(vmem_limit_bytes=VMEM_LIMIT),
        cost_estimate=pl.CostEstimate(flops=10**5, bytes_accessed=4 * 10**5, transcendentals=0),
        name="corners",
    )(side_a, strip_b, table)


def weights(ends, frac, tick):
    first, second = ends
    return jnp.where(tick == first, 1.0 - frac, 0.0) + jnp.where(tick == second, frac, 0.0)


def weights_z(depth, size_z):
    shape = (depth, size_z)
    fine = lane_ids(shape)
    lower = (2 * fine + 5) // 8 - 1
    frac = (2 * fine - 3 - 8 * lower).astype(F32) / 8.0
    ends = jnp.clip(lower, 0, depth - 1), jnp.clip(lower + 1, 0, depth - 1)
    return weights(ends, frac, row_ids(shape))


def interpolate(rows, along_z, size_y):
    deep = jnp.dot(rows, along_z, precision=HIGHEST, preferred_element_type=F32)
    shape = (size_y + 2 * HALO, 2 * ROWS)
    fine = row_ids(shape)
    fine = jnp.where(fine >= size_y + HALO, fine - shape[0], fine)
    lower = (2 * fine + 13) // 8 - 2
    frac = (2 * fine - 3 - 8 * lower).astype(F32) / 8.0
    along_y = weights((lower + 1, lower + 2), frac, lane_ids(shape))
    return [
        jnp.dot(along_y, deep[at : at + 2 * ROWS], precision=HIGHEST, preferred_element_type=F32)
        for at in range(0, rows.shape[0], 2 * ROWS)
    ]


def blend(x, fans):
    lower = (2 * x - 3) // 8
    frac = (2 * x - 3 - 8 * lower) / 8.0
    return (1.0 - frac) * fans[lower] + frac * fans[lower + 1]


def turn(value, by, axis):
    return pltpu.roll(value, by % value.shape[axis], axis)


def z_matrices(size_z):
    shape = (size_z, size_z)
    source, target = row_ids(shape), lane_ids(shape)
    hit = lambda at: (source == at).astype(F32)
    end = size_z - 1
    gradient = hit(jnp.minimum(target + 1, end)) - hit(jnp.maximum(target - 1, 0))
    difference = hit(target + 1) - hit(target - 1)
    laplace = hit(jnp.minimum(target + 2, end)) + hit(jnp.maximum(target - 2, 0)) - 6.0 * hit(target)
    return tuple(m.astype(jnp.bfloat16) for m in (gradient, difference, laplace))


def matrix_kernel(size_z, tile, out, along_z):
    for n, matrix in enumerate(z_matrices(size_z)):
        out[n] = matrix
    along_z[...] = weights_z(*along_z.shape)


def z_products(size_z, tile):
    square = jax.ShapeDtypeStruct((3, size_z, size_z), jnp.bfloat16)
    return pl.pallas_call(
        functools.partial(matrix_kernel, size_z),
        out_shape=(square, jax.ShapeDtypeStruct((size_z // 4, size_z), F32)),
        in_specs=[anywhere()],
        out_specs=[vmem()] * 2,
        compiler_params=pltpu.CompilerParams(vmem_limit_bytes=VMEM_LIMIT),
        cost_estimate=pl.CostEstimate(flops=10**6, bytes_accessed=4 * 10**5, transcendentals=0),
        name="products",
    )(tile)


def along(slabs, matrix):
    value = slabs.reshape(-1, slabs.shape[-1])
    coarse = value.astype(jnp.bfloat16)
    rest = (value - coarse.astype(F32)).astype(jnp.bfloat16)
    product = jnp.dot(coarse, matrix, preferred_element_type=F32) + jnp.dot(rest, matrix, preferred_element_type=F32)
    return product.reshape(slabs.shape)


def flux(before, here, after, along_z):
    along_x = after - before
    along_y = turn(here, -1, 0) - turn(here, 1, 0)
    sq_x = along_x * along_x
    sq_y = along_y * along_y
    both = sq_x + sq_y
    inverse = 1.0 / (both + 4.0)
    factor = 1.0 + anisotropy * (both * both - 8.0 * (sq_x * sq_y)) * (inverse * inverse)
    stiff = (0.25 * time_step) * (factor * factor)
    return stiff * along_x, stiff * along_y, stiff * along_z


def spread(flux_y):
    return turn(flux_y, -1, 0) - turn(flux_y, 1, 0)


def phase_change(here, conc, theta, divergence):
    square = 1.0 - here * here
    drive = square * (here - (coupling * square) * (theta + conc))
    return divergence + time_step * drive


def solute_step(conc, beyond_x, beyond_y, along_z, change):
    return conc + (0.25 * time_step) * (beyond_x + beyond_y + along_z) + rejection * change


def next_row(conc):
    return turn(conc, -2, 0) + turn(conc, 2, 0)


def restrict(change, at, coarse_width):
    size_y, size_z = change.shape
    shape = (size_z // 4, size_z)
    pool_z = (lane_ids(shape) // 4 == row_ids(shape)).astype(F32)
    shape = (size_y, coarse_width)
    pool_y = jnp.where(row_ids(shape) // 4 + at == lane_ids(shape), 0.5 / 64.0, 0.0)
    change = lax.dot_general(
        pool_z, change, (((1,), (1,)), ((), ())), precision=HIGHEST, preferred_element_type=F32
    )
    return jnp.dot(change, pool_y, precision=HIGHEST, preferred_element_type=F32)


def coarse_lane(u, size_x, size_y, coarse_y):
    last = size_x // 4 - 1
    x = u + lax.rem(lax.axis_index("gx"), 2) * (last - 2 * u)
    return x * coarse_y + lax.axis_index("gy") * (size_y // 4)


KEPT = ("p0", "c0", "dz0", "cz0", "gx0", "dv0", "p1", "c1", "dz1", "cz1", "gx1", "dv1", "th")


def spans(size_x):
    widths = dict(p0=0, c0=0, dz0=0, cz0=0, gx0=1, dv0=1, p1=2, c1=2, dz1=2, cz1=2, gx1=3, dv1=3, th=2)
    return {name: (widths[name], size_x - widths[name]) for name in KEPT}


def halo_rows(tile, top):
    zero = jnp.zeros_like(tile[0])
    low = tile[0], tile[2], pltpu.roll(tile[0], 3, 0), zero
    high = tile[1], tile[2], pltpu.roll(tile[1], 5, 0), zero
    return [
        (jnp.where(top, h, l), pltpu.roll(jnp.where(top, l, h), HALO, 0)) for l, h in zip(low, high)
    ]


def inner_kernel(
    coarse_y, phase, solute, side_a, strip_b, rest_b, coarse, matrices, along_z, phase_new, solute_new, latent, ends, *rest
):
    kept = dict(zip(KEPT, rest[: len(KEPT)]))
    (fz,) = rest[len(KEPT) :]
    size_x, size_y, size_z = phase.shape
    span = spans(size_x)
    odd_x = lax.rem(lax.axis_index("gx"), 2)
    even_y = lax.rem(lax.axis_index("gy"), 2) == 0
    at = lambda name, u: kept[name].at[u - span[name][0]]
    get = lambda name, u: kept[name][u - span[name][0]]
    place = lambda u: u + odd_x * (size_x - 1 - 2 * u)
    top = row_ids((ROWS, size_z)) < HALO
    for u in range(size_x):
        first = side_a[place(u)]
        if STRIP <= u < size_x - STRIP:
            second = rest_b[place(u) - STRIP]
        else:
            at_strip = u if u < STRIP else u - size_x + 2 * STRIP
            second = strip_b[at_strip + odd_x * (2 * STRIP - 1 - 2 * at_strip)]
        low, high = jnp.where(even_y, second, first), jnp.where(even_y, first, second)
        at("p0", u)[pl.ds(0, size_y), :] = phase[place(u)]
        at("c0", u)[pl.ds(0, size_y), :] = solute[place(u)]
        at("p0", u)[pl.ds(size_y, ROWS), :] = jnp.where(top, high, low)
        at("c0", u)[pl.ds(size_y, ROWS), :] = pltpu.roll(jnp.where(top, low, high), HALO, 0)
    block = coarse[...]
    block = [near_rows(block[:, at : at + coarse_y], coarse_y) for at in range(0, block.shape[1], coarse_y)]
    fans = dict(enumerate(interpolate(jnp.concatenate(block, axis=0), along_z[...], size_y)))
    ends[0], ends[1] = fans[0], fans[len(fans) - 1]
    for u in range(*span["th"]):
        at("th", u)[...] = blend(u, fans)

    for step in "01":
        p, c, dz, cz, gx, dv = (name + step for name in ("p", "c", "dz", "cz", "gx", "dv"))
        kept[dz][...] = along(kept[p][...], matrices[0])
        kept[cz][...] = along(kept[c][...], matrices[2])
        begin, end = span[gx]
        for u in range(begin, end):
            flux_x, flux_y, flux_z = flux(get(p, u - 1), get(p, u), get(p, u + 1), get(dz, u))
            at(gx, u)[...] = flux_x
            at(dv, u)[...] = spread(flux_y)
            fz[u - begin] = flux_z
        kept[dv][...] += along(fz[pl.ds(0, end - begin)], matrices[1])
        take = (lambda v: v) if step == "0" else (lambda v: v[:size_y])
        for u in range(begin + 1, end - 1):
            here, conc = take(get(p, u)), get(c, u)
            divergence = take(get(gx, u + 1)) - take(get(gx, u - 1)) + take(get(dv, u))
            change = phase_change(here, take(conc), take(get("th", u)), divergence)
            beyond = take(get(c, u + 2)) + take(get(c, u - 2))
            new_conc = solute_step(take(conc), beyond, take(next_row(conc)), take(get(cz, u)), change)
            if step == "0":
                at("p1", u)[...] = here + change
                at("c1", u)[...] = new_conc
            else:
                phase_new[place(u) - HALO] = here + change
                solute_new[place(u) - HALO] = new_conc
    total = jnp.zeros(latent.shape, F32)
    for k in range(1, size_x // 4 - 1):
        change = jnp.zeros((size_y, size_z), F32)
        for u in range(4 * k, 4 * k + 4):
            change = change + (phase_new[place(u) - HALO] - get("p0", u)[:size_y])
        total = total + restrict(change, coarse_lane(k, size_x, size_y, coarse_y), latent.shape[1])
    latent[...] = total


def inner(phase, solute, side_a, strip_b, rest_b, coarse, matrices, along_z, coarse_y):
    size_x, size_y, size_z = phase.shape
    rows = size_y + 2 * HALO
    part = jax.ShapeDtypeStruct((size_x - 2 * HALO, size_y, size_z), F32)
    kept = [jax.ShapeDtypeStruct((end - begin, rows, size_z), F32) for begin, end in spans(size_x).values()]
    latent = jax.ShapeDtypeStruct((size_z // 4, coarse.shape[1]), F32)
    return pl.pallas_call(
        functools.partial(inner_kernel, coarse_y),
        out_shape=(part, part, latent, jax.ShapeDtypeStruct((2, rows, size_z), F32), *kept),
        in_specs=[vmem()] * 8,
        out_specs=[vmem()] * (4 + len(kept)),
        scratch_shapes=[pltpu.VMEM((size_x - 2, rows, size_z), F32)],
        compiler_params=pltpu.CompilerParams(vmem_limit_bytes=VMEM_LIMIT),
        cost_estimate=pl.CostEstimate(flops=10 * 10**8, bytes_accessed=10 * 10**6, transcendentals=0),
        name="inner",
    )(phase, solute, side_a, strip_b, rest_b, coarse, matrices, along_z)


def rim_steps(
    coarse_y, width, near, size_x, face, corner, fans, matrices, along_z, kept, scratch, phase_new, solute_new
):
    hp0, hc0, p1, c1, gx, dv, dz, cz, fz, th = scratch
    _, size_y, size_z = phase_new.shape
    span = spans(size_x)
    odd_x = lax.rem(lax.axis_index("gx"), 2)
    flip = odd_x if near else 1 - odd_x
    spot = lambda v: v + (1 - flip) * (HALO - 1 - 2 * v)
    top = row_ids((ROWS, size_z)) < HALO
    for d, (p_rows, c_rows) in enumerate(halo_rows(corner, top)):
        layer = d + flip * (HALO - 1 - 2 * d)
        for n, (field, rows) in enumerate(((hp0, p_rows), (hc0, c_rows))):
            field[HALO - 1 - d, pl.ds(0, size_y), :] = face[n, layer]
            field[HALO - 1 - d, pl.ds(size_y, ROWS), :] = rows
    edge = jnp.where(row_ids(corner.shape[1:]) < 2, corner[0], pltpu.roll(corner[1], 4, 0))
    fans = {-1: interpolate(unpack_edge(edge), along_z[...], size_y)[0], 0: fans[1 if near else 0]}
    for v in range(-2, 2):
        th[v + 2] = blend(v, fans)

    def get(name, v):
        begin, end = span[name]
        if v >= begin:
            found = kept[name][(size_x - 1 - v if near else v) - begin]
            return -found if near and name.startswith("gx") else found
        own, first = dict(
            p0=(hp0, -4), c0=(hc0, -4), dz0=(dz, -3), cz0=(cz, -2), gx0=(gx, -3), dv0=(dv, -2),
            p1=(p1, -2), c1=(c1, -2), dz1=(dz, -1), cz1=(cz, 0), gx1=(gx, -1), dv1=(dv, 0), th=(th, -2),
        )[name]
        return own[v - first]

    for step, begin in (("0", -3), ("1", -1)):
        p, c, gx_, dv_, dz_, cz_ = (name + step for name in ("p", "c", "gx", "dv", "dz", "cz"))
        fields = (hp0[pl.ds(1, 3)], hc0[pl.ds(2, 2)]) if step == "0" else (p1[pl.ds(1, 3)], c1[pl.ds(2, 2)])
        dz[...] = along(fields[0], matrices[0])
        cz[...] = along(fields[1], matrices[2])
        for v in range(begin, begin + 4):
            flux_x, flux_y, flux_z = flux(get(p, v - 1), get(p, v), get(p, v + 1), get(dz_, v))
            gx[v - begin] = flux_x
            if v > begin:
                dv[v - begin - 1] = spread(flux_y)
                fz[v - begin - 1] = flux_z
        dv[...] += along(fz[...], matrices[1])
        take = (lambda w: w) if step == "0" else (lambda w: w[:size_y])
        for v in range(begin + 1, begin + 5):
            here, conc = take(get(p, v)), get(c, v)
            divergence = take(get(gx_, v + 1)) - take(get(gx_, v - 1)) + take(get(dv_, v))
            change = phase_change(here, take(conc), take(get("th", v)), divergence)
            beyond = take(get(c, v + 2)) + take(get(c, v - 2))
            new_conc = solute_step(take(conc), beyond, take(next_row(conc)), take(get(cz_, v)), change)
            if step == "0":
                p1[v + 2], c1[v + 2] = here + change, new_conc
            else:
                phase_new[spot(v)], solute_new[spot(v)] = here + change, new_conc
    change = jnp.zeros((size_y, size_z), F32)
    for v in range(HALO):
        change = change + (phase_new[spot(v)] - get("p0", v)[:size_y])
    u = size_x // 4 - 1 if near else 0
    return restrict(change, coarse_lane(u, size_x, size_y, coarse_y), width)


def near_kernel(coarse_y, size_x, face, corner, fans, matrices, along_z, *rest):
    kept = dict(zip(KEPT, rest[: len(KEPT)]))
    phase_new, solute_new, latent = rest[len(KEPT) : len(KEPT) + 3]
    latent[...] = rim_steps(
        coarse_y, latent.shape[1], True, size_x, face, corner, fans, matrices, along_z, kept,
        rest[len(KEPT) + 3 :], phase_new, solute_new,
    )


def far_kernel(coarse_y, size_x, face, corner, fans, matrices, along_z, inner_latent, near_latent, *rest):
    kept = dict(zip(KEPT, rest[: len(KEPT)]))
    phase_new, solute_new, keep, send, *scratch, total = rest[len(KEPT) :]
    mine = rim_steps(
        coarse_y, total.shape[1], False, size_x, face, corner, fans, matrices, along_z, kept, scratch, phase_new,
        solute_new,
    )
    total[...] = mine + inner_latent[...] + near_latent[...]
    halve(total, lax.div(2 * lax.axis_index("gy"), lax.axis_size("gy")), keep, send)


def halve(total, side, keep, send):
    half = keep.shape[0]
    keep[...] = total[pl.ds(pl.multiple_of(side * half, half), half), :]
    send[...] = total[pl.ds(pl.multiple_of((1 - side) * half, half), half), :]


def rim_scratch(size_y, size_z):
    counts = 4, 4, 4, 4, 4, 3, 3, 2, 3, 4
    return [pltpu.VMEM((count, size_y + 2 * HALO, size_z), F32) for count in counts]


def near_rim(shape, face, corner, fans, matrices, along_z, kept, width, coarse_y):
    size_x, size_y, size_z = shape
    part = jax.ShapeDtypeStruct((HALO, size_y, size_z), F32)
    return pl.pallas_call(
        functools.partial(near_kernel, coarse_y, size_x),
        out_shape=(part, part, jax.ShapeDtypeStruct((size_z // 4, width), F32)),
        in_specs=[vmem()] * (5 + len(kept)),
        out_specs=[vmem()] * 3,
        scratch_shapes=rim_scratch(size_y, size_z),
        compiler_params=pltpu.CompilerParams(vmem_limit_bytes=VMEM_LIMIT),
        cost_estimate=pl.CostEstimate(flops=20 * 10**8, bytes_accessed=20 * 10**6, transcendentals=0),
        name="near",
    )(face, corner, fans, matrices, along_z, *kept)


def far_rim(shape, face, corner, fans, matrices, along_z, inner_latent, near_latent, kept, coarse_y):
    size_x, size_y, size_z = shape
    part = jax.ShapeDtypeStruct((HALO, size_y, size_z), F32)
    width = inner_latent.shape[1]
    half = jax.ShapeDtypeStruct((size_z // 8, width), F32)
    return pl.pallas_call(
        functools.partial(far_kernel, coarse_y, size_x),
        out_shape=(part, part, half, half),
        in_specs=[vmem()] * (7 + len(kept)),
        out_specs=[vmem()] * 4,
        scratch_shapes=[*rim_scratch(size_y, size_z), pltpu.VMEM((size_z // 4, width), F32)],
        compiler_params=pltpu.CompilerParams(vmem_limit_bytes=VMEM_LIMIT),
        cost_estimate=pl.CostEstimate(flops=10**7, bytes_accessed=3 * 10**6, transcendentals=0),
        name="far",
    )(face, corner, fans, matrices, along_z, inner_latent, near_latent, *kept)


def store_kernel(*refs):
    parts, (phase_out, solute_out, sems) = refs[:6], refs[6:]
    size_x = phase_out.shape[0]
    odd_x = lax.rem(lax.axis_index("gx"), 2)
    near = (1 - odd_x) * (size_x - HALO)
    copies = []
    for begin, pair in ((HALO, parts[:2]), (near, parts[2:4]), (size_x - HALO - near, parts[4:])):
        for part, out in zip(pair, (phase_out, solute_out)):
            copies.append((part, out.at[pl.ds(begin, part.shape[0])]))
    wait_all(start_all(copies, sems))


def store(shape, parts):
    out = jax.ShapeDtypeStruct(shape, F32)
    return pl.pallas_call(
        store_kernel,
        out_shape=(out, out),
        in_specs=[vmem()] * 6,
        out_specs=[hbm()] * 2,
        scratch_shapes=[pltpu.SemaphoreType.DMA((6,))],
        compiler_params=pltpu.CompilerParams(vmem_limit_bytes=VMEM_LIMIT),
        cost_estimate=pl.CostEstimate(flops=0, bytes_accessed=4 * 10**6, transcendentals=0),
        name="store",
    )(*parts)


def merge_kernel(mine, arrived, keep, send, total):
    total[...] = mine[...] + arrived[...]
    halve(total, lax.rem(lax.axis_index("gy"), 2), keep, send)


def merge(mine, arrived):
    half = jax.ShapeDtypeStruct((mine.shape[0] // 2, mine.shape[1]), F32)
    return pl.pallas_call(
        merge_kernel,
        out_shape=(half, half),
        in_specs=[vmem()] * 2,
        out_specs=[vmem()] * 2,
        scratch_shapes=[pltpu.VMEM(mine.shape, F32)],
        compiler_params=pltpu.CompilerParams(vmem_limit_bytes=VMEM_LIMIT),
        cost_estimate=pl.CostEstimate(flops=10**4, bytes_accessed=10**5, transcendentals=0),
        name="merge",
    )(mine, arrived)


def owner_kernel(mine, arrived, out):
    total = mine[...] + arrived[...]
    coarse_x, _, coarse_y = out.shape
    for k in range(coarse_x):
        out[k] = total[:, k * coarse_y : (k + 1) * coarse_y]


def owner(mine, arrived, coarse_x, coarse_y):
    coarse_z = mine.shape[0]
    return pl.pallas_call(
        owner_kernel,
        out_shape=jax.ShapeDtypeStruct((coarse_x, coarse_z, coarse_y), F32),
        in_specs=[vmem()] * 2,
        out_specs=vmem(),
        compiler_params=pltpu.CompilerParams(vmem_limit_bytes=VMEM_LIMIT),
        cost_estimate=pl.CostEstimate(flops=10**4, bytes_accessed=10**5, transcendentals=0),
        name="owner",
    )(mine, arrived)


def body(phase, solute, macro_temp):
    count_x, count_y = lax.axis_size("gx"), lax.axis_size("gy")
    coarse_x, coarse_y, coarse_z = macro_temp.shape
    near_x, far_x = pairs(count_x, 0), pairs(count_x, 1)
    near_y, far_y = pairs(count_y, 0), pairs(count_y, 1)
    across = [(k, (k + count_y // 2) % count_y) for k in range(count_y)]
    ride = count_y == 4
    macro = jnp.swapaxes(macro_temp, 1, 2)
    still = [pltpu.with_memory_space_constraint(v, pltpu.HBM) for v in (phase, solute, macro)]
    phase, solute, face_a, face_b, side_a, strip_b, rest_b, table = pack(*still, ride)
    coarse_shape = (coarse_z * count_y, coarse_x * coarse_y)
    face_a = lax.ppermute(face_a, "gx", near_x)
    side_a = lax.ppermute(side_a, "gy", near_y)
    if ride:
        strip_b = append(side_a, strip_b)
    else:
        table = lax.all_gather(table, "gy").reshape(coarse_shape)
    matrices, along_z = z_products(phase.shape[2], strip_b)
    face_b, rest_b, matrices = lax.optimization_barrier((face_b, rest_b, matrices))
    strip_b = lax.ppermute(strip_b, "gy", far_y)
    rest_b = lax.ppermute(rest_b, "gy", far_y)
    face_b = lax.ppermute(face_b, "gx", far_x)
    coarse, corner_a, corner_b = corners(side_a, strip_b, table, coarse_y, coarse_shape)
    corner_a = lax.ppermute(corner_a, "gx", near_x)
    corner_b = lax.ppermute(corner_b, "gx", far_x)
    results = inner(phase, solute, side_a, strip_b, rest_b, coarse, matrices, along_z, coarse_y)
    middle, inner_latent, fans, kept = results[:2], results[2], results[3], results[4:]
    *near, near_latent = near_rim(
        phase.shape, face_a, corner_a, fans, matrices, along_z, kept, coarse_shape[1], coarse_y
    )
    *far, mine, send = far_rim(
        phase.shape, face_b, corner_b, fans, matrices, along_z, inner_latent, near_latent, kept, coarse_y
    )
    phase_out, solute_out = store(phase.shape, (*middle, *near, *far))
    if ride:
        mine, send = merge(mine, lax.ppermute(send, "gy", across))
        latent = owner(mine, lax.ppermute(send, "gy", near_y), coarse_x, coarse_y)
    else:
        low = lax.axis_index("gy") < count_y // 2
        total = jnp.concatenate([jnp.where(low, mine, send), jnp.where(low, send, mine)])
        latent = lax.psum_scatter(total, "gy", scatter_dimension=0, tiled=True)
        latent = jnp.swapaxes(latent.reshape(coarse_z, coarse_x, coarse_y), 0, 1)
    latent = jnp.swapaxes(latent, 1, 2)
    return phase_out, solute_out, latent


def solution(mesh):
    in_specs = (P("gx", "gy", None), P("gx", "gy", None), P("gx", None, "gy"))
    out_specs = (P("gx", "gy", None), P("gx", "gy", None), P("gx", None, "gy"))
    return jax.shard_map(body, mesh=mesh, in_specs=in_specs, out_specs=out_specs, check_vma=False)
```

time: 29.8 us -> 28.1 us (0.943)
  starting transfers between devices: 15.4 us -> 14 us
  waiting for transfers between devices: 3.55 us -> 2.97 us
  Pallas kernels: 10 us -> 10.3 us
    ppermute x1, starting transfers between devices: 1.24 us -> 0.02 us  [body(): corner_a = lax.ppermute(corner_a, 'gx', near_x)]
    ppermute x4, waiting for transfers between devices: 3.53 us -> 2.4 us  [the longest x1 2.24 us: body(): mine, send = merge(mine, lax.ppermute(send, 'gy', across))]
    ppermute x1, starting transfers between devices: 3.84 us -> 3.17 us  [body(): corner_b = lax.ppermute(corner_b, 'gx', far_x)]
    ppermute x1, waiting for transfers between devices: 0.01 us -> 0.56 us  [body(): corner_a = lax.ppermute(corner_a, 'gx', near_x)]
    ppermute x4, starting transfers between devices: 2.89 us -> 3.37 us  [the longest x1 1.56 us: body(): mine, send = merge(mine, lax.ppermute(send, 'gy', across))]
    pallas_call x5 -> x7, Pallas kernels: 8.39 us -> 8.43 us  [the longest x1 3.61 us: inner(): pl.pallas_call(functools.partial(inner_kernel, coarse_y), out_shape=(part...]
  transfers between devices with their start and end apart: 9 -> 9, of which waited for: 3 -> 3; matrix products, arithmetic and copies ran while one was open for 0% -> 0% of each run, Pallas kernels for 18% -> 24%
where the time goes in v4:
time: 28.1 us; the launch traced here: 27.9 us
  starting transfers between devices  14 us (50%)
  Pallas kernels  10.3 us (37%)
  waiting for transfers between devices  2.97 us (11%)
  between operations  0.69 us (2%)
    ppermute x1, starting transfers between devices, body(): face_b = lax.ppermute(face_b, 'gx', far_x)  4.32 us
    pallas_call x1, Pallas kernels, inner(): pl.pallas_call(functools.partial(inner_kernel, coarse_y), out_shape=(part...  3.61 us
    ppermute x1, starting transfers between devices, body(): corner_b = lax.ppermute(corner_b, 'gx', far_x)  3.17 us
    ppermute x1, starting transfers between devices, body(): face_a = lax.ppermute(face_a, 'gx', near_x)  2.59 us
    ppermute x1, waiting for transfers between devices, body(): mine, send = merge(mine, lax.ppermute(send, 'gy', across))  2.24 us
    ppermute x1, starting transfers between devices, body(): mine, send = merge(mine, lax.ppermute(send, 'gy', across))  1.56 us
    pallas_call x1, Pallas kernels, pack(): pl.pallas_call(pack_kernel, out_shape=(field, field, face, face, *sides,...  1.5 us
    pallas_call x1, Pallas kernels, far_rim(): pl.pallas_call(functools.partial(far_kernel, coarse_y, size_x), out_shape...  1.46 us
  transfers between devices with their start and end apart: 9, of which 3 were waited for; matrix products, arithmetic and copies ran while one was open for 0% of the time, Pallas kernels for 24%

profile of v4, /device:TPU:0, one launch (start us, length us, event | category | flops | bytes accessed | tf_op | source)
XLA Modules:
  0.0 27.9 jit_solution(13177055539484617877)
XLA Ops:
  0.6 1.5 %pack.1 = (f32[16,32,256]{2,1,0:T(8,128)S(1)}, f32[16,32,256]{2,1,0:T(8,128)S(1)}, f32[2,4,32,256]{3,2,1,0:T(8,128)S(1)}, f32[2,4,32,256]{3,2,1,0:T(8,128)S(1)},...) custom-call(f32[16,32,256]{2,1,0:T(8,128)} %phase.1, ...), custom_call_target="tpu_custom_call" | custom-call | flops 100000 | bytes 2000000 | tf_op jit(solution)/shard_map/pack/pallas_call | solution.py:117
  2.1 0.5 %collective-permute-start = (f32[17,8,256]{2,1,0:T(8,128)S(1)}, f32[17,8,256]{2,1,0:T(8,128)S(1)}, u32[]{:S(2)}, u32[]{:S(2)}) collective-permute-start(f32[17,8,256]{2,1,0:T(8,128)S(1)} %get-tuple-element.49), channel_id=1, source_target_pairs={{0,1},{2,3},{1,0},{3,2},{4,5},{6,7},{5,4},{7,6},{8,9},{10,11},{9,8... | collective-permute-start | bytes 417800 | tf_op jit(solution)/shard_map/ppermute | solution.py:640
  2.7 2.6 %collective-permute-start.3 = (f32[2,4,32,256]{3,2,1,0:T(8,128)S(1)}, f32[2,4,32,256]{3,2,1,0:T(8,128)S(1)}, u32[]{:S(2)}, u32[]{:S(2)}) collective-permute-start(f32[2,4,32,256]{3,2,1,0:T(8,128)S(1)} %get-tuple-element.61), channel_id=1, source_target_pairs={{0,4},{8,12},{16,20},{24,28},{4,0},{12,8},{20,16},{28,24},{1,5},{9... | collective-permute-start | bytes 786440 | tf_op jit(solution)/shard_map/ppermute | solution.py:639
  5.3 0.0 collective-permute-done.arrived.side_a
  5.3 1.3 %collective-permute-start.1 = (f32[10,8,256]{2,1,0:T(8,128)S(1)}, f32[10,8,256]{2,1,0:T(8,128)S(1)}, u32[]{:S(2)}, u32[]{:S(2)}) collective-permute-start(f32[10,8,256]{2,1,0:T(8,128)S(1)} %append.1.tile), channel_id=1, source_target_pairs={{1,2},{3,0},{2,1},{0,3},{5,6},{7,4},{6,5},{4,7},{9,10},{11,8},{10,... | collective-permute-start | bytes 245768 | tf_op jit(solution)/shard_map/ppermute | solution.py:647
  6.5 0.1 products.1
  6.7 0.5 %collective-permute-start.2 = (f32[8,8,256]{2,1,0:T(8,128)S(1)}, f32[8,8,256]{2,1,0:T(8,128)S(1)}, u32[]{:S(2)}, u32[]{:S(2)}) collective-permute-start(f32[8,8,256]{2,1,0:T(8,128)S(1)} %get-tuple-element.54), channel_id=1, source_target_pairs={{1,2},{3,0},{2,1},{0,3},{5,6},{7,4},{6,5},{4,7},{9,10},{11,8},{10,... | collective-permute-start | bytes 196616 | tf_op jit(solution)/shard_map/ppermute | solution.py:648
  7.2 4.3 %collective-permute-start.5 = (f32[2,4,32,256]{3,2,1,0:T(8,128)S(1)}, f32[2,4,32,256]{3,2,1,0:T(8,128)S(1)}, u32[]{:S(2)}, u32[]{:S(2)}) collective-permute-start(f32[2,4,32,256]{3,2,1,0:T(8,128)S(1)} %get-tuple-element.79), channel_id=1, source_target_pairs={{4,8},{12,16},{20,24},{28,0},{8,4},{16,12},{24,20},{0,28},{5,9},{1... | collective-permute-start | bytes 786440 | tf_op jit(solution)/shard_map/ppermute | solution.py:649
  11.5 0.0 collective-permute-done.1.strip_b
  11.5 0.4 %corners.1 = (f32[64,128]{1,0:T(8,128)S(1)}, f32[3,8,256]{2,1,0:T(8,128)S(1)}, f32[3,8,256]{2,1,0:T(8,128)S(1)}) custom-call(f32[17,8,256]{2,1,0:T(8,128)S(1)} %collective-permute-done.arrived.side_a, f32[10,8,256]{2,1,0:T(8,128)S(1)} %collective-permute-done.1.strip_b, f32[16,128]{1,0:T(8,128)S(1)} %get-tuple-element.55.table), custom_call_target="tpu_custom_call" | custom-call | flops 100000 | bytes 400000 | tf_op jit(solution)/shard_map/corners/pallas_call | solution.py:204
  12.0 0.0 collective-permute-start.4
  12.0 3.2 %collective-permute-start.6 = (f32[3,8,256]{2,1,0:T(8,128)S(1)}, f32[3,8,256]{2,1,0:T(8,128)S(1)}, u32[]{:S(2)}, u32[]{:S(2)}) collective-permute-start(f32[3,8,256]{2,1,0:T(8,128)S(1)} %get-tuple-element.80), channel_id=1, source_target_pairs={{4,8},{12,16},{20,24},{28,0},{8,4},{16,12},{24,20},{0,28},{5,9},{1... | collective-permute-start | bytes 73736 | tf_op jit(solution)/shard_map/ppermute | solution.py:652
  15.2 0.0 collective-permute-done.2.rest_b
  15.2 3.6 %inner.1 = (f32[8,32,256]{2,1,0:T(8,128)S(1)}, f32[8,32,256]{2,1,0:T(8,128)S(1)}, f32[64,128]{1,0:T(8,128)S(1)}, f32[2,40,256]{2,1,0:T(8,128)S(1)}, f32[16,40,25...) custom-call(f32[16,32,256]{2,1,0:T(8,128)S(1)} %get-tuple-element.47, ...), custom_call_target="tpu_custom_call" | custom-call | flops 1000000000 | bytes 10000000 | tf_op jit(solution)/shard_map/inner/pallas_call | solution.py:427
  18.8 0.6 %collective-permute-done.4.corner = f32[3,8,256]{2,1,0:T(8,128)S(1)} collective-permute-done((f32[3,8,256]{2,1,0:T(8,128)S(1)}, f32[3,8,256]{2,1,0:T(8,128)S(1)}, u32[]{:S(2)}, u32[]{:S(2)}) %collective-permute-start.4) | collective-permute-done | bytes 24608 | tf_op jit(solution)/shard_map/ppermute | solution.py:651
  19.3 0.0 collective-permute-done.3.face
  19.3 1.4 %near.1 = (f32[4,32,256]{2,1,0:T(8,128)S(1)}, f32[4,32,256]{2,1,0:T(8,128)S(1)}, f32[64,128]{1,0:T(8,128)S(1)}) custom-call(f32[2,4,32,256]{3,2,1,0:T(8,128)S(1)} %collective-permute-done.3.face, f32[3,8,256]{2,1,0:T(8,128)S(1)} %collective-permute-done.4.corner, f32[2,40,256]{2,1,0:T(8,128)S(1)} %get-tuple-element.63.fans, ...), custom_call_target="tpu_custom_call" | custom-call | flops 2000000000 | bytes 20000000 | tf_op jit(solution)/shard_map/near/pallas_call | solution.py:534
  20.8 0.0 collective-permute-done.6.corner
  20.8 0.0 collective-permute-done.5.face
  20.8 1.5 %far.1 = (f32[4,32,256]{2,1,0:T(8,128)S(1)}, f32[4,32,256]{2,1,0:T(8,128)S(1)}, f32[32,128]{1,0:T(8,128)S(1)}, f32[32,128]{1,0:T(8,128)S(1)}) custom-call(f32[2,4,32,256]{3,2,1,0:T(8,128)S(1)} %collective-permute-done.5.face, f32[3,8,256]{2,1,0:T(8,128)S(1)} %collective-permute-done.6.corner, f32[2,40,256]{2,1,0:T(8,128)S(1)} %get-tuple-element.63.fans, ...), custom_call_target="tpu_custom_call" | custom-call | flops 10000000 | bytes 3000000 | tf_op jit(solution)/shard_map/far/pallas_call | solution.py:551
  22.3 1.6 %collective-permute-start.7 = (f32[32,128]{1,0:T(8,128)S(1)}, f32[32,128]{1,0:T(8,128)S(1)}, u32[]{:S(2)}, u32[]{:S(2)}) collective-permute-start(f32[32,128]{1,0:T(8,128)S(1)} %get-tuple-element.88), channel_id=1, source_target_pairs={{0,2},{1,3},{2,0},{3,1},{4,6},{5,7},{6,4},{7,5},{8,10},{9,11},{10,... | collective-permute-start | bytes 49160 | tf_op jit(solution)/shard_map/ppermute | solution.py:663
  23.8 2.2 %collective-permute-done.7.arrived = f32[32,128]{1,0:T(8,128)S(1)} collective-permute-done((f32[32,128]{1,0:T(8,128)S(1)}, f32[32,128]{1,0:T(8,128)S(1)}, u32[]{:S(2)}, u32[]{:S(2)}) %collective-permute-start.7) | collective-permute-done | bytes 16416 | tf_op jit(solution)/shard_map/ppermute | solution.py:663
  26.1 0.0 collective-permute-start.8
  26.1 1.0 %store.1 = (f32[16,32,256]{2,1,0:T(8,128)}, f32[16,32,256]{2,1,0:T(8,128)}) custom-call(f32[8,32,256]{2,1,0:T(8,128)S(1)} %get-tuple-element.59.refs_0_, f32[8,32,256]{2,1,0:T(8,128)S(1)} %get-tuple-element.60.refs_1_, f32[4,32,256]{2,1,0:T(8,128)S(1)} %get-tuple-element.77.refs_2_, f32[4,32,256]{2,1,0:T(8,128)S(1)} %get-tuple-element.78.refs_3_, ...), custom_call_target="tpu_custom_call" | custom-call | bytes 4000000 | tf_op jit(solution)/shard_map/store/pallas_call | solution.py:577
  27.1 0.1 collective-permute-done.8.arrived
  27.3 0.7 %owner.1 = f32[4,16,32]{2,1,0:T(8,128)} custom-call(f32[16,128]{1,0:T(8,128)S(1)} %get-tuple-element.89.mine, f32[16,128]{1,0:T(8,128)S(1)} %collective-permute-done.8.arrived), custom_call_target="tpu_custom_call" | custom-call | flops 10000 | bytes 100000 | tf_op jit(solution)/shard_map/owner/pallas_call | solution.py:617
  (2 shorter events, 0.0 us)
Async XLA Ops:
  2.1 3.1 %collective-permute-start = (f32[17,8,256]{2,1,0:T(8,128)S(1)}, f32[17,8,256]{2,1,0:T(8,128)S(1)}, u32[]{:S(2)}, u32[]{:S(2)}) collective-permute-start(f32[17,8,256]{2,1,0:T(8,128)S(1)} %get-tuple-element.49), channel_id=1, source_target_pairs={{0,1},{2,3},{1,0},{3,2},{4,5},{6,7},{5,4},{7,6},{8,9},{10,11},{9,8... | collective-permute-start | bytes 417800 | tf_op jit(solution)/shard_map/ppermute | solution.py:640
  2.7 16.7 %collective-permute-start.3 = (f32[2,4,32,256]{3,2,1,0:T(8,128)S(1)}, f32[2,4,32,256]{3,2,1,0:T(8,128)S(1)}, u32[]{:S(2)}, u32[]{:S(2)}) collective-permute-start(f32[2,4,32,256]{3,2,1,0:T(8,128)S(1)} %get-tuple-element.61), channel_id=1, source_target_pairs={{0,4},{8,12},{16,20},{24,28},{4,0},{12,8},{20,16},{28,24},{1,5},{9... | collective-permute-start | bytes 786440 | tf_op jit(solution)/shard_map/ppermute | solution.py:639
  5.3 6.3 %collective-permute-start.1 = (f32[10,8,256]{2,1,0:T(8,128)S(1)}, f32[10,8,256]{2,1,0:T(8,128)S(1)}, u32[]{:S(2)}, u32[]{:S(2)}) collective-permute-start(f32[10,8,256]{2,1,0:T(8,128)S(1)} %append.1.tile), channel_id=1, source_target_pairs={{1,2},{3,0},{2,1},{0,3},{5,6},{7,4},{6,5},{4,7},{9,10},{11,8},{10,... | collective-permute-start | bytes 245768 | tf_op jit(solution)/shard_map/ppermute | solution.py:647
  6.7 8.5 %collective-permute-start.2 = (f32[8,8,256]{2,1,0:T(8,128)S(1)}, f32[8,8,256]{2,1,0:T(8,128)S(1)}, u32[]{:S(2)}, u32[]{:S(2)}) collective-permute-start(f32[8,8,256]{2,1,0:T(8,128)S(1)} %get-tuple-element.54), channel_id=1, source_target_pairs={{1,2},{3,0},{2,1},{0,3},{5,6},{7,4},{6,5},{4,7},{9,10},{11,8},{10,... | collective-permute-start | bytes 196616 | tf_op jit(solution)/shard_map/ppermute | solution.py:648
  7.2 13.6 %collective-permute-start.5 = (f32[2,4,32,256]{3,2,1,0:T(8,128)S(1)}, f32[2,4,32,256]{3,2,1,0:T(8,128)S(1)}, u32[]{:S(2)}, u32[]{:S(2)}) collective-permute-start(f32[2,4,32,256]{3,2,1,0:T(8,128)S(1)} %get-tuple-element.79), channel_id=1, source_target_pairs={{4,8},{12,16},{20,24},{28,0},{8,4},{16,12},{24,20},{0,28},{5,9},{1... | collective-permute-start | bytes 786440 | tf_op jit(solution)/shard_map/ppermute | solution.py:649
  12.0 7.4 %collective-permute-start.4 = (f32[3,8,256]{2,1,0:T(8,128)S(1)}, f32[3,8,256]{2,1,0:T(8,128)S(1)}, u32[]{:S(2)}, u32[]{:S(2)}) collective-permute-start(f32[3,8,256]{2,1,0:T(8,128)S(1)} %get-tuple-element.62), channel_id=1, source_target_pairs={{0,4},{8,12},{16,20},{24,28},{4,0},{12,8},{20,16},{28,24},{1,5},{9... | collective-permute-start | bytes 73736 | tf_op jit(solution)/shard_map/ppermute | solution.py:651
  12.0 8.8 %collective-permute-start.6 = (f32[3,8,256]{2,1,0:T(8,128)S(1)}, f32[3,8,256]{2,1,0:T(8,128)S(1)}, u32[]{:S(2)}, u32[]{:S(2)}) collective-permute-start(f32[3,8,256]{2,1,0:T(8,128)S(1)} %get-tuple-element.80), channel_id=1, source_target_pairs={{4,8},{12,16},{20,24},{28,0},{8,4},{16,12},{24,20},{0,28},{5,9},{1... | collective-permute-start | bytes 73736 | tf_op jit(solution)/shard_map/ppermute | solution.py:652
  22.3 3.8 %collective-permute-start.7 = (f32[32,128]{1,0:T(8,128)S(1)}, f32[32,128]{1,0:T(8,128)S(1)}, u32[]{:S(2)}, u32[]{:S(2)}) collective-permute-start(f32[32,128]{1,0:T(8,128)S(1)} %get-tuple-element.88), channel_id=1, source_target_pairs={{0,2},{1,3},{2,0},{3,1},{4,6},{5,7},{6,4},{7,5},{8,10},{9,11},{10,... | collective-permute-start | bytes 49160 | tf_op jit(solution)/shard_map/ppermute | solution.py:663
  26.1 1.2 %collective-permute-start.8 = (f32[16,128]{1,0:T(8,128)S(1)}, f32[16,128]{1,0:T(8,128)S(1)}, u32[]{:S(2)}, u32[]{:S(2)}) collective-permute-start(f32[16,128]{1,0:T(8,128)S(1)} %get-tuple-element.90), channel_id=1, source_target_pairs={{0,1},{2,3},{1,0},{3,2},{4,5},{6,7},{5,4},{7,6},{8,9},{10,11},{9,8... | collective-permute-start | bytes 24584 | tf_op jit(solution)/shard_map/ppermute | solution.py:664

commit v5 on v4

--- a/solution.py
+++ b/solution.py
@@ -13,7 +13,6 @@
 rejection = 0.5
 
 F32 = jnp.float32
-HIGHEST = lax.Precision.HIGHEST
 HALO = 4
 STRIP = 4
 ROWS = 8
@@ -41,6 +40,20 @@
 def flips(me):
     odd = lax.rem(me, 2)
     return me, me + 1 - 2 * odd, lax.rem(me + 2, 4), 3 - me
+
+
+def halves(value):
+    coarse = value.astype(jnp.bfloat16)
+    return coarse, (value - coarse.astype(F32)).astype(jnp.bfloat16)
+
+
+def product(left, right, contract):
+    dot = lambda a, b: lax.dot_general(a, b, ((contract[:1], contract[1:]), ((), ())), preferred_element_type=F32)
+    if left.dtype == jnp.bfloat16:
+        parts = [dot(left, part) for part in halves(right)]
+    else:
+        parts = [dot(part, right) for part in halves(left)]
+    return parts[0] + parts[1]
 
 
 def row_ids(shape):
@@ -146,8 +159,8 @@
 def near_rows(block, coarse_y):
     shape = (2 * ROWS, coarse_y)
     wanted = lax.rem(row_ids(shape) + lax.axis_index("gy") * ROWS + coarse_y - 1, coarse_y)
-    pick = (lane_ids(shape) == wanted).astype(F32)
-    return lax.dot_general(pick, block, (((1,), (1,)), ((), ())), precision=HIGHEST, preferred_element_type=F32)
+    pick = (lane_ids(shape) == wanted).astype(F32).astype(jnp.bfloat16)
+    return product(pick, block, (1, 1))
 
 
 def pack_edge(rows):
@@ -227,15 +240,15 @@
 
 
 def interpolate(rows, along_z, size_y):
-    deep = jnp.dot(rows, along_z, precision=HIGHEST, preferred_element_type=F32)
+    deep = product(rows, along_z, (1, 0))
     shape = (size_y + 2 * HALO, 2 * ROWS)
     fine = row_ids(shape)
     fine = jnp.where(fine >= size_y + HALO, fine - shape[0], fine)
     lower = (2 * fine + 13) // 8 - 2
     frac = (2 * fine - 3 - 8 * lower).astype(F32) / 8.0
-    along_y = weights((lower + 1, lower + 2), frac, lane_ids(shape))
+    along_y = weights((lower + 1, lower + 2), frac, lane_ids(shape)).astype(jnp.bfloat16)
     return [
-        jnp.dot(along_y, deep[at : at + 2 * ROWS], precision=HIGHEST, preferred_element_type=F32)
+        product(along_y, deep[at : at + 2 * ROWS], (1, 0))
         for at in range(0, rows.shape[0], 2 * ROWS)
     ]
 
@@ -264,14 +277,14 @@
 def matrix_kernel(size_z, tile, out, along_z):
     for n, matrix in enumerate(z_matrices(size_z)):
         out[n] = matrix
-    along_z[...] = weights_z(*along_z.shape)
+    along_z[...] = weights_z(*along_z.shape).astype(jnp.bfloat16)
 
 
 def z_products(size_z, tile):
     square = jax.ShapeDtypeStruct((3, size_z, size_z), jnp.bfloat16)
     return pl.pallas_call(
         functools.partial(matrix_kernel, size_z),
-        out_shape=(square, jax.ShapeDtypeStruct((size_z // 4, size_z), F32)),
+        out_shape=(square, jax.ShapeDtypeStruct((size_z // 4, size_z), jnp.bfloat16)),
         in_specs=[anywhere()],
         out_specs=[vmem()] * 2,
         compiler_params=pltpu.CompilerParams(vmem_limit_bytes=VMEM_LIMIT),
@@ -281,11 +294,7 @@
 
 
 def along(slabs, matrix):
-    value = slabs.reshape(-1, slabs.shape[-1])
-    coarse = value.astype(jnp.bfloat16)
-    rest = (value - coarse.astype(F32)).astype(jnp.bfloat16)
-    product = jnp.dot(coarse, matrix, preferred_element_type=F32) + jnp.dot(rest, matrix, preferred_element_type=F32)
-    return product.reshape(slabs.shape)
+    return product(slabs.reshape(-1, slabs.shape[-1]), matrix, (1, 0)).reshape(slabs.shape)
 
 
 def flux(before, here, after, along_z):
@@ -318,16 +327,14 @@
     return turn(conc, -2, 0) + turn(conc, 2, 0)
 
 
-def restrict(change, at, coarse_width):
-    size_y, size_z = change.shape
+def restrict(changes, lanes, size_y, size_z, coarse_width):
     shape = (size_z // 4, size_z)
-    pool_z = (lane_ids(shape) // 4 == row_ids(shape)).astype(F32)
+    pool_z = (lane_ids(shape) // 4 == row_ids(shape)).astype(F32).astype(jnp.bfloat16)
     shape = (size_y, coarse_width)
-    pool_y = jnp.where(row_ids(shape) // 4 + at == lane_ids(shape), 0.5 / 64.0, 0.0)
-    change = lax.dot_general(
-        pool_z, change, (((1,), (1,)), ((), ())), precision=HIGHEST, preferred_element_type=F32
-    )
-    return jnp.dot(change, pool_y, precision=HIGHEST, preferred_element_type=F32)
+    cell, lane = row_ids(shape) // 4, lane_ids(shape)
+    pool_y = [jnp.where(cell + at == lane, 0.5 / 64.0, 0.0).astype(jnp.bfloat16) for at in lanes]
+    pooled = product(pool_z, jnp.concatenate(changes, axis=0), (1, 1))
+    return product(pooled, jnp.concatenate(pool_y, axis=0), (1, 0))
 
 
 def coarse_lane(u, size_x, size_y, coarse_y):
@@ -409,13 +416,14 @@
             else:
                 phase_new[place(u) - HALO] = here + change
                 solute_new[place(u) - HALO] = new_conc
-    total = jnp.zeros(latent.shape, F32)
+    changes, lanes = [], []
     for k in range(1, size_x // 4 - 1):
         change = jnp.zeros((size_y, size_z), F32)
         for u in range(4 * k, 4 * k + 4):
             change = change + (phase_new[place(u) - HALO] - get("p0", u)[:size_y])
-        total = total + restrict(change, coarse_lane(k, size_x, size_y, coarse_y), latent.shape[1])
-    latent[...] = total
+        changes.append(change)
+        lanes.append(coarse_lane(k, size_x, size_y, coarse_y))
+    latent[...] = restrict(changes, lanes, size_y, size_z, latent.shape[1])
 
 
 def inner(phase, solute, side_a, strip_b, rest_b, coarse, matrices, along_z, coarse_y):
@@ -431,30 +439,33 @@
         out_specs=[vmem()] * (4 + len(kept)),
         scratch_shapes=[pltpu.VMEM((size_x - 2, rows, size_z), F32)],
         compiler_params=pltpu.CompilerParams(vmem_limit_bytes=VMEM_LIMIT),
-        cost_estimate=pl.CostEstimate(flops=10 * 10**8, bytes_accessed=10 * 10**6, transcendentals=0),
+        cost_estimate=pl.CostEstimate(flops=5 * 10**8, bytes_accessed=5 * 10**6, transcendentals=0),
         name="inner",
     )(phase, solute, side_a, strip_b, rest_b, coarse, matrices, along_z)
 
 
-def rim_steps(
-    coarse_y, width, near, size_x, face, corner, fans, matrices, along_z, kept, scratch, phase_new, solute_new
-):
-    hp0, hc0, p1, c1, gx, dv, dz, cz, fz, th = scratch
+def rim_halo(near, face, corner, along_z, phase_halo, solute_halo, fan):
+    _, _, size_y, size_z = face.shape
+    odd_x = lax.rem(lax.axis_index("gx"), 2)
+    flip = odd_x if near else 1 - odd_x
+    top = row_ids((ROWS, size_z)) < HALO
+    for d, (p_rows, c_rows) in enumerate(halo_rows(corner, top)):
+        layer = d + flip * (HALO - 1 - 2 * d)
+        for n, (field, rows) in enumerate(((phase_halo, p_rows), (solute_halo, c_rows))):
+            field[HALO - 1 - d, pl.ds(0, size_y), :] = face[n, layer]
+            field[HALO - 1 - d, pl.ds(size_y, ROWS), :] = rows
+    edge = jnp.where(row_ids(corner.shape[1:]) < 2, corner[0], pltpu.roll(corner[1], 4, 0))
+    fan[...] = interpolate(unpack_edge(edge), along_z[...], size_y)[0]
+
+
+def rim_march(near, size_x, halo, fans, matrices, kept, scratch, phase_new, solute_new, result):
+    hp0, hc0, fan = halo
+    p1, c1, gx, dv, dz, cz, fz, th = scratch
     _, size_y, size_z = phase_new.shape
     span = spans(size_x)
     odd_x = lax.rem(lax.axis_index("gx"), 2)
     flip = odd_x if near else 1 - odd_x
     spot = lambda v: v + (1 - flip) * (HALO - 1 - 2 * v)
-    top = row_ids((ROWS, size_z)) < HALO
-    for d, (p_rows, c_rows) in enumerate(halo_rows(corner, top)):
-        layer = d + flip * (HALO - 1 - 2 * d)
-        for n, (field, rows) in enumerate(((hp0, p_rows), (hc0, c_rows))):
-            field[HALO - 1 - d, pl.ds(0, size_y), :] = face[n, layer]
-            field[HALO - 1 - d, pl.ds(size_y, ROWS), :] = rows
-    edge = jnp.where(row_ids(corner.shape[1:]) < 2, corner[0], pltpu.roll(corner[1], 4, 0))
-    fans = {-1: interpolate(unpack_edge(edge), along_z[...], size_y)[0], 0: fans[1 if near else 0]}
-    for v in range(-2, 2):
-        th[v + 2] = blend(v, fans)
 
     def get(name, v):
         begin, end = span[name]
@@ -467,18 +478,24 @@
         )[name]
         return own[v - first]
 
+    ends = {-1: fan[...], 0: fans[1 if near else 0]}
+    for v in range(-2, 2):
+        th[v + 2] = blend(v, ends)
     for step, begin in (("0", -3), ("1", -1)):
         p, c, gx_, dv_, dz_, cz_ = (name + step for name in ("p", "c", "gx", "dv", "dz", "cz"))
         fields = (hp0[pl.ds(1, 3)], hc0[pl.ds(2, 2)]) if step == "0" else (p1[pl.ds(1, 3)], c1[pl.ds(2, 2)])
         dz[...] = along(fields[0], matrices[0])
         cz[...] = along(fields[1], matrices[2])
+        yield
         for v in range(begin, begin + 4):
             flux_x, flux_y, flux_z = flux(get(p, v - 1), get(p, v), get(p, v + 1), get(dz_, v))
             gx[v - begin] = flux_x
             if v > begin:
                 dv[v - begin - 1] = spread(flux_y)
                 fz[v - begin - 1] = flux_z
+        yield
         dv[...] += along(fz[...], matrices[1])
+        yield
         take = (lambda w: w) if step == "0" else (lambda w: w[:size_y])
         for v in range(begin + 1, begin + 5):
             here, conc = take(get(p, v)), get(c, v)
@@ -490,30 +507,51 @@
                 p1[v + 2], c1[v + 2] = here + change, new_conc
             else:
                 phase_new[spot(v)], solute_new[spot(v)] = here + change, new_conc
+        yield
     change = jnp.zeros((size_y, size_z), F32)
     for v in range(HALO):
         change = change + (phase_new[spot(v)] - get("p0", v)[:size_y])
-    u = size_x // 4 - 1 if near else 0
-    return restrict(change, coarse_lane(u, size_x, size_y, coarse_y), width)
-
-
-def near_kernel(coarse_y, size_x, face, corner, fans, matrices, along_z, *rest):
+    result.append(change)
+
+
+def near_kernel(face, corner, along_z, phase_halo, solute_halo, fan):
+    rim_halo(True, face, corner, along_z, phase_halo, solute_halo, fan)
+
+
+def near_halo(face, corner, along_z):
+    _, _, size_y, size_z = face.shape
+    rows = size_y + 2 * HALO
+    slabs = jax.ShapeDtypeStruct((HALO, rows, size_z), F32)
+    return pl.pallas_call(
+        near_kernel,
+        out_shape=(slabs, slabs, jax.ShapeDtypeStruct((rows, size_z), F32)),
+        in_specs=[vmem()] * 3,
+        out_specs=[vmem()] * 3,
+        compiler_params=pltpu.CompilerParams(vmem_limit_bytes=VMEM_LIMIT),
+        cost_estimate=pl.CostEstimate(flops=15 * 10**8, bytes_accessed=15 * 10**6, transcendentals=0),
+        name="near",
+    )(face, corner, along_z)
+
+
+def rim_kernel(
+    coarse_y, size_x, face, corner, near_phase, near_solute, near_fan, fans, matrices, along_z, inner_latent, *rest
+):
     kept = dict(zip(KEPT, rest[: len(KEPT)]))
-    phase_new, solute_new, latent = rest[len(KEPT) : len(KEPT) + 3]
-    latent[...] = rim_steps(
-        coarse_y, latent.shape[1], True, size_x, face, corner, fans, matrices, along_z, kept,
-        rest[len(KEPT) + 3 :], phase_new, solute_new,
-    )
-
-
-def far_kernel(coarse_y, size_x, face, corner, fans, matrices, along_z, inner_latent, near_latent, *rest):
-    kept = dict(zip(KEPT, rest[: len(KEPT)]))
-    phase_new, solute_new, keep, send, *scratch, total = rest[len(KEPT) :]
-    mine = rim_steps(
-        coarse_y, total.shape[1], False, size_x, face, corner, fans, matrices, along_z, kept, scratch, phase_new,
-        solute_new,
-    )
-    total[...] = mine + inner_latent[...] + near_latent[...]
+    near_new, far_new, (keep, send) = rest[len(KEPT) :][:2], rest[len(KEPT) :][2:4], rest[len(KEPT) :][4:6]
+    far_phase, far_solute, far_fan, total, *scratch = rest[len(KEPT) + 6 :]
+    _, _, size_y, size_z = face.shape
+    width = total.shape[1]
+    rim_halo(False, face, corner, along_z, far_phase, far_solute, far_fan)
+    changes = []
+    half = len(scratch) // 2
+    sides = [
+        rim_march(True, size_x, (near_phase, near_solute, near_fan), fans, matrices, kept, scratch[:half], *near_new, changes),
+        rim_march(False, size_x, (far_phase, far_solute, far_fan), fans, matrices, kept, scratch[half:], *far_new, changes),
+    ]
+    while sides:
+        sides = [side for side in sides if next(side, sides) is not sides]
+    lanes = [coarse_lane(u, size_x, size_y, coarse_y) for u in (size_x // 4 - 1, 0)]
+    total[...] = restrict(changes, lanes, size_y, size_z, width) + inner_latent[...]
     halve(total, lax.div(2 * lax.axis_index("gy"), lax.axis_size("gy")), keep, send)
 
 
@@ -523,41 +561,26 @@
     send[...] = total[pl.ds(pl.multiple_of((1 - side) * half, half), half), :]
 
 
-def rim_scratch(size_y, size_z):
-    counts = 4, 4, 4, 4, 4, 3, 3, 2, 3, 4
-    return [pltpu.VMEM((count, size_y + 2 * HALO, size_z), F32) for count in counts]
-
-
-def near_rim(shape, face, corner, fans, matrices, along_z, kept, width, coarse_y):
+def rims(shape, face, corner, near, fans, matrices, along_z, inner_latent, kept, coarse_y):
     size_x, size_y, size_z = shape
-    part = jax.ShapeDtypeStruct((HALO, size_y, size_z), F32)
-    return pl.pallas_call(
-        functools.partial(near_kernel, coarse_y, size_x),
-        out_shape=(part, part, jax.ShapeDtypeStruct((size_z // 4, width), F32)),
-        in_specs=[vmem()] * (5 + len(kept)),
-        out_specs=[vmem()] * 3,
-        scratch_shapes=rim_scratch(size_y, size_z),
-        compiler_params=pltpu.CompilerParams(vmem_limit_bytes=VMEM_LIMIT),
-        cost_estimate=pl.CostEstimate(flops=20 * 10**8, bytes_accessed=20 * 10**6, transcendentals=0),
-        name="near",
-    )(face, corner, fans, matrices, along_z, *kept)
-
-
-def far_rim(shape, face, corner, fans, matrices, along_z, inner_latent, near_latent, kept, coarse_y):
-    size_x, size_y, size_z = shape
+    rows = size_y + 2 * HALO
     part = jax.ShapeDtypeStruct((HALO, size_y, size_z), F32)
     width = inner_latent.shape[1]
     half = jax.ShapeDtypeStruct((size_z // 8, width), F32)
-    return pl.pallas_call(
-        functools.partial(far_kernel, coarse_y, size_x),
-        out_shape=(part, part, half, half),
-        in_specs=[vmem()] * (7 + len(kept)),
-        out_specs=[vmem()] * 4,
-        scratch_shapes=[*rim_scratch(size_y, size_z), pltpu.VMEM((size_z // 4, width), F32)],
+    slabs = lambda count: pltpu.VMEM((count, rows, size_z), F32)
+    return pl.pallas_call(
+        functools.partial(rim_kernel, coarse_y, size_x),
+        out_shape=(part, part, part, part, half, half),
+        in_specs=[vmem()] * (9 + len(kept)),
+        out_specs=[vmem()] * 6,
+        scratch_shapes=[
+            slabs(HALO), slabs(HALO), pltpu.VMEM((rows, size_z), F32), pltpu.VMEM((size_z // 4, width), F32),
+            *[slabs(count) for count in 2 * (4, 4, 4, 3, 3, 2, 3, 4)],
+        ],
         compiler_params=pltpu.CompilerParams(vmem_limit_bytes=VMEM_LIMIT),
         cost_estimate=pl.CostEstimate(flops=10**7, bytes_accessed=3 * 10**6, transcendentals=0),
-        name="far",
-    )(face, corner, fans, matrices, along_z, inner_latent, near_latent, *kept)
+        name="rims",
+    )(face, corner, *near, fans, matrices, along_z, inner_latent, *kept)
 
 
 def store_kernel(*refs):
@@ -652,13 +675,11 @@
     corner_b = lax.ppermute(corner_b, "gx", far_x)
     results = inner(phase, solute, side_a, strip_b, rest_b, coarse, matrices, along_z, coarse_y)
     middle, inner_latent, fans, kept = results[:2], results[2], results[3], results[4:]
-    *near, near_latent = near_rim(
-        phase.shape, face_a, corner_a, fans, matrices, along_z, kept, coarse_shape[1], coarse_y
+    near = near_halo(face_a, corner_a, along_z)
+    *edges, mine, send = rims(
+        phase.shape, face_b, corner_b, near, fans, matrices, along_z, inner_latent, kept, coarse_y
     )
-    *far, mine, send = far_rim(
-        phase.shape, face_b, corner_b, fans, matrices, along_z, inner_latent, near_latent, kept, coarse_y
-    )
-    phase_out, solute_out = store(phase.shape, (*middle, *near, *far))
+    phase_out, solute_out = store(phase.shape, (*middle, *edges))
     if ride:
         mine, send = merge(mine, lax.ppermute(send, "gy", across))
         latent = owner(mine, lax.ppermute(send, "gy", near_y), coarse_x, coarse_y)

time: 28.1 us -> 27.3 us (0.972)
  Pallas kernels: 10.3 us -> 9.33 us
    pallas_call x2, Pallas kernels: 2.89 us -> 2.39 us  [the longest x1 2.07 us: rims(): pl.pallas_call(functools.partial(rim_kernel, coarse_y, size_x), out_shape...]
    pallas_call x1, Pallas kernels: 3.61 us -> 3.21 us  [inner(): pl.pallas_call(functools.partial(inner_kernel, coarse_y), out_shape=(part...]
    ppermute x1, starting transfers between devices: 0.55 us -> 0.21 us  [body(): rest_b = lax.ppermute(rest_b, 'gy', far_y)]
  transfers between devices with their start and end apart: 9 -> 9, of which waited for: 3 -> 4; matrix products, arithmetic and copies ran while one was open for 0% -> 0% of each run, Pallas kernels for 24% -> 19%
where the time goes in v5:
time: 27.3 us; the launch traced here: 27.2 us
  starting transfers between devices  14 us (51%)
  Pallas kernels  9.33 us (34%)
  waiting for transfers between devices  3.12 us (11%)
  between operations  0.69 us (3%)
    ppermute x1, starting transfers between devices, body(): face_b = lax.ppermute(face_b, 'gx', far_x)  4.38 us
    ppermute x1, starting transfers between devices, body(): corner_b = lax.ppermute(corner_b, 'gx', far_x)  3.45 us
    pallas_call x1, Pallas kernels, inner(): pl.pallas_call(functools.partial(inner_kernel, coarse_y), out_shape=(part...  3.21 us
    ppermute x1, starting transfers between devices, body(): face_a = lax.ppermute(face_a, 'gx', near_x)  2.59 us
    ppermute x1, waiting for transfers between devices, body(): mine, send = merge(mine, lax.ppermute(send, 'gy', across))  2.22 us
    pallas_call x1, Pallas kernels, rims(): pl.pallas_call(functools.partial(rim_kernel, coarse_y, size_x), out_shape...  2.07 us
    ppermute x1, starting transfers between devices, body(): mine, send = merge(mine, lax.ppermute(send, 'gy', across))  1.58 us
    pallas_call x1, Pallas kernels, pack(): pl.pallas_call(pack_kernel, out_shape=(field, field, face, face, *sides,...  1.5 us
  transfers between devices with their start and end apart: 9, of which 4 were waited for; matrix products, arithmetic and copies ran while one was open for 0% of the time, Pallas kernels for 19%

profile of v5, /device:TPU:0, one launch (start us, length us, event | category | flops | bytes accessed | tf_op | source)
XLA Modules:
  0.0 27.2 jit_solution(4624229002592258034)
XLA Ops:
  0.6 1.5 %pack.1 = (f32[16,32,256]{2,1,0:T(8,128)S(1)}, f32[16,32,256]{2,1,0:T(8,128)S(1)}, f32[2,4,32,256]{3,2,1,0:T(8,128)S(1)}, f32[2,4,32,256]{3,2,1,0:T(8,128)S(1)},...) custom-call(f32[16,32,256]{2,1,0:T(8,128)} %phase.1, ...), custom_call_target="tpu_custom_call" | custom-call | flops 100000 | bytes 2000000 | tf_op jit(solution)/shard_map/pack/pallas_call | solution.py:130
  2.1 0.5 %collective-permute-start = (f32[17,8,256]{2,1,0:T(8,128)S(1)}, f32[17,8,256]{2,1,0:T(8,128)S(1)}, u32[]{:S(2)}, u32[]{:S(2)}) collective-permute-start(f32[17,8,256]{2,1,0:T(8,128)S(1)} %get-tuple-element.51), channel_id=1, source_target_pairs={{0,1},{2,3},{1,0},{3,2},{4,5},{6,7},{5,4},{7,6},{8,9},{10,11},{9,8... | collective-permute-start | bytes 417800 | tf_op jit(solution)/shard_map/ppermute | solution.py:663
  2.7 2.6 %collective-permute-start.5 = (f32[2,4,32,256]{3,2,1,0:T(8,128)S(1)}, f32[2,4,32,256]{3,2,1,0:T(8,128)S(1)}, u32[]{:S(2)}, u32[]{:S(2)}) collective-permute-start(f32[2,4,32,256]{3,2,1,0:T(8,128)S(1)} %get-tuple-element.65), channel_id=1, source_target_pairs={{0,4},{8,12},{16,20},{24,28},{4,0},{12,8},{20,16},{28,24},{1,5},{9... | collective-permute-start | bytes 786440 | tf_op jit(solution)/shard_map/ppermute | solution.py:662
  5.3 0.0 collective-permute-done.arrived.side_a
  5.3 1.3 %collective-permute-start.1 = (f32[10,8,256]{2,1,0:T(8,128)S(1)}, f32[10,8,256]{2,1,0:T(8,128)S(1)}, u32[]{:S(2)}, u32[]{:S(2)}) collective-permute-start(f32[10,8,256]{2,1,0:T(8,128)S(1)} %append.1.tile), channel_id=1, source_target_pairs={{1,2},{3,0},{2,1},{0,3},{5,6},{7,4},{6,5},{4,7},{9,10},{11,8},{10,... | collective-permute-start | bytes 245768 | tf_op jit(solution)/shard_map/ppermute | solution.py:670
  6.5 0.1 products.1
  6.7 4.4 %collective-permute-start.3 = (f32[2,4,32,256]{3,2,1,0:T(8,128)S(1)}, f32[2,4,32,256]{3,2,1,0:T(8,128)S(1)}, u32[]{:S(2)}, u32[]{:S(2)}) collective-permute-start(f32[2,4,32,256]{3,2,1,0:T(8,128)S(1)} %get-tuple-element.63), channel_id=1, source_target_pairs={{4,8},{12,16},{20,24},{28,0},{8,4},{16,12},{24,20},{0,28},{5,9},{1... | collective-permute-start | bytes 786440 | tf_op jit(solution)/shard_map/ppermute | solution.py:672
  11.0 0.2 collective-permute-start.2
  11.3 0.0 collective-permute-done.1.strip_b
  11.3 0.4 %corners.1 = (f32[64,128]{1,0:T(8,128)S(1)}, f32[3,8,256]{2,1,0:T(8,128)S(1)}, f32[3,8,256]{2,1,0:T(8,128)S(1)}) custom-call(f32[17,8,256]{2,1,0:T(8,128)S(1)} %collective-permute-done.arrived.side_a, f32[10,8,256]{2,1,0:T(8,128)S(1)} %collective-permute-done.1.strip_b, f32[16,128]{1,0:T(8,128)S(1)} %get-tuple-element.57.table), custom_call_target="tpu_custom_call" | custom-call | flops 100000 | bytes 400000 | tf_op jit(solution)/shard_map/corners/pallas_call | solution.py:217
  11.6 0.0 collective-permute-start.6
  11.7 3.5 %collective-permute-start.4 = (f32[3,8,256]{2,1,0:T(8,128)S(1)}, f32[3,8,256]{2,1,0:T(8,128)S(1)}, u32[]{:S(2)}, u32[]{:S(2)}) collective-permute-start(f32[3,8,256]{2,1,0:T(8,128)S(1)} %get-tuple-element.64), channel_id=1, source_target_pairs={{4,8},{12,16},{20,24},{28,0},{8,4},{16,12},{24,20},{0,28},{5,9},{1... | collective-permute-start | bytes 73736 | tf_op jit(solution)/shard_map/ppermute | solution.py:675
  15.1 0.1 collective-permute-done.2.rest_b
  15.2 3.2 %inner.1 = (f32[8,32,256]{2,1,0:T(8,128)S(1)}, f32[8,32,256]{2,1,0:T(8,128)S(1)}, f32[64,128]{1,0:T(8,128)S(1)}, f32[2,40,256]{2,1,0:T(8,128)S(1)}, f32[16,40,25...) custom-call(f32[16,32,256]{2,1,0:T(8,128)S(1)} %get-tuple-element.49, ...), custom_call_target="tpu_custom_call" | custom-call | flops 500000000 | bytes 5000000 | tf_op jit(solution)/shard_map/inner/pallas_call | solution.py:435
  18.4 0.6 %collective-permute-done.6.corner = f32[3,8,256]{2,1,0:T(8,128)S(1)} collective-permute-done((f32[3,8,256]{2,1,0:T(8,128)S(1)}, f32[3,8,256]{2,1,0:T(8,128)S(1)}, u32[]{:S(2)}, u32[]{:S(2)}) %collective-permute-start.6) | collective-permute-done | bytes 24608 | tf_op jit(solution)/shard_map/ppermute | solution.py:674
  19.0 0.0 collective-permute-done.5.face
  19.0 0.3 %near.1 = (f32[4,40,256]{2,1,0:T(8,128)S(1)}, f32[4,40,256]{2,1,0:T(8,128)S(1)}, f32[40,256]{1,0:T(8,128)S(1)}) custom-call(f32[2,4,32,256]{3,2,1,0:T(8,128)S(1)} %collective-permute-done.5.face, f32[3,8,256]{2,1,0:T(8,128)S(1)} %collective-permute-done.6.corner, bf16[64,256]{1,0:T(8,128)(2,1)S(1)} %get-tuple-element.60.along_z), custom_call_target="tpu_custom_call" | custom-call | flops 1500000000 | bytes 15000000 | tf_op jit(solution)/shard_map/near/pallas_call | solution.py:525
  19.4 0.0 collective-permute-done.4.corner
  19.4 0.0 collective-permute-done.3.face
  19.4 2.1 %rims.1 = (f32[4,32,256]{2,1,0:T(8,128)S(1)}, f32[4,32,256]{2,1,0:T(8,128)S(1)}, f32[4,32,256]{2,1,0:T(8,128)S(1)}, f32[4,32,256]{2,1,0:T(8,128)S(1)}, f32[32,128]{1,0:T(8,128)S(1)}, /*index=5*/f32[32,128]{1,0:T(8,128)S(1)}) custom-call(f32[2,4,32,256]{3,2,1,0:T(8,128)S(1)} %collective-permute-done.3.face, f32[3,8,256]{2,1,0:T(8,128)S(1)} %collective-permute-done.4.corner, ...), custom_call_target="tpu_custom_call" | custom-call | flops 10000000 | bytes 3000000 | tf_op jit(solution)/shard_map/rims/pallas_call | solution.py:571
  21.5 1.6 %collective-permute-start.7 = (f32[32,128]{1,0:T(8,128)S(1)}, f32[32,128]{1,0:T(8,128)S(1)}, u32[]{:S(2)}, u32[]{:S(2)}) collective-permute-start(f32[32,128]{1,0:T(8,128)S(1)} %get-tuple-element.92), channel_id=1, source_target_pairs={{0,2},{1,3},{2,0},{3,1},{4,6},{5,7},{6,4},{7,5},{8,10},{9,11},{10,... | collective-permute-start | bytes 49160 | tf_op jit(solution)/shard_map/ppermute | solution.py:684
  23.1 2.2 %collective-permute-done.7.arrived = f32[32,128]{1,0:T(8,128)S(1)} collective-permute-done((f32[32,128]{1,0:T(8,128)S(1)}, f32[32,128]{1,0:T(8,128)S(1)}, u32[]{:S(2)}, u32[]{:S(2)}) %collective-permute-start.7) | collective-permute-done | bytes 16416 | tf_op jit(solution)/shard_map/ppermute | solution.py:684
  25.3 0.0 collective-permute-start.8
  25.3 1.0 %store.1 = (f32[16,32,256]{2,1,0:T(8,128)}, f32[16,32,256]{2,1,0:T(8,128)}) custom-call(f32[8,32,256]{2,1,0:T(8,128)S(1)} %get-tuple-element.61.refs_0_, f32[8,32,256]{2,1,0:T(8,128)S(1)} %get-tuple-element.62.refs_1_, f32[4,32,256]{2,1,0:T(8,128)S(1)} %get-tuple-element.85.refs_2_, f32[4,32,256]{2,1,0:T(8,128)S(1)} %get-tuple-element.86.refs_3_, ...), custom_call_target="tpu_custom_call" | custom-call | bytes 4000000 | tf_op jit(solution)/shard_map/store/pallas_call | solution.py:600
  26.3 0.1 collective-permute-done.8.arrived
  26.5 0.7 %owner.1 = f32[4,16,32]{2,1,0:T(8,128)} custom-call(f32[16,128]{1,0:T(8,128)S(1)} %get-tuple-element.93.mine, f32[16,128]{1,0:T(8,128)S(1)} %collective-permute-done.8.arrived), custom_call_target="tpu_custom_call" | custom-call | flops 10000 | bytes 100000 | tf_op jit(solution)/shard_map/owner/pallas_call | solution.py:640
  (2 shorter events, 0.0 us)
Async XLA Ops:
  2.1 3.1 %collective-permute-start = (f32[17,8,256]{2,1,0:T(8,128)S(1)}, f32[17,8,256]{2,1,0:T(8,128)S(1)}, u32[]{:S(2)}, u32[]{:S(2)}) collective-permute-start(f32[17,8,256]{2,1,0:T(8,128)S(1)} %get-tuple-element.51), channel_id=1, source_target_pairs={{0,1},{2,3},{1,0},{3,2},{4,5},{6,7},{5,4},{7,6},{8,9},{10,11},{9,8... | collective-permute-start | bytes 417800 | tf_op jit(solution)/shard_map/ppermute | solution.py:663
  2.7 16.4 %collective-permute-start.5 = (f32[2,4,32,256]{3,2,1,0:T(8,128)S(1)}, f32[2,4,32,256]{3,2,1,0:T(8,128)S(1)}, u32[]{:S(2)}, u32[]{:S(2)}) collective-permute-start(f32[2,4,32,256]{3,2,1,0:T(8,128)S(1)} %get-tuple-element.65), channel_id=1, source_target_pairs={{0,4},{8,12},{16,20},{24,28},{4,0},{12,8},{20,16},{28,24},{1,5},{9... | collective-permute-start | bytes 786440 | tf_op jit(solution)/shard_map/ppermute | solution.py:662
  5.3 6.0 %collective-permute-start.1 = (f32[10,8,256]{2,1,0:T(8,128)S(1)}, f32[10,8,256]{2,1,0:T(8,128)S(1)}, u32[]{:S(2)}, u32[]{:S(2)}) collective-permute-start(f32[10,8,256]{2,1,0:T(8,128)S(1)} %append.1.tile), channel_id=1, source_target_pairs={{1,2},{3,0},{2,1},{0,3},{5,6},{7,4},{6,5},{4,7},{9,10},{11,8},{10,... | collective-permute-start | bytes 245768 | tf_op jit(solution)/shard_map/ppermute | solution.py:670
  6.7 12.7 %collective-permute-start.3 = (f32[2,4,32,256]{3,2,1,0:T(8,128)S(1)}, f32[2,4,32,256]{3,2,1,0:T(8,128)S(1)}, u32[]{:S(2)}, u32[]{:S(2)}) collective-permute-start(f32[2,4,32,256]{3,2,1,0:T(8,128)S(1)} %get-tuple-element.63), channel_id=1, source_target_pairs={{4,8},{12,16},{20,24},{28,0},{8,4},{16,12},{24,20},{0,28},{5,9},{1... | collective-permute-start | bytes 786440 | tf_op jit(solution)/shard_map/ppermute | solution.py:672
  11.0 4.1 %collective-permute-start.2 = (f32[8,8,256]{2,1,0:T(8,128)S(1)}, f32[8,8,256]{2,1,0:T(8,128)S(1)}, u32[]{:S(2)}, u32[]{:S(2)}) collective-permute-start(f32[8,8,256]{2,1,0:T(8,128)S(1)} %get-tuple-element.56), channel_id=1, source_target_pairs={{1,2},{3,0},{2,1},{0,3},{5,6},{7,4},{6,5},{4,7},{9,10},{11,8},{10,... | collective-permute-start | bytes 196616 | tf_op jit(solution)/shard_map/ppermute | solution.py:671
  11.6 7.4 %collective-permute-start.6 = (f32[3,8,256]{2,1,0:T(8,128)S(1)}, f32[3,8,256]{2,1,0:T(8,128)S(1)}, u32[]{:S(2)}, u32[]{:S(2)}) collective-permute-start(f32[3,8,256]{2,1,0:T(8,128)S(1)} %get-tuple-element.66), channel_id=1, source_target_pairs={{0,4},{8,12},{16,20},{24,28},{4,0},{12,8},{20,16},{28,24},{1,5},{9... | collective-permute-start | bytes 73736 | tf_op jit(solution)/shard_map/ppermute | solution.py:674
  11.7 7.7 %collective-permute-start.4 = (f32[3,8,256]{2,1,0:T(8,128)S(1)}, f32[3,8,256]{2,1,0:T(8,128)S(1)}, u32[]{:S(2)}, u32[]{:S(2)}) collective-permute-start(f32[3,8,256]{2,1,0:T(8,128)S(1)} %get-tuple-element.64), channel_id=1, source_target_pairs={{4,8},{12,16},{20,24},{28,0},{8,4},{16,12},{24,20},{0,28},{5,9},{1... | collective-permute-start | bytes 73736 | tf_op jit(solution)/shard_map/ppermute | solution.py:675
  21.5 3.8 %collective-permute-start.7 = (f32[32,128]{1,0:T(8,128)S(1)}, f32[32,128]{1,0:T(8,128)S(1)}, u32[]{:S(2)}, u32[]{:S(2)}) collective-permute-start(f32[32,128]{1,0:T(8,128)S(1)} %get-tuple-element.92), channel_id=1, source_target_pairs={{0,2},{1,3},{2,0},{3,1},{4,6},{5,7},{6,4},{7,5},{8,10},{9,11},{10,... | collective-permute-start | bytes 49160 | tf_op jit(solution)/shard_map/ppermute | solution.py:684
  25.3 1.2 %collective-permute-start.8 = (f32[16,128]{1,0:T(8,128)S(1)}, f32[16,128]{1,0:T(8,128)S(1)}, u32[]{:S(2)}, u32[]{:S(2)}) collective-permute-start(f32[16,128]{1,0:T(8,128)S(1)} %get-tuple-element.94), channel_id=1, source_target_pairs={{0,1},{2,3},{1,0},{3,2},{4,5},{6,7},{5,4},{7,6},{8,9},{10,11},{9,8... | collective-permute-start | bytes 24584 | tf_op jit(solution)/shard_map/ppermute | solution.py:685

commit v6 on v5

--- a/solution.py
+++ b/solution.py
@@ -297,6 +297,18 @@
     return product(slabs.reshape(-1, slabs.shape[-1]), matrix, (1, 0)).reshape(slabs.shape)
 
 
+def z_difference(value, clamp):
+    first, second = value[:, :LANES], value[:, LANES:]
+    lane = lane_ids(first.shape)
+    head, tail = lane == 0, lane == LANES - 1
+    ends = (first, second) if clamp else (0.0, 0.0)
+    ahead = turn(first, -1, 1), turn(second, -1, 1)
+    behind = turn(first, 1, 1), turn(second, 1, 1)
+    low = jnp.where(tail, ahead[1], ahead[0]) - jnp.where(head, ends[0], behind[0])
+    high = jnp.where(tail, ends[1], ahead[1]) - jnp.where(head, behind[0], behind[1])
+    return jnp.concatenate([low, high], axis=1)
+
+
 def flux(before, here, after, along_z):
     along_x = after - before
     along_y = turn(here, -1, 0) - turn(here, 1, 0)
@@ -328,13 +340,13 @@
 
 
 def restrict(changes, lanes, size_y, size_z, coarse_width):
-    shape = (size_z // 4, size_z)
-    pool_z = (lane_ids(shape) // 4 == row_ids(shape)).astype(F32).astype(jnp.bfloat16)
+    shape = (size_z, size_z // 4)
+    pool_z = (row_ids(shape) // 4 == lane_ids(shape)).astype(F32).astype(jnp.bfloat16)
     shape = (size_y, coarse_width)
     cell, lane = row_ids(shape) // 4, lane_ids(shape)
     pool_y = [jnp.where(cell + at == lane, 0.5 / 64.0, 0.0).astype(jnp.bfloat16) for at in lanes]
-    pooled = product(pool_z, jnp.concatenate(changes, axis=0), (1, 1))
-    return product(pooled, jnp.concatenate(pool_y, axis=0), (1, 0))
+    pooled = product(jnp.concatenate(changes, axis=0), pool_z, (1, 0))
+    return product(pooled, jnp.concatenate(pool_y, axis=0), (0, 0))
 
 
 def coarse_lane(u, size_x, size_y, coarse_y):
@@ -444,7 +456,7 @@
     )(phase, solute, side_a, strip_b, rest_b, coarse, matrices, along_z)
 
 
-def rim_halo(near, face, corner, along_z, phase_halo, solute_halo, fan):
+def rim_halo(near, face, corner, phase_halo, solute_halo):
     _, _, size_y, size_z = face.shape
     odd_x = lax.rem(lax.axis_index("gx"), 2)
     flip = odd_x if near else 1 - odd_x
@@ -454,18 +466,25 @@
         for n, (field, rows) in enumerate(((phase_halo, p_rows), (solute_halo, c_rows))):
             field[HALO - 1 - d, pl.ds(0, size_y), :] = face[n, layer]
             field[HALO - 1 - d, pl.ds(size_y, ROWS), :] = rows
+
+
+def edge_fan(corner, along_z, size_y):
     edge = jnp.where(row_ids(corner.shape[1:]) < 2, corner[0], pltpu.roll(corner[1], 4, 0))
-    fan[...] = interpolate(unpack_edge(edge), along_z[...], size_y)[0]
-
-
-def rim_march(near, size_x, halo, fans, matrices, kept, scratch, phase_new, solute_new, result):
+    return interpolate(unpack_edge(edge), along_z[...], size_y)[0]
+
+
+def rim_spot(near):
+    odd_x = lax.rem(lax.axis_index("gx"), 2)
+    flip = odd_x if near else 1 - odd_x
+    return lambda v: v + (1 - flip) * (HALO - 1 - 2 * v)
+
+
+def rim_march(near, size_x, halo, fans, matrices, kept, scratch, p1, c1, phase_new, result):
     hp0, hc0, fan = halo
-    p1, c1, gx, dv, dz, cz, fz, th = scratch
+    gx, dv, dz, cz, th = scratch
     _, size_y, size_z = phase_new.shape
     span = spans(size_x)
-    odd_x = lax.rem(lax.axis_index("gx"), 2)
-    flip = odd_x if near else 1 - odd_x
-    spot = lambda v: v + (1 - flip) * (HALO - 1 - 2 * v)
+    spot = rim_spot(near)
 
     def get(name, v):
         begin, end = span[name]
@@ -474,79 +493,77 @@
             return -found if near and name.startswith("gx") else found
         own, first = dict(
             p0=(hp0, -4), c0=(hc0, -4), dz0=(dz, -3), cz0=(cz, -2), gx0=(gx, -3), dv0=(dv, -2),
-            p1=(p1, -2), c1=(c1, -2), dz1=(dz, -1), cz1=(cz, 0), gx1=(gx, -1), dv1=(dv, 0), th=(th, -2),
+            p1=(p1, -2), c1=(c1, -2), dz1=(dz, -1), gx1=(gx, -1), dv1=(dv, 0), th=(th, -2),
         )[name]
         return own[v - first]
 
-    ends = {-1: fan[...], 0: fans[1 if near else 0]}
+    moved = []
+    ends = {-1: fan, 0: fans[1 if near else 0]}
     for v in range(-2, 2):
         th[v + 2] = blend(v, ends)
     for step, begin in (("0", -3), ("1", -1)):
         p, c, gx_, dv_, dz_, cz_ = (name + step for name in ("p", "c", "gx", "dv", "dz", "cz"))
-        fields = (hp0[pl.ds(1, 3)], hc0[pl.ds(2, 2)]) if step == "0" else (p1[pl.ds(1, 3)], c1[pl.ds(2, 2)])
-        dz[...] = along(fields[0], matrices[0])
-        cz[...] = along(fields[1], matrices[2])
+        for n in range(3):
+            dz[n] = z_difference((hp0 if step == "0" else p1)[n + 1], True)
+        if step == "0":
+            cz[...] = along(hc0[pl.ds(2, 2)], matrices[2])
         yield
         for v in range(begin, begin + 4):
             flux_x, flux_y, flux_z = flux(get(p, v - 1), get(p, v), get(p, v + 1), get(dz_, v))
             gx[v - begin] = flux_x
             if v > begin:
-                dv[v - begin - 1] = spread(flux_y)
-                fz[v - begin - 1] = flux_z
-        yield
-        dv[...] += along(fz[...], matrices[1])
+                dv[v - begin - 1] = spread(flux_y) + z_difference(flux_z, False)
         yield
         take = (lambda w: w) if step == "0" else (lambda w: w[:size_y])
         for v in range(begin + 1, begin + 5):
             here, conc = take(get(p, v)), get(c, v)
             divergence = take(get(gx_, v + 1)) - take(get(gx_, v - 1)) + take(get(dv_, v))
             change = phase_change(here, take(conc), take(get("th", v)), divergence)
-            beyond = take(get(c, v + 2)) + take(get(c, v - 2))
-            new_conc = solute_step(take(conc), beyond, take(next_row(conc)), take(get(cz_, v)), change)
             if step == "0":
-                p1[v + 2], c1[v + 2] = here + change, new_conc
+                beyond = get(c, v + 2) + get(c, v - 2)
+                p1[v + 2] = here + change
+                c1[v + 2] = solute_step(conc, beyond, next_row(conc), get(cz_, v), change)
             else:
-                phase_new[spot(v)], solute_new[spot(v)] = here + change, new_conc
+                phase_new[spot(v)] = here + change
+                moved.append(here + change - get("p0", v)[:size_y])
         yield
-    change = jnp.zeros((size_y, size_z), F32)
-    for v in range(HALO):
-        change = change + (phase_new[spot(v)] - get("p0", v)[:size_y])
-    result.append(change)
-
-
-def near_kernel(face, corner, along_z, phase_halo, solute_halo, fan):
-    rim_halo(True, face, corner, along_z, phase_halo, solute_halo, fan)
-
-
-def near_halo(face, corner, along_z):
+    result.append((moved[0] + moved[1]) + (moved[2] + moved[3]))
+
+
+def near_kernel(face, corner, phase_halo, solute_halo):
+    rim_halo(True, face, corner, phase_halo, solute_halo)
+
+
+def near_halo(face, corner):
     _, _, size_y, size_z = face.shape
-    rows = size_y + 2 * HALO
-    slabs = jax.ShapeDtypeStruct((HALO, rows, size_z), F32)
+    slabs = jax.ShapeDtypeStruct((HALO, size_y + 2 * HALO, size_z), F32)
     return pl.pallas_call(
         near_kernel,
-        out_shape=(slabs, slabs, jax.ShapeDtypeStruct((rows, size_z), F32)),
-        in_specs=[vmem()] * 3,
-        out_specs=[vmem()] * 3,
+        out_shape=(slabs, slabs),
+        in_specs=[vmem()] * 2,
+        out_specs=[vmem()] * 2,
         compiler_params=pltpu.CompilerParams(vmem_limit_bytes=VMEM_LIMIT),
         cost_estimate=pl.CostEstimate(flops=15 * 10**8, bytes_accessed=15 * 10**6, transcendentals=0),
         name="near",
-    )(face, corner, along_z)
+    )(face, corner)
 
 
 def rim_kernel(
-    coarse_y, size_x, face, corner, near_phase, near_solute, near_fan, fans, matrices, along_z, inner_latent, *rest
+    coarse_y, size_x, face, corner, near_phase, near_solute, near_corner, fans, matrices, along_z, inner_latent, *rest
 ):
     kept = dict(zip(KEPT, rest[: len(KEPT)]))
-    near_new, far_new, (keep, send) = rest[len(KEPT) :][:2], rest[len(KEPT) :][2:4], rest[len(KEPT) :][4:6]
-    far_phase, far_solute, far_fan, total, *scratch = rest[len(KEPT) + 6 :]
+    outs, (far_phase, far_solute, total, *scratch) = rest[len(KEPT) : len(KEPT) + 8], rest[len(KEPT) + 8 :]
+    near_new, far_new, keep, send = outs[:3], outs[3:6], outs[6], outs[7]
     _, _, size_y, size_z = face.shape
     width = total.shape[1]
-    rim_halo(False, face, corner, along_z, far_phase, far_solute, far_fan)
+    rim_halo(False, face, corner, far_phase, far_solute)
     changes = []
     half = len(scratch) // 2
+    near = near_phase, near_solute, edge_fan(near_corner, along_z, size_y)
+    far = far_phase, far_solute, edge_fan(corner, along_z, size_y)
     sides = [
-        rim_march(True, size_x, (near_phase, near_solute, near_fan), fans, matrices, kept, scratch[:half], *near_new, changes),
-        rim_march(False, size_x, (far_phase, far_solute, far_fan), fans, matrices, kept, scratch[half:], *far_new, changes),
+        rim_march(True, size_x, near, fans, matrices, kept, scratch[:half], *near_new, changes),
+        rim_march(False, size_x, far, fans, matrices, kept, scratch[half:], *far_new, changes),
     ]
     while sides:
         sides = [side for side in sides if next(side, sides) is not sides]
@@ -567,15 +584,16 @@
     part = jax.ShapeDtypeStruct((HALO, size_y, size_z), F32)
     width = inner_latent.shape[1]
     half = jax.ShapeDtypeStruct((size_z // 8, width), F32)
+    state = jax.ShapeDtypeStruct((HALO, rows, size_z), F32)
     slabs = lambda count: pltpu.VMEM((count, rows, size_z), F32)
     return pl.pallas_call(
         functools.partial(rim_kernel, coarse_y, size_x),
-        out_shape=(part, part, part, part, half, half),
+        out_shape=(state, state, part, state, state, part, half, half),
         in_specs=[vmem()] * (9 + len(kept)),
-        out_specs=[vmem()] * 6,
+        out_specs=[vmem()] * 8,
         scratch_shapes=[
-            slabs(HALO), slabs(HALO), pltpu.VMEM((rows, size_z), F32), pltpu.VMEM((size_z // 4, width), F32),
-            *[slabs(count) for count in 2 * (4, 4, 4, 3, 3, 2, 3, 4)],
+            slabs(HALO), slabs(HALO), pltpu.VMEM((size_z // 4, width), F32),
+            *[slabs(count) for count in 2 * (4, 3, 3, 2, 4)],
         ],
         compiler_params=pltpu.CompilerParams(vmem_limit_bytes=VMEM_LIMIT),
         cost_estimate=pl.CostEstimate(flops=10**7, bytes_accessed=3 * 10**6, transcendentals=0),
@@ -583,30 +601,66 @@
     )(face, corner, *near, fans, matrices, along_z, inner_latent, *kept)
 
 
-def store_kernel(*refs):
-    parts, (phase_out, solute_out, sems) = refs[:6], refs[6:]
+def rim_solute(near, size_x, p1, c1, phase_new, matrices, kept, out):
+    _, size_y, size_z = phase_new.shape
+    span = spans(size_x)
+    spot = rim_spot(near)
+    own = {"p1": p1[...], "c1": c1[...], "cz1": along(c1[pl.ds(2, 2)], matrices[2])}
+
+    def get(name, v):
+        begin, _ = span[name]
+        if v >= begin:
+            return kept[name][(size_x - 1 - v if near else v) - begin]
+        return own[name][v if name == "cz1" else v + 2]
+
+    for v in range(HALO):
+        conc = get("c1", v)
+        change = phase_new[spot(v)] - get("p1", v)[:size_y]
+        beyond = get("c1", v + 2)[:size_y] + get("c1", v - 2)[:size_y]
+        out[spot(v)] = solute_step(
+            conc[:size_y], beyond, next_row(conc)[:size_y], get("cz1", v)[:size_y], change
+        )
+
+
+def store_kernel(
+    middle_phase, middle_solute, near_p1, near_c1, near_phase, far_p1, far_c1, far_phase, matrices, p1, c1, cz1,
+    phase_out, solute_out, near_solute, far_solute, sems,
+):
     size_x = phase_out.shape[0]
     odd_x = lax.rem(lax.axis_index("gx"), 2)
     near = (1 - odd_x) * (size_x - HALO)
-    copies = []
-    for begin, pair in ((HALO, parts[:2]), (near, parts[2:4]), (size_x - HALO - near, parts[4:])):
-        for part, out in zip(pair, (phase_out, solute_out)):
-            copies.append((part, out.at[pl.ds(begin, part.shape[0])]))
-    wait_all(start_all(copies, sems))
-
-
-def store(shape, parts):
+    far = size_x - HALO - near
+    put = lambda part, out, at: (part, out.at[pl.ds(at, part.shape[0])])
+    copies = start_all(
+        [
+            put(middle_phase, phase_out, HALO), put(middle_solute, solute_out, HALO), put(near_phase, phase_out, near),
+            put(far_phase, phase_out, far),
+        ],
+        sems,
+    )
+    kept = dict(p1=p1, c1=c1, cz1=cz1)
+    rim_solute(True, size_x, near_p1, near_c1, near_phase, matrices, kept, near_solute)
+    rim_solute(False, size_x, far_p1, far_c1, far_phase, matrices, kept, far_solute)
+    copies += start_all(
+        [put(near_solute, solute_out, near), put(far_solute, solute_out, far)], sems.at[pl.ds(4, 2)]
+    )
+    wait_all(copies)
+
+
+def store(shape, middle, edges, matrices, kept):
+    kept = dict(zip(KEPT, kept))
     out = jax.ShapeDtypeStruct(shape, F32)
+    part = pltpu.VMEM((HALO, *shape[1:]), F32)
     return pl.pallas_call(
         store_kernel,
         out_shape=(out, out),
-        in_specs=[vmem()] * 6,
+        in_specs=[vmem()] * 12,
         out_specs=[hbm()] * 2,
-        scratch_shapes=[pltpu.SemaphoreType.DMA((6,))],
+        scratch_shapes=[part, part, pltpu.SemaphoreType.DMA((6,))],
         compiler_params=pltpu.CompilerParams(vmem_limit_bytes=VMEM_LIMIT),
         cost_estimate=pl.CostEstimate(flops=0, bytes_accessed=4 * 10**6, transcendentals=0),
         name="store",
-    )(*parts)
+    )(*middle, *edges, matrices, kept["p1"], kept["c1"], kept["cz1"])
 
 
 def merge_kernel(mine, arrived, keep, send, total):
@@ -675,11 +729,11 @@
     corner_b = lax.ppermute(corner_b, "gx", far_x)
     results = inner(phase, solute, side_a, strip_b, rest_b, coarse, matrices, along_z, coarse_y)
     middle, inner_latent, fans, kept = results[:2], results[2], results[3], results[4:]
-    near = near_halo(face_a, corner_a, along_z)
+    near = (*near_halo(face_a, corner_a), corner_a)
     *edges, mine, send = rims(
         phase.shape, face_b, corner_b, near, fans, matrices, along_z, inner_latent, kept, coarse_y
     )
-    phase_out, solute_out = store(phase.shape, (*middle, *edges))
+    phase_out, solute_out = store(phase.shape, middle, edges, matrices, kept)
     if ride:
         mine, send = merge(mine, lax.ppermute(send, "gy", across))
         latent = owner(mine, lax.ppermute(send, "gy", near_y), coarse_x, coarse_y)

time: 27.3 us -> 26.5 us (0.971)
  Pallas kernels: 9.33 us -> 8.64 us
    pallas_call x1, Pallas kernels: 2.07 us -> 1.62 us  [rims(): pl.pallas_call(functools.partial(rim_kernel, coarse_y, size_x), out_shape...]
  transfers between devices with their start and end apart: 9 -> 9, of which waited for: 4 -> 4; matrix products, arithmetic and copies ran while one was open for 0% -> 0% of each run, Pallas kernels for 19% -> 18%
where the time goes in v6:
time: 26.5 us; the launch traced here: 26.4 us
  starting transfers between devices  14 us (53%)
  Pallas kernels  8.64 us (33%)
  waiting for transfers between devices  3.06 us (12%)
  between operations  0.69 us (3%)
    ppermute x1, starting transfers between devices, body(): face_b = lax.ppermute(face_b, 'gx', far_x)  4.38 us
    ppermute x1, starting transfers between devices, body(): corner_b = lax.ppermute(corner_b, 'gx', far_x)  3.45 us
    pallas_call x1, Pallas kernels, inner(): pl.pallas_call(functools.partial(inner_kernel, coarse_y), out_shape=(part...  3.24 us
    ppermute x1, starting transfers between devices, body(): face_a = lax.ppermute(face_a, 'gx', near_x)  2.59 us
    ppermute x1, waiting for transfers between devices, body(): mine, send = merge(mine, lax.ppermute(send, 'gy', across))  2.23 us
    pallas_call x1, Pallas kernels, rims(): pl.pallas_call(functools.partial(rim_kernel, coarse_y, size_x), out_shape...  1.62 us
    ppermute x1, starting transfers between devices, body(): mine, send = merge(mine, lax.ppermute(send, 'gy', across))  1.58 us
    pallas_call x1, Pallas kernels, pack(): pl.pallas_call(pack_kernel, out_shape=(field, field, face, face, *sides,...  1.51 us
  transfers between devices with their start and end apart: 9, of which 4 were waited for; matrix products, arithmetic and copies ran while one was open for 0% of the time, Pallas kernels for 18%

profile of v6, /device:TPU:0, one launch (start us, length us, event | category | flops | bytes accessed | tf_op | source)
XLA Modules:
  0.0 26.4 jit_solution(17733419873780030054)
XLA Ops:
  0.6 1.5 %pack.1 = (f32[16,32,256]{2,1,0:T(8,128)S(1)}, f32[16,32,256]{2,1,0:T(8,128)S(1)}, f32[2,4,32,256]{3,2,1,0:T(8,128)S(1)}, f32[2,4,32,256]{3,2,1,0:T(8,128)S(1)},...) custom-call(f32[16,32,256]{2,1,0:T(8,128)} %phase.1, ...), custom_call_target="tpu_custom_call" | custom-call | flops 100000 | bytes 2000000 | tf_op jit(solution)/shard_map/pack/pallas_call | solution.py:130
  2.1 0.5 %collective-permute-start = (f32[17,8,256]{2,1,0:T(8,128)S(1)}, f32[17,8,256]{2,1,0:T(8,128)S(1)}, u32[]{:S(2)}, u32[]{:S(2)}) collective-permute-start(f32[17,8,256]{2,1,0:T(8,128)S(1)} %get-tuple-element.52), channel_id=1, source_target_pairs={{0,1},{2,3},{1,0},{3,2},{4,5},{6,7},{5,4},{7,6},{8,9},{10,11},{9,8... | collective-permute-start | bytes 417800 | tf_op jit(solution)/shard_map/ppermute | solution.py:717
  2.7 2.6 %collective-permute-start.5 = (f32[2,4,32,256]{3,2,1,0:T(8,128)S(1)}, f32[2,4,32,256]{3,2,1,0:T(8,128)S(1)}, u32[]{:S(2)}, u32[]{:S(2)}) collective-permute-start(f32[2,4,32,256]{3,2,1,0:T(8,128)S(1)} %get-tuple-element.66), channel_id=1, source_target_pairs={{0,4},{8,12},{16,20},{24,28},{4,0},{12,8},{20,16},{28,24},{1,5},{9... | collective-permute-start | bytes 786440 | tf_op jit(solution)/shard_map/ppermute | solution.py:716
  5.3 0.0 collective-permute-done.arrived.side_a
  5.3 1.3 %collective-permute-start.1 = (f32[10,8,256]{2,1,0:T(8,128)S(1)}, f32[10,8,256]{2,1,0:T(8,128)S(1)}, u32[]{:S(2)}, u32[]{:S(2)}) collective-permute-start(f32[10,8,256]{2,1,0:T(8,128)S(1)} %append.1.tile), channel_id=1, source_target_pairs={{1,2},{3,0},{2,1},{0,3},{5,6},{7,4},{6,5},{4,7},{9,10},{11,8},{10,... | collective-permute-start | bytes 245768 | tf_op jit(solution)/shard_map/ppermute | solution.py:724
  6.5 0.1 products.1
  6.7 4.4 %collective-permute-start.3 = (f32[2,4,32,256]{3,2,1,0:T(8,128)S(1)}, f32[2,4,32,256]{3,2,1,0:T(8,128)S(1)}, u32[]{:S(2)}, u32[]{:S(2)}) collective-permute-start(f32[2,4,32,256]{3,2,1,0:T(8,128)S(1)} %get-tuple-element.64), channel_id=1, source_target_pairs={{4,8},{12,16},{20,24},{28,0},{8,4},{16,12},{24,20},{0,28},{5,9},{1... | collective-permute-start | bytes 786440 | tf_op jit(solution)/shard_map/ppermute | solution.py:726
  11.1 0.2 collective-permute-start.2
  11.3 0.0 collective-permute-done.1.strip_b
  11.3 0.4 %corners.1 = (f32[64,128]{1,0:T(8,128)S(1)}, f32[3,8,256]{2,1,0:T(8,128)S(1)}, f32[3,8,256]{2,1,0:T(8,128)S(1)}) custom-call(f32[17,8,256]{2,1,0:T(8,128)S(1)} %collective-permute-done.arrived.side_a, f32[10,8,256]{2,1,0:T(8,128)S(1)} %collective-permute-done.1.strip_b, f32[16,128]{1,0:T(8,128)S(1)} %get-tuple-element.58.table), custom_call_target="tpu_custom_call" | custom-call | flops 100000 | bytes 400000 | tf_op jit(solution)/shard_map/corners/pallas_call | solution.py:217
  11.6 0.0 collective-permute-start.6
  11.7 3.5 %collective-permute-start.4 = (f32[3,8,256]{2,1,0:T(8,128)S(1)}, f32[3,8,256]{2,1,0:T(8,128)S(1)}, u32[]{:S(2)}, u32[]{:S(2)}) collective-permute-start(f32[3,8,256]{2,1,0:T(8,128)S(1)} %get-tuple-element.65), channel_id=1, source_target_pairs={{4,8},{12,16},{20,24},{28,0},{8,4},{16,12},{24,20},{0,28},{5,9},{1... | collective-permute-start | bytes 73736 | tf_op jit(solution)/shard_map/ppermute | solution.py:729
  15.1 0.1 collective-permute-done.2.rest_b
  15.2 3.2 %inner.1 = (f32[8,32,256]{2,1,0:T(8,128)S(1)}, f32[8,32,256]{2,1,0:T(8,128)S(1)}, f32[64,128]{1,0:T(8,128)S(1)}, f32[2,40,256]{2,1,0:T(8,128)S(1)}, f32[16,40,25...) custom-call(f32[16,32,256]{2,1,0:T(8,128)S(1)} %get-tuple-element.50, ...), custom_call_target="tpu_custom_call" | custom-call | flops 500000000 | bytes 5000000 | tf_op jit(solution)/shard_map/inner/pallas_call | solution.py:447
  18.4 0.6 %collective-permute-done.6.corner.near_corner = f32[3,8,256]{2,1,0:T(8,128)S(1)} collective-permute-done((f32[3,8,256]{2,1,0:T(8,128)S(1)}, f32[3,8,256]{2,1,0:T(8,128)S(1)}, u32[]{:S(2)}, u32[]{:S(2)}) %collective-permute-start.6) | collective-permute-done | bytes 24608 | tf_op jit(solution)/shard_map/ppermute | solution.py:728
  19.0 0.0 collective-permute-done.5.face
  19.1 0.0 collective-permute-done.4.corner
  19.1 0.0 collective-permute-done.3.face
  19.1 1.6 %rims.1 = (f32[4,40,256]{2,1,0:T(8,128)S(1)}, f32[4,40,256]{2,1,0:T(8,128)S(1)}, f32[4,32,256]{2,1,0:T(8,128)S(1)}, f32[4,40,256]{2,1,0:T(8,128)S(1)}, f32[4,40,...) custom-call(f32[2,4,32,256]{3,2,1,0:T(8,128)S(1)} %collective-permute-done.3.face, ...), custom_call_target="tpu_custom_call" | custom-call | flops 10000000 | bytes 3000000 | tf_op jit(solution)/shard_map/rims/pallas_call | solution.py:589
  20.7 1.6 %collective-permute-start.7 = (f32[32,128]{1,0:T(8,128)S(1)}, f32[32,128]{1,0:T(8,128)S(1)}, u32[]{:S(2)}, u32[]{:S(2)}) collective-permute-start(f32[32,128]{1,0:T(8,128)S(1)} %get-tuple-element.94), channel_id=1, source_target_pairs={{0,2},{1,3},{2,0},{3,1},{4,6},{5,7},{6,4},{7,5},{8,10},{9,11},{10,... | collective-permute-start | bytes 49160 | tf_op jit(solution)/shard_map/ppermute | solution.py:738
  22.3 2.2 %collective-permute-done.7.arrived = f32[32,128]{1,0:T(8,128)S(1)} collective-permute-done((f32[32,128]{1,0:T(8,128)S(1)}, f32[32,128]{1,0:T(8,128)S(1)}, u32[]{:S(2)}, u32[]{:S(2)}) %collective-permute-start.7) | collective-permute-done | bytes 16416 | tf_op jit(solution)/shard_map/ppermute | solution.py:738
  24.5 0.0 collective-permute-start.8
  24.5 1.0 %store.1 = (f32[16,32,256]{2,1,0:T(8,128)}, f32[16,32,256]{2,1,0:T(8,128)}) custom-call(f32[8,32,256]{2,1,0:T(8,128)S(1)} %get-tuple-element.62.middle_phase, f32[8,32,256]{2,1,0:T(8,128)S(1)} %get-tuple-element.63.middle_solute, f32[4,40,256]{2,1,0:T(8,128)S(1)} %get-tuple-element.85.near_p1, f32[4,40,256]{2,1,0:T(8,128)S(1)} %get-tuple-element.86.near_c1, ...), custom_call_target="tpu_custom_call" | custom-call | bytes 4000000 | tf_op jit(solution)/shard_map/store/pallas_call | solution.py:654
  25.6 0.1 collective-permute-done.8.arrived
  25.7 0.7 %owner.1 = f32[4,16,32]{2,1,0:T(8,128)} custom-call(f32[16,128]{1,0:T(8,128)S(1)} %get-tuple-element.95.mine, f32[16,128]{1,0:T(8,128)S(1)} %collective-permute-done.8.arrived), custom_call_target="tpu_custom_call" | custom-call | flops 10000 | bytes 100000 | tf_op jit(solution)/shard_map/owner/pallas_call | solution.py:694
  (3 shorter events, 0.0 us)
Async XLA Ops:
  2.1 3.1 %collective-permute-start = (f32[17,8,256]{2,1,0:T(8,128)S(1)}, f32[17,8,256]{2,1,0:T(8,128)S(1)}, u32[]{:S(2)}, u32[]{:S(2)}) collective-permute-start(f32[17,8,256]{2,1,0:T(8,128)S(1)} %get-tuple-element.52), channel_id=1, source_target_pairs={{0,1},{2,3},{1,0},{3,2},{4,5},{6,7},{5,4},{7,6},{8,9},{10,11},{9,8... | collective-permute-start | bytes 417800 | tf_op jit(solution)/shard_map/ppermute | solution.py:717
  2.7 16.4 %collective-permute-start.5 = (f32[2,4,32,256]{3,2,1,0:T(8,128)S(1)}, f32[2,4,32,256]{3,2,1,0:T(8,128)S(1)}, u32[]{:S(2)}, u32[]{:S(2)}) collective-permute-start(f32[2,4,32,256]{3,2,1,0:T(8,128)S(1)} %get-tuple-element.66), channel_id=1, source_target_pairs={{0,4},{8,12},{16,20},{24,28},{4,0},{12,8},{20,16},{28,24},{1,5},{9... | collective-permute-start | bytes 786440 | tf_op jit(solution)/shard_map/ppermute | solution.py:716
  5.3 6.0 %collective-permute-start.1 = (f32[10,8,256]{2,1,0:T(8,128)S(1)}, f32[10,8,256]{2,1,0:T(8,128)S(1)}, u32[]{:S(2)}, u32[]{:S(2)}) collective-permute-start(f32[10,8,256]{2,1,0:T(8,128)S(1)} %append.1.tile), channel_id=1, source_target_pairs={{1,2},{3,0},{2,1},{0,3},{5,6},{7,4},{6,5},{4,7},{9,10},{11,8},{10,... | collective-permute-start | bytes 245768 | tf_op jit(solution)/shard_map/ppermute | solution.py:724
  6.7 12.4 %collective-permute-start.3 = (f32[2,4,32,256]{3,2,1,0:T(8,128)S(1)}, f32[2,4,32,256]{3,2,1,0:T(8,128)S(1)}, u32[]{:S(2)}, u32[]{:S(2)}) collective-permute-start(f32[2,4,32,256]{3,2,1,0:T(8,128)S(1)} %get-tuple-element.64), channel_id=1, source_target_pairs={{4,8},{12,16},{20,24},{28,0},{8,4},{16,12},{24,20},{0,28},{5,9},{1... | collective-permute-start | bytes 786440 | tf_op jit(solution)/shard_map/ppermute | solution.py:726
  11.1 4.1 %collective-permute-start.2 = (f32[8,8,256]{2,1,0:T(8,128)S(1)}, f32[8,8,256]{2,1,0:T(8,128)S(1)}, u32[]{:S(2)}, u32[]{:S(2)}) collective-permute-start(f32[8,8,256]{2,1,0:T(8,128)S(1)} %get-tuple-element.57), channel_id=1, source_target_pairs={{1,2},{3,0},{2,1},{0,3},{5,6},{7,4},{6,5},{4,7},{9,10},{11,8},{10,... | collective-permute-start | bytes 196616 | tf_op jit(solution)/shard_map/ppermute | solution.py:725
  11.6 7.4 %collective-permute-start.6 = (f32[3,8,256]{2,1,0:T(8,128)S(1)}, f32[3,8,256]{2,1,0:T(8,128)S(1)}, u32[]{:S(2)}, u32[]{:S(2)}) collective-permute-start(f32[3,8,256]{2,1,0:T(8,128)S(1)} %get-tuple-element.67), channel_id=1, source_target_pairs={{0,4},{8,12},{16,20},{24,28},{4,0},{12,8},{20,16},{28,24},{1,5},{9... | collective-permute-start | bytes 73736 | tf_op jit(solution)/shard_map/ppermute | solution.py:728
  11.7 7.4 %collective-permute-start.4 = (f32[3,8,256]{2,1,0:T(8,128)S(1)}, f32[3,8,256]{2,1,0:T(8,128)S(1)}, u32[]{:S(2)}, u32[]{:S(2)}) collective-permute-start(f32[3,8,256]{2,1,0:T(8,128)S(1)} %get-tuple-element.65), channel_id=1, source_target_pairs={{4,8},{12,16},{20,24},{28,0},{8,4},{16,12},{24,20},{0,28},{5,9},{1... | collective-permute-start | bytes 73736 | tf_op jit(solution)/shard_map/ppermute | solution.py:729
  20.7 3.8 %collective-permute-start.7 = (f32[32,128]{1,0:T(8,128)S(1)}, f32[32,128]{1,0:T(8,128)S(1)}, u32[]{:S(2)}, u32[]{:S(2)}) collective-permute-start(f32[32,128]{1,0:T(8,128)S(1)} %get-tuple-element.94), channel_id=1, source_target_pairs={{0,2},{1,3},{2,0},{3,1},{4,6},{5,7},{6,4},{7,5},{8,10},{9,11},{10,... | collective-permute-start | bytes 49160 | tf_op jit(solution)/shard_map/ppermute | solution.py:738
  24.5 1.2 %collective-permute-start.8 = (f32[16,128]{1,0:T(8,128)S(1)}, f32[16,128]{1,0:T(8,128)S(1)}, u32[]{:S(2)}, u32[]{:S(2)}) collective-permute-start(f32[16,128]{1,0:T(8,128)S(1)} %get-tuple-element.96), channel_id=1, source_target_pairs={{0,1},{2,3},{1,0},{3,2},{4,5},{6,7},{5,4},{7,6},{8,9},{10,11},{9,8... | collective-permute-start | bytes 24584 | tf_op jit(solution)/shard_map/ppermute | solution.py:739

commit v7 on v6

--- a/solution.py
+++ b/solution.py
@@ -707,7 +707,7 @@
     coarse_x, coarse_y, coarse_z = macro_temp.shape
     near_x, far_x = pairs(count_x, 0), pairs(count_x, 1)
     near_y, far_y = pairs(count_y, 0), pairs(count_y, 1)
-    across = [(k, (k + count_y // 2) % count_y) for k in range(count_y)]
+    across = [(k, count_y - 1 - k) for k in range(count_y)]
     ride = count_y == 4
     macro = jnp.swapaxes(macro_temp, 1, 2)
     still = [pltpu.with_memory_space_constraint(v, pltpu.HBM) for v in (phase, solute, macro)]

time: 26.5 us -> 26 us (0.981)
  starting transfers between devices: 14 us -> 13.4 us
    ppermute x1, starting transfers between devices: 1.58 us -> 0.84 us  [body(): mine, send = merge(mine, lax.ppermute(send, 'gy', across))]
  transfers between devices with their start and end apart: 9 -> 9, of which waited for: 4 -> 3; matrix products, arithmetic and copies ran while one was open for 0% -> 0% of each run, Pallas kernels for 18% -> 19%
where the time goes in v7:
time: 26 us; the launch traced here: 25.8 us
  starting transfers between devices  13.4 us (52%)
  Pallas kernels  8.64 us (33%)
  waiting for transfers between devices  3.11 us (12%)
  between operations  0.69 us (3%)
    ppermute x1, starting transfers between devices, body(): face_b = lax.ppermute(face_b, 'gx', far_x)  4.38 us
    ppermute x1, starting transfers between devices, body(): corner_b = lax.ppermute(corner_b, 'gx', far_x)  3.45 us
    pallas_call x1, Pallas kernels, inner(): pl.pallas_call(functools.partial(inner_kernel, coarse_y), out_shape=(part...  3.24 us
    ppermute x1, starting transfers between devices, body(): face_a = lax.ppermute(face_a, 'gx', near_x)  2.59 us
    ppermute x1, waiting for transfers between devices, body(): mine, send = merge(mine, lax.ppermute(send, 'gy', across))  2.39 us
    pallas_call x1, Pallas kernels, rims(): pl.pallas_call(functools.partial(rim_kernel, coarse_y, size_x), out_shape...  1.62 us
    pallas_call x1, Pallas kernels, pack(): pl.pallas_call(pack_kernel, out_shape=(field, field, face, face, *sides,...  1.51 us
    ppermute x1, starting transfers between devices, body(): strip_b = lax.ppermute(strip_b, 'gy', far_y)  1.26 us
  transfers between devices with their start and end apart: 9, of which 3 were waited for; matrix products, arithmetic and copies ran while one was open for 0% of the time, Pallas kernels for 19%

profile of v7, /device:TPU:0, one launch (start us, length us, event | category | flops | bytes accessed | tf_op | source)
XLA Modules:
  0.0 25.8 jit_solution(12074350984626086652)
XLA Ops:
  0.6 1.5 %pack.1 = (f32[16,32,256]{2,1,0:T(8,128)S(1)}, f32[16,32,256]{2,1,0:T(8,128)S(1)}, f32[2,4,32,256]{3,2,1,0:T(8,128)S(1)}, f32[2,4,32,256]{3,2,1,0:T(8,128)S(1)},...) custom-call(f32[16,32,256]{2,1,0:T(8,128)} %phase.1, ...), custom_call_target="tpu_custom_call" | custom-call | flops 100000 | bytes 2000000 | tf_op jit(solution)/shard_map/pack/pallas_call | solution.py:130
  2.1 0.5 %collective-permute-start = (f32[17,8,256]{2,1,0:T(8,128)S(1)}, f32[17,8,256]{2,1,0:T(8,128)S(1)}, u32[]{:S(2)}, u32[]{:S(2)}) collective-permute-start(f32[17,8,256]{2,1,0:T(8,128)S(1)} %get-tuple-element.52), channel_id=1, source_target_pairs={{0,1},{2,3},{1,0},{3,2},{4,5},{6,7},{5,4},{7,6},{8,9},{10,11},{9,8... | collective-permute-start | bytes 417800 | tf_op jit(solution)/shard_map/ppermute | solution.py:717
  2.7 2.6 %collective-permute-start.5 = (f32[2,4,32,256]{3,2,1,0:T(8,128)S(1)}, f32[2,4,32,256]{3,2,1,0:T(8,128)S(1)}, u32[]{:S(2)}, u32[]{:S(2)}) collective-permute-start(f32[2,4,32,256]{3,2,1,0:T(8,128)S(1)} %get-tuple-element.66), channel_id=1, source_target_pairs={{0,4},{8,12},{16,20},{24,28},{4,0},{12,8},{20,16},{28,24},{1,5},{9... | collective-permute-start | bytes 786440 | tf_op jit(solution)/shard_map/ppermute | solution.py:716
  5.3 0.0 collective-permute-done.arrived.side_a
  5.3 1.3 %collective-permute-start.1 = (f32[10,8,256]{2,1,0:T(8,128)S(1)}, f32[10,8,256]{2,1,0:T(8,128)S(1)}, u32[]{:S(2)}, u32[]{:S(2)}) collective-permute-start(f32[10,8,256]{2,1,0:T(8,128)S(1)} %append.1.tile), channel_id=1, source_target_pairs={{1,2},{3,0},{2,1},{0,3},{5,6},{7,4},{6,5},{4,7},{9,10},{11,8},{10,... | collective-permute-start | bytes 245768 | tf_op jit(solution)/shard_map/ppermute | solution.py:724
  6.5 0.1 products.1
  6.7 4.4 %collective-permute-start.3 = (f32[2,4,32,256]{3,2,1,0:T(8,128)S(1)}, f32[2,4,32,256]{3,2,1,0:T(8,128)S(1)}, u32[]{:S(2)}, u32[]{:S(2)}) collective-permute-start(f32[2,4,32,256]{3,2,1,0:T(8,128)S(1)} %get-tuple-element.64), channel_id=1, source_target_pairs={{4,8},{12,16},{20,24},{28,0},{8,4},{16,12},{24,20},{0,28},{5,9},{1... | collective-permute-start | bytes 786440 | tf_op jit(solution)/shard_map/ppermute | solution.py:726
  11.1 0.2 collective-permute-start.2
  11.3 0.0 collective-permute-done.1.strip_b
  11.3 0.4 %corners.1 = (f32[64,128]{1,0:T(8,128)S(1)}, f32[3,8,256]{2,1,0:T(8,128)S(1)}, f32[3,8,256]{2,1,0:T(8,128)S(1)}) custom-call(f32[17,8,256]{2,1,0:T(8,128)S(1)} %collective-permute-done.arrived.side_a, f32[10,8,256]{2,1,0:T(8,128)S(1)} %collective-permute-done.1.strip_b, f32[16,128]{1,0:T(8,128)S(1)} %get-tuple-element.58.table), custom_call_target="tpu_custom_call" | custom-call | flops 100000 | bytes 400000 | tf_op jit(solution)/shard_map/corners/pallas_call | solution.py:217
  11.6 0.0 collective-permute-start.6
  11.7 3.5 %collective-permute-start.4 = (f32[3,8,256]{2,1,0:T(8,128)S(1)}, f32[3,8,256]{2,1,0:T(8,128)S(1)}, u32[]{:S(2)}, u32[]{:S(2)}) collective-permute-start(f32[3,8,256]{2,1,0:T(8,128)S(1)} %get-tuple-element.65), channel_id=1, source_target_pairs={{4,8},{12,16},{20,24},{28,0},{8,4},{16,12},{24,20},{0,28},{5,9},{1... | collective-permute-start | bytes 73736 | tf_op jit(solution)/shard_map/ppermute | solution.py:729
  15.1 0.1 collective-permute-done.2.rest_b
  15.2 3.2 %inner.1 = (f32[8,32,256]{2,1,0:T(8,128)S(1)}, f32[8,32,256]{2,1,0:T(8,128)S(1)}, f32[64,128]{1,0:T(8,128)S(1)}, f32[2,40,256]{2,1,0:T(8,128)S(1)}, f32[16,40,25...) custom-call(f32[16,32,256]{2,1,0:T(8,128)S(1)} %get-tuple-element.50, ...), custom_call_target="tpu_custom_call" | custom-call | flops 500000000 | bytes 5000000 | tf_op jit(solution)/shard_map/inner/pallas_call | solution.py:447
  18.4 0.6 %collective-permute-done.6.corner.near_corner = f32[3,8,256]{2,1,0:T(8,128)S(1)} collective-permute-done((f32[3,8,256]{2,1,0:T(8,128)S(1)}, f32[3,8,256]{2,1,0:T(8,128)S(1)}, u32[]{:S(2)}, u32[]{:S(2)}) %collective-permute-start.6) | collective-permute-done | bytes 24608 | tf_op jit(solution)/shard_map/ppermute | solution.py:728
  19.0 0.0 collective-permute-done.5.face
  19.1 0.0 collective-permute-done.4.corner
  19.1 0.0 collective-permute-done.3.face
  19.1 1.6 %rims.1 = (f32[4,40,256]{2,1,0:T(8,128)S(1)}, f32[4,40,256]{2,1,0:T(8,128)S(1)}, f32[4,32,256]{2,1,0:T(8,128)S(1)}, f32[4,40,256]{2,1,0:T(8,128)S(1)}, f32[4,40,...) custom-call(f32[2,4,32,256]{3,2,1,0:T(8,128)S(1)} %collective-permute-done.3.face, ...), custom_call_target="tpu_custom_call" | custom-call | flops 10000000 | bytes 3000000 | tf_op jit(solution)/shard_map/rims/pallas_call | solution.py:589
  20.7 0.8 %collective-permute-start.7 = (f32[32,128]{1,0:T(8,128)S(1)}, f32[32,128]{1,0:T(8,128)S(1)}, u32[]{:S(2)}, u32[]{:S(2)}) collective-permute-start(f32[32,128]{1,0:T(8,128)S(1)} %get-tuple-element.94), channel_id=1, source_target_pairs={{0,3},{1,2},{2,1},{3,0},{4,7},{5,6},{6,5},{7,4},{8,11},{9,10},{10,... | collective-permute-start | bytes 49160 | tf_op jit(solution)/shard_map/ppermute | solution.py:738
  21.6 2.4 %collective-permute-done.7.arrived = f32[32,128]{1,0:T(8,128)S(1)} collective-permute-done((f32[32,128]{1,0:T(8,128)S(1)}, f32[32,128]{1,0:T(8,128)S(1)}, u32[]{:S(2)}, u32[]{:S(2)}) %collective-permute-start.7) | collective-permute-done | bytes 16416 | tf_op jit(solution)/shard_map/ppermute | solution.py:738
  24.0 0.1 collective-permute-start.8
  24.1 1.0 %store.1 = (f32[16,32,256]{2,1,0:T(8,128)}, f32[16,32,256]{2,1,0:T(8,128)}) custom-call(f32[8,32,256]{2,1,0:T(8,128)S(1)} %get-tuple-element.62.middle_phase, f32[8,32,256]{2,1,0:T(8,128)S(1)} %get-tuple-element.63.middle_solute, f32[4,40,256]{2,1,0:T(8,128)S(1)} %get-tuple-element.85.near_p1, f32[4,40,256]{2,1,0:T(8,128)S(1)} %get-tuple-element.86.near_c1, ...), custom_call_target="tpu_custom_call" | custom-call | bytes 4000000 | tf_op jit(solution)/shard_map/store/pallas_call | solution.py:654
  25.1 0.0 collective-permute-done.8.arrived
  25.1 0.7 %owner.1 = f32[4,16,32]{2,1,0:T(8,128)} custom-call(f32[16,128]{1,0:T(8,128)S(1)} %get-tuple-element.95.mine, f32[16,128]{1,0:T(8,128)S(1)} %collective-permute-done.8.arrived), custom_call_target="tpu_custom_call" | custom-call | flops 10000 | bytes 100000 | tf_op jit(solution)/shard_map/owner/pallas_call | solution.py:694
  (3 shorter events, 0.0 us)
Async XLA Ops:
  2.1 3.1 %collective-permute-start = (f32[17,8,256]{2,1,0:T(8,128)S(1)}, f32[17,8,256]{2,1,0:T(8,128)S(1)}, u32[]{:S(2)}, u32[]{:S(2)}) collective-permute-start(f32[17,8,256]{2,1,0:T(8,128)S(1)} %get-tuple-element.52), channel_id=1, source_target_pairs={{0,1},{2,3},{1,0},{3,2},{4,5},{6,7},{5,4},{7,6},{8,9},{10,11},{9,8... | collective-permute-start | bytes 417800 | tf_op jit(solution)/shard_map/ppermute | solution.py:717
  2.7 16.4 %collective-permute-start.5 = (f32[2,4,32,256]{3,2,1,0:T(8,128)S(1)}, f32[2,4,32,256]{3,2,1,0:T(8,128)S(1)}, u32[]{:S(2)}, u32[]{:S(2)}) collective-permute-start(f32[2,4,32,256]{3,2,1,0:T(8,128)S(1)} %get-tuple-element.66), channel_id=1, source_target_pairs={{0,4},{8,12},{16,20},{24,28},{4,0},{12,8},{20,16},{28,24},{1,5},{9... | collective-permute-start | bytes 786440 | tf_op jit(solution)/shard_map/ppermute | solution.py:716
  5.3 6.0 %collective-permute-start.1 = (f32[10,8,256]{2,1,0:T(8,128)S(1)}, f32[10,8,256]{2,1,0:T(8,128)S(1)}, u32[]{:S(2)}, u32[]{:S(2)}) collective-permute-start(f32[10,8,256]{2,1,0:T(8,128)S(1)} %append.1.tile), channel_id=1, source_target_pairs={{1,2},{3,0},{2,1},{0,3},{5,6},{7,4},{6,5},{4,7},{9,10},{11,8},{10,... | collective-permute-start | bytes 245768 | tf_op jit(solution)/shard_map/ppermute | solution.py:724
  6.7 12.4 %collective-permute-start.3 = (f32[2,4,32,256]{3,2,1,0:T(8,128)S(1)}, f32[2,4,32,256]{3,2,1,0:T(8,128)S(1)}, u32[]{:S(2)}, u32[]{:S(2)}) collective-permute-start(f32[2,4,32,256]{3,2,1,0:T(8,128)S(1)} %get-tuple-element.64), channel_id=1, source_target_pairs={{4,8},{12,16},{20,24},{28,0},{8,4},{16,12},{24,20},{0,28},{5,9},{1... | collective-permute-start | bytes 786440 | tf_op jit(solution)/shard_map/ppermute | solution.py:726
  11.1 4.1 %collective-permute-start.2 = (f32[8,8,256]{2,1,0:T(8,128)S(1)}, f32[8,8,256]{2,1,0:T(8,128)S(1)}, u32[]{:S(2)}, u32[]{:S(2)}) collective-permute-start(f32[8,8,256]{2,1,0:T(8,128)S(1)} %get-tuple-element.57), channel_id=1, source_target_pairs={{1,2},{3,0},{2,1},{0,3},{5,6},{7,4},{6,5},{4,7},{9,10},{11,8},{10,... | collective-permute-start | bytes 196616 | tf_op jit(solution)/shard_map/ppermute | solution.py:725
  11.6 7.4 %collective-permute-start.6 = (f32[3,8,256]{2,1,0:T(8,128)S(1)}, f32[3,8,256]{2,1,0:T(8,128)S(1)}, u32[]{:S(2)}, u32[]{:S(2)}) collective-permute-start(f32[3,8,256]{2,1,0:T(8,128)S(1)} %get-tuple-element.67), channel_id=1, source_target_pairs={{0,4},{8,12},{16,20},{24,28},{4,0},{12,8},{20,16},{28,24},{1,5},{9... | collective-permute-start | bytes 73736 | tf_op jit(solution)/shard_map/ppermute | solution.py:728
  11.7 7.4 %collective-permute-start.4 = (f32[3,8,256]{2,1,0:T(8,128)S(1)}, f32[3,8,256]{2,1,0:T(8,128)S(1)}, u32[]{:S(2)}, u32[]{:S(2)}) collective-permute-start(f32[3,8,256]{2,1,0:T(8,128)S(1)} %get-tuple-element.65), channel_id=1, source_target_pairs={{4,8},{12,16},{20,24},{28,0},{8,4},{16,12},{24,20},{0,28},{5,9},{1... | collective-permute-start | bytes 73736 | tf_op jit(solution)/shard_map/ppermute | solution.py:729
  20.7 3.2 %collective-permute-start.7 = (f32[32,128]{1,0:T(8,128)S(1)}, f32[32,128]{1,0:T(8,128)S(1)}, u32[]{:S(2)}, u32[]{:S(2)}) collective-permute-start(f32[32,128]{1,0:T(8,128)S(1)} %get-tuple-element.94), channel_id=1, source_target_pairs={{0,3},{1,2},{2,1},{3,0},{4,7},{5,6},{6,5},{7,4},{8,11},{9,10},{10,... | collective-permute-start | bytes 49160 | tf_op jit(solution)/shard_map/ppermute | solution.py:738
  24.0 1.2 %collective-permute-start.8 = (f32[16,128]{1,0:T(8,128)S(1)}, f32[16,128]{1,0:T(8,128)S(1)}, u32[]{:S(2)}, u32[]{:S(2)}) collective-permute-start(f32[16,128]{1,0:T(8,128)S(1)} %get-tuple-element.96), channel_id=1, source_target_pairs={{0,1},{2,3},{1,0},{3,2},{4,5},{6,7},{5,4},{7,6},{8,9},{10,11},{9,8... | collective-permute-start | bytes 24584 | tf_op jit(solution)/shard_map/ppermute | solution.py:739

commit v8 on v7

--- a/solution.py
+++ b/solution.py
@@ -91,20 +91,21 @@
     size_x, size_y, size_z = phase.shape
     odd_x = lax.rem(lax.axis_index("gx"), 2)
     even_y = lax.rem(lax.axis_index("gy"), 2) == 0
-    copies = []
-    for at in range(0, size_x, HALO):
-        for ref, here in ((phase, phase_here), (solute, solute_here)):
+    copies = [(macro, local)]
+    for ref, here in ((phase, phase_here), (solute, solute_here)):
+        for at in range(0, size_x, HALO):
             copies.append((ref.at[pl.ds(at, HALO)], here.at[pl.ds(at, HALO)]))
-    copies.append((macro, local))
     copies = start_all(copies, sems)
-    wait_all(copies)
-    for field, here in enumerate((phase_here, solute_here)):
+    half = 1 + size_x // HALO
+    for field, (here, batch) in enumerate(((phase_here, copies[:half]), (solute_here, copies[half:]))):
+        wait_all(batch)
         face_a[field] = here[pl.ds((1 - odd_x) * (size_x - HALO), HALO)]
         face_b[field] = here[pl.ds(odd_x * (size_x - HALO), HALO)]
+        if field == 0:
+            wide = jnp.concatenate([local[k] for k in range(local.shape[0])], axis=1)
+            table[...] = wide
     low = [here[:, pl.ds(0, ROWS), :] for here in (phase_here, solute_here)]
     high = [here[:, pl.ds(size_y - ROWS, ROWS), :] for here in (phase_here, solute_here)]
-    wide = jnp.concatenate([local[k] for k in range(local.shape[0])], axis=1)
-    table[...] = wide
     top = row_ids((size_x, ROWS, size_z)) < HALO
     low_side = jnp.where(top, low[0], pltpu.roll(low[1], HALO, 1))
     high_side = jnp.where(top, pltpu.roll(high[1], HALO, 1), high[0])
@@ -720,7 +721,7 @@
     else:
         table = lax.all_gather(table, "gy").reshape(coarse_shape)
     matrices, along_z = z_products(phase.shape[2], strip_b)
-    face_b, rest_b, matrices = lax.optimization_barrier((face_b, rest_b, matrices))
+    face_b, rest_b, strip_b = lax.optimization_barrier((face_b, rest_b, strip_b))
     strip_b = lax.ppermute(strip_b, "gy", far_y)
     rest_b = lax.ppermute(rest_b, "gy", far_y)
     face_b = lax.ppermute(face_b, "gx", far_x)

time: 26 us -> 25.7 us (0.988)
  waiting for transfers between devices: 3.11 us -> 2.68 us
  transfers between devices with their start and end apart: 9 -> 9, of which waited for: 3 -> 2; matrix products, arithmetic and copies ran while one was open for 0% -> 0% of each run, Pallas kernels for 19% -> 19%
where the time goes in v8:
time: 25.7 us; the launch traced here: 25.5 us
  starting transfers between devices  13.6 us (53%)
  Pallas kernels  8.58 us (33%)
  waiting for transfers between devices  2.68 us (10%)
  between operations  0.7 us (3%)
    ppermute x1, starting transfers between devices, body(): face_b = lax.ppermute(face_b, 'gx', far_x)  4.31 us
    ppermute x1, starting transfers between devices, body(): corner_b = lax.ppermute(corner_b, 'gx', far_x)  3.5 us
    pallas_call x1, Pallas kernels, inner(): pl.pallas_call(functools.partial(inner_kernel, coarse_y), out_shape=(part...  3.24 us
    ppermute x1, starting transfers between devices, body(): face_a = lax.ppermute(face_a, 'gx', near_x)  2.59 us
    ppermute x1, waiting for transfers between devices, body(): mine, send = merge(mine, lax.ppermute(send, 'gy', across))  2.17 us
    pallas_call x1, Pallas kernels, rims(): pl.pallas_call(functools.partial(rim_kernel, coarse_y, size_x), out_shape...  1.62 us
    pallas_call x1, Pallas kernels, pack(): pl.pallas_call(pack_kernel, out_shape=(field, field, face, face, *sides,...  1.44 us
    ppermute x1, starting transfers between devices, body(): strip_b = lax.ppermute(strip_b, 'gy', far_y)  1.26 us
  transfers between devices with their start and end apart: 9, of which 2 were waited for; matrix products, arithmetic and copies ran while one was open for 0% of the time, Pallas kernels for 19%

profile of v8, /device:TPU:0, one launch (start us, length us, event | category | flops | bytes accessed | tf_op | source)
XLA Modules:
  0.0 25.5 jit_solution(15836736271149612569)
XLA Ops:
  0.6 1.4 %pack.1 = (f32[16,32,256]{2,1,0:T(8,128)S(1)}, f32[16,32,256]{2,1,0:T(8,128)S(1)}, f32[2,4,32,256]{3,2,1,0:T(8,128)S(1)}, f32[2,4,32,256]{3,2,1,0:T(8,128)S(1)},...) custom-call(f32[16,32,256]{2,1,0:T(8,128)} %phase.1, ...), custom_call_target="tpu_custom_call" | custom-call | flops 100000 | bytes 2000000 | tf_op jit(solution)/shard_map/pack/pallas_call | solution.py:131
  2.1 0.5 %collective-permute-start = (f32[17,8,256]{2,1,0:T(8,128)S(1)}, f32[17,8,256]{2,1,0:T(8,128)S(1)}, u32[]{:S(2)}, u32[]{:S(2)}) collective-permute-start(f32[17,8,256]{2,1,0:T(8,128)S(1)} %get-tuple-element.52), channel_id=1, source_target_pairs={{0,1},{2,3},{1,0},{3,2},{4,5},{6,7},{5,4},{7,6},{8,9},{10,11},{9,8... | collective-permute-start | bytes 417800 | tf_op jit(solution)/shard_map/ppermute | solution.py:718
  2.6 2.6 %collective-permute-start.5 = (f32[2,4,32,256]{3,2,1,0:T(8,128)S(1)}, f32[2,4,32,256]{3,2,1,0:T(8,128)S(1)}, u32[]{:S(2)}, u32[]{:S(2)}) collective-permute-start(f32[2,4,32,256]{3,2,1,0:T(8,128)S(1)} %get-tuple-element.66), channel_id=1, source_target_pairs={{0,4},{8,12},{16,20},{24,28},{4,0},{12,8},{20,16},{28,24},{1,5},{9... | collective-permute-start | bytes 786440 | tf_op jit(solution)/shard_map/ppermute | solution.py:717
  5.2 0.0 collective-permute-done.arrived.side_a
  5.2 1.3 %collective-permute-start.1 = (f32[10,8,256]{2,1,0:T(8,128)S(1)}, f32[10,8,256]{2,1,0:T(8,128)S(1)}, u32[]{:S(2)}, u32[]{:S(2)}) collective-permute-start(f32[10,8,256]{2,1,0:T(8,128)S(1)} %append.1.tile), channel_id=1, source_target_pairs={{1,2},{3,0},{2,1},{0,3},{5,6},{7,4},{6,5},{4,7},{9,10},{11,8},{10,... | collective-permute-start | bytes 245768 | tf_op jit(solution)/shard_map/ppermute | solution.py:725
  6.5 4.3 %collective-permute-start.3 = (f32[2,4,32,256]{3,2,1,0:T(8,128)S(1)}, f32[2,4,32,256]{3,2,1,0:T(8,128)S(1)}, u32[]{:S(2)}, u32[]{:S(2)}) collective-permute-start(f32[2,4,32,256]{3,2,1,0:T(8,128)S(1)} %get-tuple-element.64), channel_id=1, source_target_pairs={{4,8},{12,16},{20,24},{28,0},{8,4},{16,12},{24,20},{0,28},{5,9},{1... | collective-permute-start | bytes 786440 | tf_op jit(solution)/shard_map/ppermute | solution.py:727
  10.8 0.2 collective-permute-start.2
  11.0 0.1 products.1
  11.1 0.0 collective-permute-done.1.strip_b
  11.1 0.4 %corners.1 = (f32[64,128]{1,0:T(8,128)S(1)}, f32[3,8,256]{2,1,0:T(8,128)S(1)}, f32[3,8,256]{2,1,0:T(8,128)S(1)}) custom-call(f32[17,8,256]{2,1,0:T(8,128)S(1)} %collective-permute-done.arrived.side_a, f32[10,8,256]{2,1,0:T(8,128)S(1)} %collective-permute-done.1.strip_b, f32[16,128]{1,0:T(8,128)S(1)} %get-tuple-element.58.table), custom_call_target="tpu_custom_call" | custom-call | flops 100000 | bytes 400000 | tf_op jit(solution)/shard_map/corners/pallas_call | solution.py:218
  11.5 0.0 collective-permute-start.6
  11.5 3.5 %collective-permute-start.4 = (f32[3,8,256]{2,1,0:T(8,128)S(1)}, f32[3,8,256]{2,1,0:T(8,128)S(1)}, u32[]{:S(2)}, u32[]{:S(2)}) collective-permute-start(f32[3,8,256]{2,1,0:T(8,128)S(1)} %get-tuple-element.65), channel_id=1, source_target_pairs={{4,8},{12,16},{20,24},{28,0},{8,4},{16,12},{24,20},{0,28},{5,9},{1... | collective-permute-start | bytes 73736 | tf_op jit(solution)/shard_map/ppermute | solution.py:730
  15.0 0.0 collective-permute-done.2.rest_b
  15.0 3.2 %inner.1 = (f32[8,32,256]{2,1,0:T(8,128)S(1)}, f32[8,32,256]{2,1,0:T(8,128)S(1)}, f32[64,128]{1,0:T(8,128)S(1)}, f32[2,40,256]{2,1,0:T(8,128)S(1)}, f32[16,40,25...) custom-call(f32[16,32,256]{2,1,0:T(8,128)S(1)} %get-tuple-element.50, ...), custom_call_target="tpu_custom_call" | custom-call | flops 500000000 | bytes 5000000 | tf_op jit(solution)/shard_map/inner/pallas_call | solution.py:448
  18.3 0.5 %collective-permute-done.6.corner.near_corner = f32[3,8,256]{2,1,0:T(8,128)S(1)} collective-permute-done((f32[3,8,256]{2,1,0:T(8,128)S(1)}, f32[3,8,256]{2,1,0:T(8,128)S(1)}, u32[]{:S(2)}, u32[]{:S(2)}) %collective-permute-start.6) | collective-permute-done | bytes 24608 | tf_op jit(solution)/shard_map/ppermute | solution.py:729
  18.8 0.0 collective-permute-done.5.face
  18.8 0.0 collective-permute-done.4.corner
  18.8 0.0 collective-permute-done.3.face
  18.8 1.6 %rims.1 = (f32[4,40,256]{2,1,0:T(8,128)S(1)}, f32[4,40,256]{2,1,0:T(8,128)S(1)}, f32[4,32,256]{2,1,0:T(8,128)S(1)}, f32[4,40,256]{2,1,0:T(8,128)S(1)}, f32[4,40,...) custom-call(f32[2,4,32,256]{3,2,1,0:T(8,128)S(1)} %collective-permute-done.3.face, ...), custom_call_target="tpu_custom_call" | custom-call | flops 10000000 | bytes 3000000 | tf_op jit(solution)/shard_map/rims/pallas_call | solution.py:590
  20.4 1.1 %collective-permute-start.7 = (f32[32,128]{1,0:T(8,128)S(1)}, f32[32,128]{1,0:T(8,128)S(1)}, u32[]{:S(2)}, u32[]{:S(2)}) collective-permute-start(f32[32,128]{1,0:T(8,128)S(1)} %get-tuple-element.94), channel_id=1, source_target_pairs={{0,3},{1,2},{2,1},{3,0},{4,7},{5,6},{6,5},{7,4},{8,11},{9,10},{10,... | collective-permute-start | bytes 49160 | tf_op jit(solution)/shard_map/ppermute | solution.py:739
  21.5 2.2 %collective-permute-done.7.arrived = f32[32,128]{1,0:T(8,128)S(1)} collective-permute-done((f32[32,128]{1,0:T(8,128)S(1)}, f32[32,128]{1,0:T(8,128)S(1)}, u32[]{:S(2)}, u32[]{:S(2)}) %collective-permute-start.7) | collective-permute-done | bytes 16416 | tf_op jit(solution)/shard_map/ppermute | solution.py:739
  23.7 0.1 collective-permute-start.8
  23.8 1.0 %store.1 = (f32[16,32,256]{2,1,0:T(8,128)}, f32[16,32,256]{2,1,0:T(8,128)}) custom-call(f32[8,32,256]{2,1,0:T(8,128)S(1)} %get-tuple-element.62.middle_phase, f32[8,32,256]{2,1,0:T(8,128)S(1)} %get-tuple-element.63.middle_solute, f32[4,40,256]{2,1,0:T(8,128)S(1)} %get-tuple-element.85.near_p1, f32[4,40,256]{2,1,0:T(8,128)S(1)} %get-tuple-element.86.near_c1, ...), custom_call_target="tpu_custom_call" | custom-call | bytes 4000000 | tf_op jit(solution)/shard_map/store/pallas_call | solution.py:655
  24.8 0.0 collective-permute-done.8.arrived
  24.9 0.7 %owner.1 = f32[4,16,32]{2,1,0:T(8,128)} custom-call(f32[16,128]{1,0:T(8,128)S(1)} %get-tuple-element.95.mine, f32[16,128]{1,0:T(8,128)S(1)} %collective-permute-done.8.arrived), custom_call_target="tpu_custom_call" | custom-call | flops 10000 | bytes 100000 | tf_op jit(solution)/shard_map/owner/pallas_call | solution.py:695
  (3 shorter events, 0.0 us)
Async XLA Ops:
  2.1 3.1 %collective-permute-start = (f32[17,8,256]{2,1,0:T(8,128)S(1)}, f32[17,8,256]{2,1,0:T(8,128)S(1)}, u32[]{:S(2)}, u32[]{:S(2)}) collective-permute-start(f32[17,8,256]{2,1,0:T(8,128)S(1)} %get-tuple-element.52), channel_id=1, source_target_pairs={{0,1},{2,3},{1,0},{3,2},{4,5},{6,7},{5,4},{7,6},{8,9},{10,11},{9,8... | collective-permute-start | bytes 417800 | tf_op jit(solution)/shard_map/ppermute | solution.py:718
  2.6 16.2 %collective-permute-start.5 = (f32[2,4,32,256]{3,2,1,0:T(8,128)S(1)}, f32[2,4,32,256]{3,2,1,0:T(8,128)S(1)}, u32[]{:S(2)}, u32[]{:S(2)}) collective-permute-start(f32[2,4,32,256]{3,2,1,0:T(8,128)S(1)} %get-tuple-element.66), channel_id=1, source_target_pairs={{0,4},{8,12},{16,20},{24,28},{4,0},{12,8},{20,16},{28,24},{1,5},{9... | collective-permute-start | bytes 786440 | tf_op jit(solution)/shard_map/ppermute | solution.py:717
  5.2 5.9 %collective-permute-start.1 = (f32[10,8,256]{2,1,0:T(8,128)S(1)}, f32[10,8,256]{2,1,0:T(8,128)S(1)}, u32[]{:S(2)}, u32[]{:S(2)}) collective-permute-start(f32[10,8,256]{2,1,0:T(8,128)S(1)} %append.1.tile), channel_id=1, source_target_pairs={{1,2},{3,0},{2,1},{0,3},{5,6},{7,4},{6,5},{4,7},{9,10},{11,8},{10,... | collective-permute-start | bytes 245768 | tf_op jit(solution)/shard_map/ppermute | solution.py:725
  6.5 12.4 %collective-permute-start.3 = (f32[2,4,32,256]{3,2,1,0:T(8,128)S(1)}, f32[2,4,32,256]{3,2,1,0:T(8,128)S(1)}, u32[]{:S(2)}, u32[]{:S(2)}) collective-permute-start(f32[2,4,32,256]{3,2,1,0:T(8,128)S(1)} %get-tuple-element.64), channel_id=1, source_target_pairs={{4,8},{12,16},{20,24},{28,0},{8,4},{16,12},{24,20},{0,28},{5,9},{1... | collective-permute-start | bytes 786440 | tf_op jit(solution)/shard_map/ppermute | solution.py:727
  10.8 4.3 %collective-permute-start.2 = (f32[8,8,256]{2,1,0:T(8,128)S(1)}, f32[8,8,256]{2,1,0:T(8,128)S(1)}, u32[]{:S(2)}, u32[]{:S(2)}) collective-permute-start(f32[8,8,256]{2,1,0:T(8,128)S(1)} %get-tuple-element.57), channel_id=1, source_target_pairs={{1,2},{3,0},{2,1},{0,3},{5,6},{7,4},{6,5},{4,7},{9,10},{11,8},{10,... | collective-permute-start | bytes 196616 | tf_op jit(solution)/shard_map/ppermute | solution.py:726
  11.5 7.3 %collective-permute-start.6 = (f32[3,8,256]{2,1,0:T(8,128)S(1)}, f32[3,8,256]{2,1,0:T(8,128)S(1)}, u32[]{:S(2)}, u32[]{:S(2)}) collective-permute-start(f32[3,8,256]{2,1,0:T(8,128)S(1)} %get-tuple-element.67), channel_id=1, source_target_pairs={{0,4},{8,12},{16,20},{24,28},{4,0},{12,8},{20,16},{28,24},{1,5},{9... | collective-permute-start | bytes 73736 | tf_op jit(solution)/shard_map/ppermute | solution.py:729
  11.5 7.3 %collective-permute-start.4 = (f32[3,8,256]{2,1,0:T(8,128)S(1)}, f32[3,8,256]{2,1,0:T(8,128)S(1)}, u32[]{:S(2)}, u32[]{:S(2)}) collective-permute-start(f32[3,8,256]{2,1,0:T(8,128)S(1)} %get-tuple-element.65), channel_id=1, source_target_pairs={{4,8},{12,16},{20,24},{28,0},{8,4},{16,12},{24,20},{0,28},{5,9},{1... | collective-permute-start | bytes 73736 | tf_op jit(solution)/shard_map/ppermute | solution.py:730
  20.4 3.2 %collective-permute-start.7 = (f32[32,128]{1,0:T(8,128)S(1)}, f32[32,128]{1,0:T(8,128)S(1)}, u32[]{:S(2)}, u32[]{:S(2)}) collective-permute-start(f32[32,128]{1,0:T(8,128)S(1)} %get-tuple-element.94), channel_id=1, source_target_pairs={{0,3},{1,2},{2,1},{3,0},{4,7},{5,6},{6,5},{7,4},{8,11},{9,10},{10,... | collective-permute-start | bytes 49160 | tf_op jit(solution)/shard_map/ppermute | solution.py:739
  23.7 1.2 %collective-permute-start.8 = (f32[16,128]{1,0:T(8,128)S(1)}, f32[16,128]{1,0:T(8,128)S(1)}, u32[]{:S(2)}, u32[]{:S(2)}) collective-permute-start(f32[16,128]{1,0:T(8,128)S(1)} %get-tuple-element.96), channel_id=1, source_target_pairs={{0,1},{2,3},{1,0},{3,2},{4,5},{6,7},{5,4},{7,6},{8,9},{10,11},{9,8... | collective-permute-start | bytes 24584 | tf_op jit(solution)/shard_map/ppermute | solution.py:740

commit v9 on v8

--- a/solution.py
+++ b/solution.py
@@ -407,15 +407,14 @@
 
     for step in "01":
         p, c, dz, cz, gx, dv = (name + step for name in ("p", "c", "dz", "cz", "gx", "dv"))
-        kept[dz][...] = along(kept[p][...], matrices[0])
+        for u in range(*span[dz]):
+            at(dz, u)[...] = z_difference(get(p, u), True)
         kept[cz][...] = along(kept[c][...], matrices[2])
         begin, end = span[gx]
         for u in range(begin, end):
             flux_x, flux_y, flux_z = flux(get(p, u - 1), get(p, u), get(p, u + 1), get(dz, u))
             at(gx, u)[...] = flux_x
-            at(dv, u)[...] = spread(flux_y)
-            fz[u - begin] = flux_z
-        kept[dv][...] += along(fz[pl.ds(0, end - begin)], matrices[1])
+            at(dv, u)[...] = spread(flux_y) + z_difference(flux_z, False)
         take = (lambda v: v) if step == "0" else (lambda v: v[:size_y])
         for u in range(begin + 1, end - 1):
             here, conc = take(get(p, u)), get(c, u)

time: 25.7 us -> 25.7 us (level)
  Pallas kernels: 8.58 us -> 8.1 us
  waiting for transfers between devices: 2.68 us -> 3.16 us
    pallas_call x1, Pallas kernels: 3.24 us -> 2.76 us  [inner(): pl.pallas_call(functools.partial(inner_kernel, coarse_y), out_shape=(part...]
    ppermute x1, waiting for transfers between devices: 0.48 us -> 0.96 us  [body(): corner_a = lax.ppermute(corner_a, 'gx', near_x)]
  transfers between devices with their start and end apart: 9 -> 9, of which waited for: 2 -> 2; matrix products, arithmetic and copies ran while one was open for 0% -> 0% of each run, Pallas kernels for 19% -> 17%
where the time goes in v9:
time: 25.7 us; the launch traced here: 25.5 us
  starting transfers between devices  13.6 us (53%)
  Pallas kernels  8.1 us (32%)
  waiting for transfers between devices  3.16 us (12%)
  between operations  0.7 us (3%)
    ppermute x1, starting transfers between devices, body(): face_b = lax.ppermute(face_b, 'gx', far_x)  4.31 us
    ppermute x1, starting transfers between devices, body(): corner_b = lax.ppermute(corner_b, 'gx', far_x)  3.5 us
    pallas_call x1, Pallas kernels, inner(): pl.pallas_call(functools.partial(inner_kernel, coarse_y), out_shape=(part...  2.76 us
    ppermute x1, starting transfers between devices, body(): face_a = lax.ppermute(face_a, 'gx', near_x)  2.59 us
    ppermute x1, waiting for transfers between devices, body(): mine, send = merge(mine, lax.ppermute(send, 'gy', across))  2.17 us
    pallas_call x1, Pallas kernels, rims(): pl.pallas_call(functools.partial(rim_kernel, coarse_y, size_x), out_shape...  1.62 us
    pallas_call x1, Pallas kernels, pack(): pl.pallas_call(pack_kernel, out_shape=(field, field, face, face, *sides,...  1.44 us
    ppermute x1, starting transfers between devices, body(): strip_b = lax.ppermute(strip_b, 'gy', far_y)  1.26 us
  transfers between devices with their start and end apart: 9, of which 2 were waited for; matrix products, arithmetic and copies ran while one was open for 0% of the time, Pallas kernels for 17%

profile of v9, /device:TPU:0, one launch (start us, length us, event | category | flops | bytes accessed | tf_op | source)
XLA Modules:
  0.0 25.5 jit_solution(10286189822857001947)
XLA Ops:
  0.6 1.4 %pack.1 = (f32[16,32,256]{2,1,0:T(8,128)S(1)}, f32[16,32,256]{2,1,0:T(8,128)S(1)}, f32[2,4,32,256]{3,2,1,0:T(8,128)S(1)}, f32[2,4,32,256]{3,2,1,0:T(8,128)S(1)},...) custom-call(f32[16,32,256]{2,1,0:T(8,128)} %phase.1, ...), custom_call_target="tpu_custom_call" | custom-call | flops 100000 | bytes 2000000 | tf_op jit(solution)/shard_map/pack/pallas_call | solution.py:131
  2.1 0.5 %collective-permute-start = (f32[17,8,256]{2,1,0:T(8,128)S(1)}, f32[17,8,256]{2,1,0:T(8,128)S(1)}, u32[]{:S(2)}, u32[]{:S(2)}) collective-permute-start(f32[17,8,256]{2,1,0:T(8,128)S(1)} %get-tuple-element.52), channel_id=1, source_target_pairs={{0,1},{2,3},{1,0},{3,2},{4,5},{6,7},{5,4},{7,6},{8,9},{10,11},{9,8... | collective-permute-start | bytes 417800 | tf_op jit(solution)/shard_map/ppermute | solution.py:717
  2.6 2.6 %collective-permute-start.5 = (f32[2,4,32,256]{3,2,1,0:T(8,128)S(1)}, f32[2,4,32,256]{3,2,1,0:T(8,128)S(1)}, u32[]{:S(2)}, u32[]{:S(2)}) collective-permute-start(f32[2,4,32,256]{3,2,1,0:T(8,128)S(1)} %get-tuple-element.66), channel_id=1, source_target_pairs={{0,4},{8,12},{16,20},{24,28},{4,0},{12,8},{20,16},{28,24},{1,5},{9... | collective-permute-start | bytes 786440 | tf_op jit(solution)/shard_map/ppermute | solution.py:716
  5.2 0.0 collective-permute-done.arrived.side_a
  5.2 1.3 %collective-permute-start.1 = (f32[10,8,256]{2,1,0:T(8,128)S(1)}, f32[10,8,256]{2,1,0:T(8,128)S(1)}, u32[]{:S(2)}, u32[]{:S(2)}) collective-permute-start(f32[10,8,256]{2,1,0:T(8,128)S(1)} %append.1.tile), channel_id=1, source_target_pairs={{1,2},{3,0},{2,1},{0,3},{5,6},{7,4},{6,5},{4,7},{9,10},{11,8},{10,... | collective-permute-start | bytes 245768 | tf_op jit(solution)/shard_map/ppermute | solution.py:724
  6.5 4.3 %collective-permute-start.3 = (f32[2,4,32,256]{3,2,1,0:T(8,128)S(1)}, f32[2,4,32,256]{3,2,1,0:T(8,128)S(1)}, u32[]{:S(2)}, u32[]{:S(2)}) collective-permute-start(f32[2,4,32,256]{3,2,1,0:T(8,128)S(1)} %get-tuple-element.64), channel_id=1, source_target_pairs={{4,8},{12,16},{20,24},{28,0},{8,4},{16,12},{24,20},{0,28},{5,9},{1... | collective-permute-start | bytes 786440 | tf_op jit(solution)/shard_map/ppermute | solution.py:726
  10.8 0.2 collective-permute-start.2
  11.0 0.1 products.1
  11.1 0.0 collective-permute-done.1.strip_b
  11.1 0.4 %corners.1 = (f32[64,128]{1,0:T(8,128)S(1)}, f32[3,8,256]{2,1,0:T(8,128)S(1)}, f32[3,8,256]{2,1,0:T(8,128)S(1)}) custom-call(f32[17,8,256]{2,1,0:T(8,128)S(1)} %collective-permute-done.arrived.side_a, f32[10,8,256]{2,1,0:T(8,128)S(1)} %collective-permute-done.1.strip_b, f32[16,128]{1,0:T(8,128)S(1)} %get-tuple-element.58.table), custom_call_target="tpu_custom_call" | custom-call | flops 100000 | bytes 400000 | tf_op jit(solution)/shard_map/corners/pallas_call | solution.py:218
  11.5 0.0 collective-permute-start.6
  11.5 3.5 %collective-permute-start.4 = (f32[3,8,256]{2,1,0:T(8,128)S(1)}, f32[3,8,256]{2,1,0:T(8,128)S(1)}, u32[]{:S(2)}, u32[]{:S(2)}) collective-permute-start(f32[3,8,256]{2,1,0:T(8,128)S(1)} %get-tuple-element.65), channel_id=1, source_target_pairs={{4,8},{12,16},{20,24},{28,0},{8,4},{16,12},{24,20},{0,28},{5,9},{1... | collective-permute-start | bytes 73736 | tf_op jit(solution)/shard_map/ppermute | solution.py:729
  15.0 0.0 collective-permute-done.2.rest_b
  15.0 2.8 %inner.1 = (f32[8,32,256]{2,1,0:T(8,128)S(1)}, f32[8,32,256]{2,1,0:T(8,128)S(1)}, f32[64,128]{1,0:T(8,128)S(1)}, f32[2,40,256]{2,1,0:T(8,128)S(1)}, f32[16,40,25...) custom-call(f32[16,32,256]{2,1,0:T(8,128)S(1)} %get-tuple-element.50, ...), custom_call_target="tpu_custom_call" | custom-call | flops 500000000 | bytes 5000000 | tf_op jit(solution)/shard_map/inner/pallas_call | solution.py:447
  17.8 1.0 %collective-permute-done.6.corner.near_corner = f32[3,8,256]{2,1,0:T(8,128)S(1)} collective-permute-done((f32[3,8,256]{2,1,0:T(8,128)S(1)}, f32[3,8,256]{2,1,0:T(8,128)S(1)}, u32[]{:S(2)}, u32[]{:S(2)}) %collective-permute-start.6) | collective-permute-done | bytes 24608 | tf_op jit(solution)/shard_map/ppermute | solution.py:728
  18.8 0.0 collective-permute-done.5.face
  18.8 0.0 collective-permute-done.4.corner
  18.8 0.0 collective-permute-done.3.face
  18.8 1.6 %rims.1 = (f32[4,40,256]{2,1,0:T(8,128)S(1)}, f32[4,40,256]{2,1,0:T(8,128)S(1)}, f32[4,32,256]{2,1,0:T(8,128)S(1)}, f32[4,40,256]{2,1,0:T(8,128)S(1)}, f32[4,40,...) custom-call(f32[2,4,32,256]{3,2,1,0:T(8,128)S(1)} %collective-permute-done.3.face, ...), custom_call_target="tpu_custom_call" | custom-call | flops 10000000 | bytes 3000000 | tf_op jit(solution)/shard_map/rims/pallas_call | solution.py:589
  20.4 1.1 %collective-permute-start.7 = (f32[32,128]{1,0:T(8,128)S(1)}, f32[32,128]{1,0:T(8,128)S(1)}, u32[]{:S(2)}, u32[]{:S(2)}) collective-permute-start(f32[32,128]{1,0:T(8,128)S(1)} %get-tuple-element.94), channel_id=1, source_target_pairs={{0,3},{1,2},{2,1},{3,0},{4,7},{5,6},{6,5},{7,4},{8,11},{9,10},{10,... | collective-permute-start | bytes 49160 | tf_op jit(solution)/shard_map/ppermute | solution.py:738
  21.5 2.2 %collective-permute-done.7.arrived = f32[32,128]{1,0:T(8,128)S(1)} collective-permute-done((f32[32,128]{1,0:T(8,128)S(1)}, f32[32,128]{1,0:T(8,128)S(1)}, u32[]{:S(2)}, u32[]{:S(2)}) %collective-permute-start.7) | collective-permute-done | bytes 16416 | tf_op jit(solution)/shard_map/ppermute | solution.py:738
  23.7 0.1 collective-permute-start.8
  23.8 1.0 %store.1 = (f32[16,32,256]{2,1,0:T(8,128)}, f32[16,32,256]{2,1,0:T(8,128)}) custom-call(f32[8,32,256]{2,1,0:T(8,128)S(1)} %get-tuple-element.62.middle_phase, f32[8,32,256]{2,1,0:T(8,128)S(1)} %get-tuple-element.63.middle_solute, f32[4,40,256]{2,1,0:T(8,128)S(1)} %get-tuple-element.85.near_p1, f32[4,40,256]{2,1,0:T(8,128)S(1)} %get-tuple-element.86.near_c1, ...), custom_call_target="tpu_custom_call" | custom-call | bytes 4000000 | tf_op jit(solution)/shard_map/store/pallas_call | solution.py:654
  24.8 0.0 collective-permute-done.8.arrived
  24.9 0.7 %owner.1 = f32[4,16,32]{2,1,0:T(8,128)} custom-call(f32[16,128]{1,0:T(8,128)S(1)} %get-tuple-element.95.mine, f32[16,128]{1,0:T(8,128)S(1)} %collective-permute-done.8.arrived), custom_call_target="tpu_custom_call" | custom-call | flops 10000 | bytes 100000 | tf_op jit(solution)/shard_map/owner/pallas_call | solution.py:694
  (3 shorter events, 0.0 us)
Async XLA Ops:
  2.1 3.1 %collective-permute-start = (f32[17,8,256]{2,1,0:T(8,128)S(1)}, f32[17,8,256]{2,1,0:T(8,128)S(1)}, u32[]{:S(2)}, u32[]{:S(2)}) collective-permute-start(f32[17,8,256]{2,1,0:T(8,128)S(1)} %get-tuple-element.52), channel_id=1, source_target_pairs={{0,1},{2,3},{1,0},{3,2},{4,5},{6,7},{5,4},{7,6},{8,9},{10,11},{9,8... | collective-permute-start | bytes 417800 | tf_op jit(solution)/shard_map/ppermute | solution.py:717
  2.6 16.2 %collective-permute-start.5 = (f32[2,4,32,256]{3,2,1,0:T(8,128)S(1)}, f32[2,4,32,256]{3,2,1,0:T(8,128)S(1)}, u32[]{:S(2)}, u32[]{:S(2)}) collective-permute-start(f32[2,4,32,256]{3,2,1,0:T(8,128)S(1)} %get-tuple-element.66), channel_id=1, source_target_pairs={{0,4},{8,12},{16,20},{24,28},{4,0},{12,8},{20,16},{28,24},{1,5},{9... | collective-permute-start | bytes 786440 | tf_op jit(solution)/shard_map/ppermute | solution.py:716
  5.2 5.9 %collective-permute-start.1 = (f32[10,8,256]{2,1,0:T(8,128)S(1)}, f32[10,8,256]{2,1,0:T(8,128)S(1)}, u32[]{:S(2)}, u32[]{:S(2)}) collective-permute-start(f32[10,8,256]{2,1,0:T(8,128)S(1)} %append.1.tile), channel_id=1, source_target_pairs={{1,2},{3,0},{2,1},{0,3},{5,6},{7,4},{6,5},{4,7},{9,10},{11,8},{10,... | collective-permute-start | bytes 245768 | tf_op jit(solution)/shard_map/ppermute | solution.py:724
  6.5 12.4 %collective-permute-start.3 = (f32[2,4,32,256]{3,2,1,0:T(8,128)S(1)}, f32[2,4,32,256]{3,2,1,0:T(8,128)S(1)}, u32[]{:S(2)}, u32[]{:S(2)}) collective-permute-start(f32[2,4,32,256]{3,2,1,0:T(8,128)S(1)} %get-tuple-element.64), channel_id=1, source_target_pairs={{4,8},{12,16},{20,24},{28,0},{8,4},{16,12},{24,20},{0,28},{5,9},{1... | collective-permute-start | bytes 786440 | tf_op jit(solution)/shard_map/ppermute | solution.py:726
  10.8 4.3 %collective-permute-start.2 = (f32[8,8,256]{2,1,0:T(8,128)S(1)}, f32[8,8,256]{2,1,0:T(8,128)S(1)}, u32[]{:S(2)}, u32[]{:S(2)}) collective-permute-start(f32[8,8,256]{2,1,0:T(8,128)S(1)} %get-tuple-element.57), channel_id=1, source_target_pairs={{1,2},{3,0},{2,1},{0,3},{5,6},{7,4},{6,5},{4,7},{9,10},{11,8},{10,... | collective-permute-start | bytes 196616 | tf_op jit(solution)/shard_map/ppermute | solution.py:725
  11.5 7.3 %collective-permute-start.6 = (f32[3,8,256]{2,1,0:T(8,128)S(1)}, f32[3,8,256]{2,1,0:T(8,128)S(1)}, u32[]{:S(2)}, u32[]{:S(2)}) collective-permute-start(f32[3,8,256]{2,1,0:T(8,128)S(1)} %get-tuple-element.67), channel_id=1, source_target_pairs={{0,4},{8,12},{16,20},{24,28},{4,0},{12,8},{20,16},{28,24},{1,5},{9... | collective-permute-start | bytes 73736 | tf_op jit(solution)/shard_map/ppermute | solution.py:728
  11.5 7.3 %collective-permute-start.4 = (f32[3,8,256]{2,1,0:T(8,128)S(1)}, f32[3,8,256]{2,1,0:T(8,128)S(1)}, u32[]{:S(2)}, u32[]{:S(2)}) collective-permute-start(f32[3,8,256]{2,1,0:T(8,128)S(1)} %get-tuple-element.65), channel_id=1, source_target_pairs={{4,8},{12,16},{20,24},{28,0},{8,4},{16,12},{24,20},{0,28},{5,9},{1... | collective-permute-start | bytes 73736 | tf_op jit(solution)/shard_map/ppermute | solution.py:729
  20.4 3.2 %collective-permute-start.7 = (f32[32,128]{1,0:T(8,128)S(1)}, f32[32,128]{1,0:T(8,128)S(1)}, u32[]{:S(2)}, u32[]{:S(2)}) collective-permute-start(f32[32,128]{1,0:T(8,128)S(1)} %get-tuple-element.94), channel_id=1, source_target_pairs={{0,3},{1,2},{2,1},{3,0},{4,7},{5,6},{6,5},{7,4},{8,11},{9,10},{10,... | collective-permute-start | bytes 49160 | tf_op jit(solution)/shard_map/ppermute | solution.py:738
  23.7 1.2 %collective-permute-start.8 = (f32[16,128]{1,0:T(8,128)S(1)}, f32[16,128]{1,0:T(8,128)S(1)}, u32[]{:S(2)}, u32[]{:S(2)}) collective-permute-start(f32[16,128]{1,0:T(8,128)S(1)} %get-tuple-element.96), channel_id=1, source_target_pairs={{0,1},{2,3},{1,0},{3,2},{4,5},{6,7},{5,4},{7,6},{8,9},{10,11},{9,8... | collective-permute-start | bytes 24584 | tf_op jit(solution)/shard_map/ppermute | solution.py:739

commit v10 on v9

--- a/solution.py
+++ b/solution.py
@@ -346,8 +346,12 @@
     shape = (size_y, coarse_width)
     cell, lane = row_ids(shape) // 4, lane_ids(shape)
     pool_y = [jnp.where(cell + at == lane, 0.5 / 64.0, 0.0).astype(jnp.bfloat16) for at in lanes]
-    pooled = product(jnp.concatenate(changes, axis=0), pool_z, (1, 0))
-    return product(pooled, jnp.concatenate(pool_y, axis=0), (0, 0))
+    parts = jnp.concatenate(halves(jnp.concatenate(changes, axis=0)), axis=1)
+    pooled = jnp.dot(parts, jnp.concatenate([pool_z, pool_z], axis=0), preferred_element_type=F32)
+    parts = jnp.concatenate(halves(pooled), axis=0)
+    return lax.dot_general(
+        parts, jnp.concatenate(pool_y + pool_y, axis=0), (((0,), (0,)), ((), ())), preferred_element_type=F32
+    )
 
 
 def coarse_lane(u, size_x, size_y, coarse_y):

time: 25.7 us -> 25.7 us (level)
  no operation moved by 1% of the time
where the time goes in v10:
time: 25.7 us; the launch traced here: 25.5 us
  starting transfers between devices  13.6 us (53%)
  Pallas kernels  7.98 us (31%)
  waiting for transfers between devices  3.26 us (13%)
  between operations  0.71 us (3%)
    ppermute x1, starting transfers between devices, body(): face_b = lax.ppermute(face_b, 'gx', far_x)  4.31 us
    ppermute x1, starting transfers between devices, body(): corner_b = lax.ppermute(corner_b, 'gx', far_x)  3.5 us
    pallas_call x1, Pallas kernels, inner(): pl.pallas_call(functools.partial(inner_kernel, coarse_y), out_shape=(part...  2.66 us
    ppermute x1, starting transfers between devices, body(): face_a = lax.ppermute(face_a, 'gx', near_x)  2.59 us
    ppermute x1, waiting for transfers between devices, body(): mine, send = merge(mine, lax.ppermute(send, 'gy', across))  2.17 us
    pallas_call x1, Pallas kernels, rims(): pl.pallas_call(functools.partial(rim_kernel, coarse_y, size_x), out_shape...  1.6 us
    pallas_call x1, Pallas kernels, pack(): pl.pallas_call(pack_kernel, out_shape=(field, field, face, face, *sides,...  1.44 us
    ppermute x1, starting transfers between devices, body(): strip_b = lax.ppermute(strip_b, 'gy', far_y)  1.26 us
  transfers between devices with their start and end apart: 9, of which 2 were waited for; matrix products, arithmetic and copies ran while one was open for 0% of the time, Pallas kernels for 17%

profile of v10, /device:TPU:0, one launch (start us, length us, event | category | flops | bytes accessed | tf_op | source)
XLA Modules:
  0.0 25.5 jit_solution(14335683910180165103)
XLA Ops:
  0.6 1.4 %pack.1 = (f32[16,32,256]{2,1,0:T(8,128)S(1)}, f32[16,32,256]{2,1,0:T(8,128)S(1)}, f32[2,4,32,256]{3,2,1,0:T(8,128)S(1)}, f32[2,4,32,256]{3,2,1,0:T(8,128)S(1)},...) custom-call(f32[16,32,256]{2,1,0:T(8,128)} %phase.1, ...), custom_call_target="tpu_custom_call" | custom-call | flops 100000 | bytes 2000000 | tf_op jit(solution)/shard_map/pack/pallas_call | solution.py:131
  2.1 0.5 %collective-permute-start = (f32[17,8,256]{2,1,0:T(8,128)S(1)}, f32[17,8,256]{2,1,0:T(8,128)S(1)}, u32[]{:S(2)}, u32[]{:S(2)}) collective-permute-start(f32[17,8,256]{2,1,0:T(8,128)S(1)} %get-tuple-element.52), channel_id=1, source_target_pairs={{0,1},{2,3},{1,0},{3,2},{4,5},{6,7},{5,4},{7,6},{8,9},{10,11},{9,8... | collective-permute-start | bytes 417800 | tf_op jit(solution)/shard_map/ppermute | solution.py:721
  2.6 2.6 %collective-permute-start.5 = (f32[2,4,32,256]{3,2,1,0:T(8,128)S(1)}, f32[2,4,32,256]{3,2,1,0:T(8,128)S(1)}, u32[]{:S(2)}, u32[]{:S(2)}) collective-permute-start(f32[2,4,32,256]{3,2,1,0:T(8,128)S(1)} %get-tuple-element.66), channel_id=1, source_target_pairs={{0,4},{8,12},{16,20},{24,28},{4,0},{12,8},{20,16},{28,24},{1,5},{9... | collective-permute-start | bytes 786440 | tf_op jit(solution)/shard_map/ppermute | solution.py:720
  5.2 0.0 collective-permute-done.arrived.side_a
  5.2 1.3 %collective-permute-start.1 = (f32[10,8,256]{2,1,0:T(8,128)S(1)}, f32[10,8,256]{2,1,0:T(8,128)S(1)}, u32[]{:S(2)}, u32[]{:S(2)}) collective-permute-start(f32[10,8,256]{2,1,0:T(8,128)S(1)} %append.1.tile), channel_id=1, source_target_pairs={{1,2},{3,0},{2,1},{0,3},{5,6},{7,4},{6,5},{4,7},{9,10},{11,8},{10,... | collective-permute-start | bytes 245768 | tf_op jit(solution)/shard_map/ppermute | solution.py:728
  6.5 4.3 %collective-permute-start.3 = (f32[2,4,32,256]{3,2,1,0:T(8,128)S(1)}, f32[2,4,32,256]{3,2,1,0:T(8,128)S(1)}, u32[]{:S(2)}, u32[]{:S(2)}) collective-permute-start(f32[2,4,32,256]{3,2,1,0:T(8,128)S(1)} %get-tuple-element.64), channel_id=1, source_target_pairs={{4,8},{12,16},{20,24},{28,0},{8,4},{16,12},{24,20},{0,28},{5,9},{1... | collective-permute-start | bytes 786440 | tf_op jit(solution)/shard_map/ppermute | solution.py:730
  10.8 0.2 collective-permute-start.2
  11.0 0.1 products.1
  11.1 0.0 collective-permute-done.1.strip_b
  11.1 0.4 %corners.1 = (f32[64,128]{1,0:T(8,128)S(1)}, f32[3,8,256]{2,1,0:T(8,128)S(1)}, f32[3,8,256]{2,1,0:T(8,128)S(1)}) custom-call(f32[17,8,256]{2,1,0:T(8,128)S(1)} %collective-permute-done.arrived.side_a, f32[10,8,256]{2,1,0:T(8,128)S(1)} %collective-permute-done.1.strip_b, f32[16,128]{1,0:T(8,128)S(1)} %get-tuple-element.58.table), custom_call_target="tpu_custom_call" | custom-call | flops 100000 | bytes 400000 | tf_op jit(solution)/shard_map/corners/pallas_call | solution.py:218
  11.5 0.0 collective-permute-start.6
  11.5 3.5 %collective-permute-start.4 = (f32[3,8,256]{2,1,0:T(8,128)S(1)}, f32[3,8,256]{2,1,0:T(8,128)S(1)}, u32[]{:S(2)}, u32[]{:S(2)}) collective-permute-start(f32[3,8,256]{2,1,0:T(8,128)S(1)} %get-tuple-element.65), channel_id=1, source_target_pairs={{4,8},{12,16},{20,24},{28,0},{8,4},{16,12},{24,20},{0,28},{5,9},{1... | collective-permute-start | bytes 73736 | tf_op jit(solution)/shard_map/ppermute | solution.py:733
  15.0 0.0 collective-permute-done.2.rest_b
  15.0 2.7 %inner.1 = (f32[8,32,256]{2,1,0:T(8,128)S(1)}, f32[8,32,256]{2,1,0:T(8,128)S(1)}, f32[64,128]{1,0:T(8,128)S(1)}, f32[2,40,256]{2,1,0:T(8,128)S(1)}, f32[16,40,25...) custom-call(f32[16,32,256]{2,1,0:T(8,128)S(1)} %get-tuple-element.50, ...), custom_call_target="tpu_custom_call" | custom-call | flops 500000000 | bytes 5000000 | tf_op jit(solution)/shard_map/inner/pallas_call | solution.py:451
  17.7 1.1 %collective-permute-done.6.corner.near_corner = f32[3,8,256]{2,1,0:T(8,128)S(1)} collective-permute-done((f32[3,8,256]{2,1,0:T(8,128)S(1)}, f32[3,8,256]{2,1,0:T(8,128)S(1)}, u32[]{:S(2)}, u32[]{:S(2)}) %collective-permute-start.6) | collective-permute-done | bytes 24608 | tf_op jit(solution)/shard_map/ppermute | solution.py:732
  18.8 0.0 collective-permute-done.5.face
  18.8 0.0 collective-permute-done.4.corner
  18.8 0.0 collective-permute-done.3.face
  18.8 1.6 %rims.1 = (f32[4,40,256]{2,1,0:T(8,128)S(1)}, f32[4,40,256]{2,1,0:T(8,128)S(1)}, f32[4,32,256]{2,1,0:T(8,128)S(1)}, f32[4,40,256]{2,1,0:T(8,128)S(1)}, f32[4,40,...) custom-call(f32[2,4,32,256]{3,2,1,0:T(8,128)S(1)} %collective-permute-done.3.face, ...), custom_call_target="tpu_custom_call" | custom-call | flops 10000000 | bytes 3000000 | tf_op jit(solution)/shard_map/rims/pallas_call | solution.py:593
  20.4 1.1 %collective-permute-start.7 = (f32[32,128]{1,0:T(8,128)S(1)}, f32[32,128]{1,0:T(8,128)S(1)}, u32[]{:S(2)}, u32[]{:S(2)}) collective-permute-start(f32[32,128]{1,0:T(8,128)S(1)} %get-tuple-element.94), channel_id=1, source_target_pairs={{0,3},{1,2},{2,1},{3,0},{4,7},{5,6},{6,5},{7,4},{8,11},{9,10},{10,... | collective-permute-start | bytes 49160 | tf_op jit(solution)/shard_map/ppermute | solution.py:742
  21.5 2.2 %collective-permute-done.7.arrived = f32[32,128]{1,0:T(8,128)S(1)} collective-permute-done((f32[32,128]{1,0:T(8,128)S(1)}, f32[32,128]{1,0:T(8,128)S(1)}, u32[]{:S(2)}, u32[]{:S(2)}) %collective-permute-start.7) | collective-permute-done | bytes 16416 | tf_op jit(solution)/shard_map/ppermute | solution.py:742
  23.7 0.1 collective-permute-start.8
  23.8 1.0 %store.1 = (f32[16,32,256]{2,1,0:T(8,128)}, f32[16,32,256]{2,1,0:T(8,128)}) custom-call(f32[8,32,256]{2,1,0:T(8,128)S(1)} %get-tuple-element.62.middle_phase, f32[8,32,256]{2,1,0:T(8,128)S(1)} %get-tuple-element.63.middle_solute, f32[4,40,256]{2,1,0:T(8,128)S(1)} %get-tuple-element.85.near_p1, f32[4,40,256]{2,1,0:T(8,128)S(1)} %get-tuple-element.86.near_c1, ...), custom_call_target="tpu_custom_call" | custom-call | bytes 4000000 | tf_op jit(solution)/shard_map/store/pallas_call | solution.py:658
  24.8 0.0 collective-permute-done.8.arrived
  24.8 0.7 %owner.1 = f32[4,16,32]{2,1,0:T(8,128)} custom-call(f32[16,128]{1,0:T(8,128)S(1)} %get-tuple-element.95.mine, f32[16,128]{1,0:T(8,128)S(1)} %collective-permute-done.8.arrived), custom_call_target="tpu_custom_call" | custom-call | flops 10000 | bytes 100000 | tf_op jit(solution)/shard_map/owner/pallas_call | solution.py:698
  (3 shorter events, 0.0 us)
Async XLA Ops:
  2.1 3.1 %collective-permute-start = (f32[17,8,256]{2,1,0:T(8,128)S(1)}, f32[17,8,256]{2,1,0:T(8,128)S(1)}, u32[]{:S(2)}, u32[]{:S(2)}) collective-permute-start(f32[17,8,256]{2,1,0:T(8,128)S(1)} %get-tuple-element.52), channel_id=1, source_target_pairs={{0,1},{2,3},{1,0},{3,2},{4,5},{6,7},{5,4},{7,6},{8,9},{10,11},{9,8... | collective-permute-start | bytes 417800 | tf_op jit(solution)/shard_map/ppermute | solution.py:721
  2.6 16.2 %collective-permute-start.5 = (f32[2,4,32,256]{3,2,1,0:T(8,128)S(1)}, f32[2,4,32,256]{3,2,1,0:T(8,128)S(1)}, u32[]{:S(2)}, u32[]{:S(2)}) collective-permute-start(f32[2,4,32,256]{3,2,1,0:T(8,128)S(1)} %get-tuple-element.66), channel_id=1, source_target_pairs={{0,4},{8,12},{16,20},{24,28},{4,0},{12,8},{20,16},{28,24},{1,5},{9... | collective-permute-start | bytes 786440 | tf_op jit(solution)/shard_map/ppermute | solution.py:720
  5.2 5.9 %collective-permute-start.1 = (f32[10,8,256]{2,1,0:T(8,128)S(1)}, f32[10,8,256]{2,1,0:T(8,128)S(1)}, u32[]{:S(2)}, u32[]{:S(2)}) collective-permute-start(f32[10,8,256]{2,1,0:T(8,128)S(1)} %append.1.tile), channel_id=1, source_target_pairs={{1,2},{3,0},{2,1},{0,3},{5,6},{7,4},{6,5},{4,7},{9,10},{11,8},{10,... | collective-permute-start | bytes 245768 | tf_op jit(solution)/shard_map/ppermute | solution.py:728
  6.5 12.4 %collective-permute-start.3 = (f32[2,4,32,256]{3,2,1,0:T(8,128)S(1)}, f32[2,4,32,256]{3,2,1,0:T(8,128)S(1)}, u32[]{:S(2)}, u32[]{:S(2)}) collective-permute-start(f32[2,4,32,256]{3,2,1,0:T(8,128)S(1)} %get-tuple-element.64), channel_id=1, source_target_pairs={{4,8},{12,16},{20,24},{28,0},{8,4},{16,12},{24,20},{0,28},{5,9},{1... | collective-permute-start | bytes 786440 | tf_op jit(solution)/shard_map/ppermute | solution.py:730
  10.8 4.3 %collective-permute-start.2 = (f32[8,8,256]{2,1,0:T(8,128)S(1)}, f32[8,8,256]{2,1,0:T(8,128)S(1)}, u32[]{:S(2)}, u32[]{:S(2)}) collective-permute-start(f32[8,8,256]{2,1,0:T(8,128)S(1)} %get-tuple-element.57), channel_id=1, source_target_pairs={{1,2},{3,0},{2,1},{0,3},{5,6},{7,4},{6,5},{4,7},{9,10},{11,8},{10,... | collective-permute-start | bytes 196616 | tf_op jit(solution)/shard_map/ppermute | solution.py:729
  11.5 7.3 %collective-permute-start.6 = (f32[3,8,256]{2,1,0:T(8,128)S(1)}, f32[3,8,256]{2,1,0:T(8,128)S(1)}, u32[]{:S(2)}, u32[]{:S(2)}) collective-permute-start(f32[3,8,256]{2,1,0:T(8,128)S(1)} %get-tuple-element.67), channel_id=1, source_target_pairs={{0,4},{8,12},{16,20},{24,28},{4,0},{12,8},{20,16},{28,24},{1,5},{9... | collective-permute-start | bytes 73736 | tf_op jit(solution)/shard_map/ppermute | solution.py:732
  11.5 7.3 %collective-permute-start.4 = (f32[3,8,256]{2,1,0:T(8,128)S(1)}, f32[3,8,256]{2,1,0:T(8,128)S(1)}, u32[]{:S(2)}, u32[]{:S(2)}) collective-permute-start(f32[3,8,256]{2,1,0:T(8,128)S(1)} %get-tuple-element.65), channel_id=1, source_target_pairs={{4,8},{12,16},{20,24},{28,0},{8,4},{16,12},{24,20},{0,28},{5,9},{1... | collective-permute-start | bytes 73736 | tf_op jit(solution)/shard_map/ppermute | solution.py:733
  20.4 3.2 %collective-permute-start.7 = (f32[32,128]{1,0:T(8,128)S(1)}, f32[32,128]{1,0:T(8,128)S(1)}, u32[]{:S(2)}, u32[]{:S(2)}) collective-permute-start(f32[32,128]{1,0:T(8,128)S(1)} %get-tuple-element.94), channel_id=1, source_target_pairs={{0,3},{1,2},{2,1},{3,0},{4,7},{5,6},{6,5},{7,4},{8,11},{9,10},{10,... | collective-permute-start | bytes 49160 | tf_op jit(solution)/shard_map/ppermute | solution.py:742
  23.7 1.2 %collective-permute-start.8 = (f32[16,128]{1,0:T(8,128)S(1)}, f32[16,128]{1,0:T(8,128)S(1)}, u32[]{:S(2)}, u32[]{:S(2)}) collective-permute-start(f32[16,128]{1,0:T(8,128)S(1)} %get-tuple-element.96), channel_id=1, source_target_pairs={{0,1},{2,3},{1,0},{3,2},{4,5},{6,7},{5,4},{7,6},{8,9},{10,11},{9,8... | collective-permute-start | bytes 24584 | tf_op jit(solution)/shard_map/ppermute | solution.py:743
